TPU v7x, 32 devices: a whole 2x2x4 slice. The times are simulated.
32 devices in a mesh: seq: 16 (over z, y, x), fsdp: 2 (over core).
Axes of the slice: x: 2, y: 2, z: 4, core: 2. Of those that a mesh axis runs over, the one named last changes fastest.
Arguments:
- tokens: bfloat16 [2, 4096, 2048], P('fsdp', 'seq'), may hold values from -6 to 6
- cotangent: bfloat16 [2, 4096, 2048], P('fsdp', 'seq'), may hold values from -6 to 6
- norm_gain: bfloat16 [2048], P('fsdp'), may hold values from 0.5 to 1.5
- in_weight: bfloat16 [2048, 8192], P('fsdp'), may hold values from -0.125 to 0.125
- conv_weight: bfloat16 [4096, 4], P('fsdp'), may hold values from -3 to 3
- conv_bias: bfloat16 [4096], P('fsdp'), may hold values from -3 to 3
- select_weight: bfloat16 [4096, 160], P('fsdp'), may hold values from -0.09375 to 0.09375
- beta_weight: bfloat16 [4096, 128], P('fsdp'), may hold values from -0.5 to 0.5
- beta_bias: bfloat16 [4096], P('fsdp'), may hold values from -14 to 0
- skip_gain: bfloat16 [4096], P('fsdp'), may hold values from 0.5 to 1.5
- out_weight: bfloat16 [4096, 2048], P('fsdp'), may hold values from -0.25 to 0.25
Outputs:
- layer_out: bfloat16 [2, 4096, 2048], P('fsdp', 'seq')
- token_grad: float32 [2, 4096, 2048], P('fsdp', 'seq')
- gain_grad: float32 [2048], P(('seq', 'fsdp'))
- in_grad: float32 [2048, 8192], P(('seq', 'fsdp'))
- conv_weight_grad: float32 [4096, 4], P(('seq', 'fsdp'))
- conv_bias_grad: float32 [4096], P(('seq', 'fsdp'))
- select_grad: float32 [4096, 160], P(('seq', 'fsdp'))
- beta_weight_grad: float32 [4096, 128], P(('seq', 'fsdp'))
- beta_bias_grad: float32 [4096], P(('seq', 'fsdp'))
- skip_grad: float32 [4096], P(('seq', 'fsdp'))
- out_grad: float32 [4096, 2048], P(('seq', 'fsdp'))
All inputs are finite; a program needn't handle non-finite values.
Results may differ from a plain program's by a relative error of at most 0.012.
Values may be sent and summed in bfloat16 or wider, within the bound.
No kernel may reach another device: no remote copies, remote signals or barrier semaphores. Data moves between devices by JAX's collectives and lax.ppermute only.
A program may use at most 320 MiB of HBM per device.

v0:
```python
import jax
import jax.numpy as jnp
from jax import lax
from jax.sharding import PartitionSpec as P

epsilon = 1e-05
block_len = 16


def prefix(value, axis, join, neutral, backward):
    count, mine = (lax.axis_size(axis), lax.axis_index(axis))
    pieces = jax.tree.map(lambda part: lax.all_gather(part, axis), value)
    if backward:
        pieces = jax.tree.map(lambda part: part[::-1], pieces)
        mine = count - 1 - mine
    so_far = jax.tree.map(
        lambda part, zero: jnp.full_like(part, 0) + jnp.asarray(zero, part.dtype), value, neutral
    )

    def lap(position, so_far):
        longer = join(so_far, jax.tree.map(lambda part: part[position], pieces))
        return jax.tree.map(lambda new, old: jnp.where(position < mine, new, old), longer, so_far)

    return lax.fori_loop(0, count - 1, lap, so_far)


def passed_along(value, axis, steps):
    count = lax.axis_size(axis)
    leading, last = (max(0, -steps), min(count, count - steps))
    return lax.ppermute(value, axis, [(source, source + steps) for source in range(leading, last)])


def shortened(shard):
    return jax.tree.map(lambda a: a.astype(jnp.bfloat16) if a.dtype == jnp.float32 else a, shard)


def matmul(left, right):
    return jnp.dot(left, right, preferred_element_type=jnp.float32)


def swish_slope(value):
    logistic = jax.nn.sigmoid(value)
    return logistic * (1.0 + value * (1.0 - logistic))


def decay_of(rate_now, key_now):
    return 1.0 - (key_now * key_now)[:, :, None] * rate_now[:, None, :]


def step_state(current, rate_now, value_now, key_now):
    fading = decay_of(rate_now, key_now)
    return (fading * current + key_now[:, :, None] * (rate_now * value_now)[:, None, :], fading)


def read_state(current, query_now):
    return jnp.sum(current * query_now[:, :, None], axis=1)


def block_run(current, step_rates, inner_vals, key_vecs, queries):
    outputs = []
    for position in range(step_rates.shape[1]):
        current, fading = step_state(
            current, step_rates[:, position], inner_vals[:, position], key_vecs[:, position]
        )
        outputs.append(read_state(current, queries[:, position]))
    return (jnp.stack(outputs, axis=1), current)


def run_blocks(initial, blocks):

    def run_advance(carried, portion):
        current, product = carried
        step_rates, inner_vals, key_vecs, queries = portion
        outputs = []
        for position in range(step_rates.shape[1]):
            current, fading = step_state(
                current, step_rates[:, position], inner_vals[:, position], key_vecs[:, position]
            )
            product = product * fading
            outputs.append(read_state(current, queries[:, position]))
        return ((current, product), (jnp.stack(outputs, axis=1), carried[0]))

    (last_state, product), (outputs, starts) = lax.scan(
        run_advance, (initial, jnp.ones_like(initial)), blocks
    )
    return (last_state, product, outputs, starts)


def run_back(carry_grad, blocks):

    def retreat(later_grad, portion):
        start_state, step_rates, inner_vals, key_vecs, queries, grad_out = portion
        unused, pullback = jax.vjp(
            block_run, start_state, step_rates, inner_vals, key_vecs, queries
        )
        d_start, d_rates, d_values, d_keys, d_queries = pullback((grad_out, later_grad))
        return (d_start, (d_rates, d_values, d_keys, d_queries))

    return lax.scan(retreat, carry_grad, blocks, reverse=True)


def suffix_summary(portions, zero_state):

    def suffix_advance(carried, portion):
        product, running = carried
        rate_rows, key_rows, query_rows, grad_rows = portion
        for position in range(rate_rows.shape[1]):
            product = product * decay_of(rate_rows[:, position], key_rows[:, position])
            running = running + product * (
                query_rows[:, position][:, :, None] * grad_rows[:, position][:, None, :]
            )
        return ((product, running), None)

    (product, running), unused = lax.scan(
        suffix_advance, (jnp.ones_like(zero_state), zero_state), portions
    )
    return running


def chain_combine(earlier, later):
    return (earlier[0] * later[0], later[0] * earlier[1] + later[1])


def prefix_states(product, last_state):
    identity = (jnp.ones_like(product), jnp.zeros_like(last_state))
    return prefix((product, last_state), "seq", chain_combine, identity, False)[1]


def suffix_grads(product, summary):
    identity = (jnp.ones_like(product), jnp.zeros_like(summary))
    return prefix((product, summary), "seq", chain_combine, identity, True)[1]


def to_blocks(source):
    seq_count, piece_len = (source.shape[0], source.shape[1])
    shaped = source.reshape((seq_count, piece_len // block_len, block_len) + source.shape[2:])
    return jnp.moveaxis(shaped, 1, 0)


def from_blocks(stacked):
    moved = jnp.moveaxis(stacked, 0, 1)
    return moved.reshape((moved.shape[0], moved.shape[1] * moved.shape[2]) + moved.shape[3:])


def gather_mixer(
    norm_gain, conv_weight, conv_bias, select_weight, beta_weight, beta_bias, skip_gain, out_weight
):
    return (
        lax.all_gather(norm_gain, "fsdp", axis=0, tiled=True),
        lax.all_gather(conv_weight, "fsdp", axis=0, tiled=True),
        lax.all_gather(conv_bias, "fsdp", axis=0, tiled=True),
        lax.all_gather(select_weight, "fsdp", axis=0, tiled=True),
        lax.all_gather(beta_weight, "fsdp", axis=0, tiled=True),
        lax.all_gather(beta_bias, "fsdp", axis=0, tiled=True),
        lax.all_gather(skip_gain, "fsdp", axis=0, tiled=True),
        lax.all_gather(out_weight, "fsdp", axis=0, tiled=True),
    )


def forward_pass(tokens, in_weight, mixer_weights):
    gain_full, conv_full, conv_shift, select_full, beta_full, beta_shift, skip_full, out_full = (
        mixer_weights
    )
    seq_count, piece_len, model_width = tokens.shape
    inner_width, conv_taps = conv_full.shape
    rank_width = beta_full.shape[1]
    state_width = (select_full.shape[1] - rank_width) // 2
    row_count = seq_count * piece_len
    token_rows = tokens.reshape(row_count, model_width).astype(jnp.float32)
    variance = jnp.mean(token_rows * token_rows, axis=1, keepdims=True)
    scaled_inv = lax.rsqrt(variance + epsilon)
    normal = token_rows * scaled_inv
    normed = (normal * gain_full.astype(jnp.float32)).astype(jnp.bfloat16)
    projected = matmul(normed, lax.all_gather(in_weight, "fsdp", axis=0, tiled=True)).astype(
        jnp.bfloat16
    )
    inner_pre = projected[:, :inner_width].reshape(seq_count, piece_len, inner_width)
    gate_act = projected[:, inner_width:].astype(jnp.float32)
    edge_rows = passed_along(inner_pre[:, piece_len - conv_taps + 1 :, :], "seq", 1)
    extended = jnp.concatenate([edge_rows, inner_pre], axis=1)
    conv_sum = conv_shift.astype(jnp.float32) + conv_full[:, 0].astype(jnp.float32) * extended[
        :, 0:piece_len, :
    ].astype(jnp.float32)
    for tap_index in range(1, conv_taps):
        conv_sum = conv_sum + conv_full[:, tap_index].astype(jnp.float32) * extended[
            :, tap_index : tap_index + piece_len, :
        ].astype(jnp.float32)
    inner_act = jax.nn.silu(conv_sum).astype(jnp.bfloat16)
    inner_flat = inner_act.reshape(row_count, inner_width)
    selected = matmul(inner_flat, select_full)
    low_rank = selected[:, :rank_width].astype(jnp.bfloat16)
    key_vecs = selected[:, rank_width : rank_width + state_width]
    queries = selected[:, rank_width + state_width :]
    logits = jnp.einsum(
        "tr,ir->ti", low_rank, beta_full, preferred_element_type=jnp.float32
    ) + beta_shift.astype(jnp.float32)
    beta_gate = jax.nn.sigmoid(logits)
    key_norm = jnp.sum(key_vecs * key_vecs, axis=1, keepdims=True)
    step_rates = beta_gate / (1.0 + beta_gate * key_norm)
    inner_vals = inner_flat.astype(jnp.float32)
    blocks = (
        to_blocks(step_rates.reshape(seq_count, piece_len, inner_width)),
        to_blocks(inner_vals.reshape(seq_count, piece_len, inner_width)),
        to_blocks(key_vecs.reshape(seq_count, piece_len, state_width)),
        to_blocks(queries.reshape(seq_count, piece_len, state_width)),
    )
    zero_state = jnp.zeros((seq_count, state_width, inner_width), jnp.float32)
    last_state, product, unused, ignored = run_blocks(zero_state, blocks)
    initial = prefix_states(product, last_state)
    last_state, again_product, outputs, starts = run_blocks(initial, blocks)
    recurrent = from_blocks(outputs).reshape(row_count, inner_width)
    skip_sum = recurrent + skip_full.astype(jnp.float32) * inner_vals
    branch = (skip_sum * jax.nn.silu(gate_act)).astype(jnp.bfloat16)
    layer_out = (
        (token_rows + matmul(branch, out_full))
        .astype(jnp.bfloat16)
        .reshape(seq_count, piece_len, model_width)
    )
    return dict(
        layer_out=layer_out,
        normal=normal,
        scaled_inv=scaled_inv,
        normed=normed,
        gate_act=gate_act,
        extended=extended,
        conv_sum=conv_sum,
        inner_flat=inner_flat,
        inner_vals=inner_vals,
        low_rank=low_rank,
        key_vecs=key_vecs,
        beta_gate=beta_gate,
        key_norm=key_norm,
        blocks=blocks,
        starts=starts,
        product=product,
        skip_sum=skip_sum,
        branch=branch,
        zero_state=zero_state,
    )


def local(
    tokens,
    cotangent,
    norm_gain,
    in_weight,
    conv_weight,
    conv_bias,
    select_weight,
    beta_weight,
    beta_bias,
    skip_gain,
    out_weight,
):
    mixer_weights = gather_mixer(
        norm_gain,
        conv_weight,
        conv_bias,
        select_weight,
        beta_weight,
        beta_bias,
        skip_gain,
        out_weight,
    )
    first_pass = forward_pass(tokens, in_weight, mixer_weights)
    mixer_weights = gather_mixer(
        norm_gain,
        conv_weight,
        conv_bias,
        select_weight,
        beta_weight,
        beta_bias,
        skip_gain,
        out_weight,
    )
    saved = forward_pass(tokens, in_weight, mixer_weights)
    gain_full, conv_full, conv_shift, select_full, beta_full, beta_shift, skip_full, out_full = (
        mixer_weights
    )
    seq_count, piece_len, model_width = tokens.shape
    inner_width, conv_taps = conv_full.shape
    row_count = seq_count * piece_len
    groups = lax.axis_size(("seq", "fsdp"))
    grad_rows = cotangent.reshape(row_count, model_width)
    branch = saved["branch"]
    d_branch = jnp.einsum("td,id->ti", grad_rows, out_full, preferred_element_type=jnp.float32)
    out_grad = lax.psum_scatter(
        jnp.einsum(
            "ti,td->id",
            lax.slice_in_dim(
                branch, 0, inner_width // groups * lax.axis_size(("seq", "fsdp")), axis=1
            ),
            grad_rows,
            preferred_element_type=jnp.float32,
        ),
        ("seq", "fsdp"),
        scatter_dimension=0,
        tiled=True,
    )
    gate_act = saved["gate_act"]
    inner_vals = saved["inner_vals"]
    d_recurrent = d_branch * jax.nn.silu(gate_act)
    d_gate = d_branch * saved["skip_sum"] * swish_slope(gate_act)
    skip_term = jnp.sum(d_recurrent * inner_vals, axis=0)
    d_inner = d_recurrent * skip_full.astype(jnp.float32)
    rate_blocks, value_blocks, key_blocks, query_blocks = saved["blocks"]
    grad_blocks = to_blocks(d_recurrent.reshape(seq_count, piece_len, inner_width))
    starts = saved["starts"]
    zero_state = saved["zero_state"]
    summary = suffix_summary((rate_blocks, key_blocks, query_blocks, grad_blocks), zero_state)
    incoming = suffix_grads(saved["product"], summary)
    unused, (d_rates, d_values, d_keys, d_queries) = run_back(
        incoming, (starts, rate_blocks, value_blocks, key_blocks, query_blocks, grad_blocks)
    )
    d_rates = from_blocks(d_rates).reshape(row_count, inner_width)
    d_values = from_blocks(d_values).reshape(row_count, inner_width)
    d_keys = from_blocks(d_keys).reshape(row_count, -1)
    d_queries = from_blocks(d_queries).reshape(row_count, -1)
    beta_gate = saved["beta_gate"]
    key_vecs = saved["key_vecs"]
    denominator = 1.0 + beta_gate * saved["key_norm"]
    squared_den = denominator * denominator
    d_norm = jnp.sum(d_rates * (-(beta_gate * beta_gate) / squared_den), axis=1, keepdims=True)
    d_keys = d_keys + 2.0 * key_vecs * d_norm
    d_logits = (d_rates / squared_den * beta_gate * (1.0 - beta_gate)).astype(jnp.bfloat16)
    beta_bias_term = jnp.sum(d_logits.astype(jnp.float32), axis=0)
    beta_weight_term = jnp.einsum(
        "ti,tr->ir", d_logits, saved["low_rank"], preferred_element_type=jnp.float32
    )
    d_low_rank = matmul(d_logits, beta_full)
    d_selected = jnp.concatenate([d_low_rank, d_keys, d_queries], axis=1).astype(jnp.bfloat16)
    inner_flat = saved["inner_flat"]
    select_term = jnp.einsum(
        "ti,tc->ic", inner_flat, d_selected, preferred_element_type=jnp.float32
    )
    d_inner = (
        d_inner
        + d_values
        + jnp.einsum("tc,ic->ti", d_selected, select_full, preferred_element_type=jnp.float32)
    )
    d_conv = d_inner.reshape(seq_count, piece_len, inner_width) * swish_slope(saved["conv_sum"])
    extended = saved["extended"]
    conv_bias_term = jnp.sum(d_conv, axis=(0, 1))
    conv_weight_term = jnp.stack(
        [
            jnp.sum(
                d_conv * extended[:, tap_index : tap_index + piece_len, :].astype(jnp.float32),
                axis=(0, 1),
            )
            for tap_index in range(conv_taps)
        ],
        axis=1,
    )
    reach = conv_taps - 1
    d_extended = jnp.pad(conv_full[:, 0].astype(jnp.float32) * d_conv, ((0, 0), (0, reach), (0, 0)))
    for tap_index in range(1, conv_taps):
        d_extended = d_extended + jnp.pad(
            conv_full[:, tap_index].astype(jnp.float32) * d_conv,
            ((0, 0), (tap_index, reach - tap_index), (0, 0)),
        )
    returned = passed_along(shortened(d_extended[:, :reach, :]), "seq", -1)
    d_inner_pre = d_extended[:, reach:, :] + jnp.pad(
        returned, ((0, 0), (piece_len - reach, 0), (0, 0))
    )
    d_projected = jnp.concatenate(
        [d_inner_pre.reshape(row_count, inner_width), d_gate], axis=1
    ).astype(jnp.bfloat16)
    d_normed = jnp.einsum(
        "tc,dc->td",
        d_projected,
        lax.all_gather(in_weight, "fsdp", axis=0, tiled=True),
        preferred_element_type=jnp.float32,
    )
    normed = saved["normed"]
    in_grad = lax.psum_scatter(
        jnp.einsum(
            "td,tc->dc",
            lax.slice_in_dim(
                normed, 0, model_width // groups * lax.axis_size(("seq", "fsdp")), axis=1
            ),
            d_projected,
            preferred_element_type=jnp.float32,
        ),
        ("seq", "fsdp"),
        scatter_dimension=0,
        tiled=True,
    )
    normal = saved["normal"]
    gain_term = jnp.sum(d_normed * normal, axis=0)
    d_normal = d_normed * gain_full.astype(jnp.float32)
    token_grad = saved["scaled_inv"] * (
        d_normal - normal * jnp.mean(normal * d_normal, axis=1, keepdims=True)
    )
    token_grad = (token_grad + grad_rows.astype(jnp.float32)).reshape(
        seq_count, piece_len, model_width
    )
    summed = (
        lax.psum_scatter(gain_term, ("seq", "fsdp"), scatter_dimension=0, tiled=True),
        lax.psum_scatter(conv_weight_term, ("seq", "fsdp"), scatter_dimension=0, tiled=True),
        lax.psum_scatter(conv_bias_term, ("seq", "fsdp"), scatter_dimension=0, tiled=True),
        lax.psum_scatter(select_term, ("seq", "fsdp"), scatter_dimension=0, tiled=True),
        lax.psum_scatter(beta_weight_term, ("seq", "fsdp"), scatter_dimension=0, tiled=True),
        lax.psum_scatter(beta_bias_term, ("seq", "fsdp"), scatter_dimension=0, tiled=True),
        lax.psum_scatter(skip_term, ("seq", "fsdp"), scatter_dimension=0, tiled=True),
    )
    return (
        first_pass["layer_out"],
        token_grad,
        summed[0],
        in_grad,
        summed[1],
        summed[2],
        summed[3],
        summed[4],
        summed[5],
        summed[6],
        out_grad,
    )


def solution(mesh):
    in_specs = (
        P("fsdp", "seq", None),
        P("fsdp", "seq", None),
        P("fsdp"),
        P("fsdp", None),
        P("fsdp", None),
        P("fsdp"),
        P("fsdp", None),
        P("fsdp", None),
        P("fsdp"),
        P("fsdp"),
        P("fsdp", None),
    )
    out_specs = (
        P("fsdp", "seq", None),
        P("fsdp", "seq", None),
        P(("seq", "fsdp")),
        P(("seq", "fsdp"), None),
        P(("seq", "fsdp"), None),
        P(("seq", "fsdp")),
        P(("seq", "fsdp"), None),
        P(("seq", "fsdp"), None),
        P(("seq", "fsdp")),
        P(("seq", "fsdp")),
        P(("seq", "fsdp"), None),
    )
    return jax.shard_map(local, mesh=mesh, in_specs=in_specs, out_specs=out_specs, check_vma=False)
```

profile of v0, /device:TPU:1, one launch (start us, length us, event | category | flops | bytes accessed | tf_op | source)
XLA Modules:
  0.0 2517.6 jit_solution(4036802645079606268)
XLA Ops:
  14.0 49.3 %all-gather.11.cloned.1.call-done = bf16[2048,8192]{1,0:T(8,128)(2,1)} async-done(((bf16[1024,8192]{1,0:T(8,128)(2,1)}), bf16[2048,8192]{1,0:T(8,128)(2,1)}) %all-gather.11.cloned.1.call-update) | async-done | bytes 33554448 | tf_op jit(solution)/shard_map/all_gather | solution.py:174
  63.3 16.7 convolution_convert_fusion
  80.2 3.6 collective-permute-start
  87.8 8.4 all-gather.17.cloned.1.call-done
  96.1 17.6 fusion.158
  119.9 6.5 multiply_divide_fusion
  126.5 95.9 %while.115 = (s32[]{:T(128)}, f32[1,16,4096]{2,1,0:T(8,128)S(1)}, f32[1,16,4096]{2,1,0:T(8,128)S(1)}, f32[16,1,16,16]{3,2,1,0:T(8,128)}, f32[16,1,16,4096]{3,2,1...) while((s32[]{:T(128)}, f32[1,16,4096]{2,1,0:T(8,128)S(1)}, ...), condition=%wide.region_3.4_spmd.clone, body=%wide.region_2.3_spmd.clone.sunk | while | flops 8585475 | bytes 4187248 | solution.py:83
  227.9 102.6 %while.117 = (s32[]{:T(128)}, f32[1,16,4096]{2,1,0:T(8,128)}, f32[1,16,4096]{2,1,0:T(8,128)S(1)}, f32[16,1,16,16]{3,2,1,0:T(8,128)}, f32[16,1,16,4096]{3,2,1,0:T...) while((s32[]{:T(128)}, f32[1,16,4096]{2,1,0:T(8,128)}, ...), condition=%wide.region_25.26_spmd.clone, body=%wide.region_24.25_spmd.clone.sunk | while | flops 6422787 | bytes 3680375 | solution.py:114
  331.8 45.1 %all-gather.21.cloned.1.call-done = f32[16,16,4096]{2,1,0:T(8,128)} async-done(((f32[1,16,4096]{2,1,0:T(8,128)}), f32[16,16,4096]{2,1,0:T(8,128)}) %all-gather.21.cloned.1.call-update) | async-done | bytes 4194320 | tf_op jit(solution)/shard_map/all_gather | solution.py:12
  376.9 19.1 while.116
  400.9 196.5 %while.113 = (s32[]{:T(128)}, f32[1,16,4096]{2,1,0:T(8,128)S(1)}, f32[16,1,16,4096]{3,2,1,0:T(8,128)}, f32[16,1,16,4096]{3,2,1,0:T(8,128)}, f32[16,1,16,16]{3,2,...) while((s32[]{:T(128)}, f32[1,16,4096]{2,1,0:T(8,128)S(1)}, ...), condition=%wide.region_45.46_spmd, body=%wide.region_28.45_spmd.sunk | while | flops 9961730 | bytes 9910393 | solution.py:83
  599.9 108.3 %while.112 = (s32[]{:T(128)}, f32[1,16,4096]{2,1,0:T(8,128)S(1)}, f32[16,1,16,4096]{3,2,1,0:T(8,128)}, f32[16,1,16,16]{3,2,1,0:T(8,128)}, f32[16,1,16,4096]{3,2,...) while((s32[]{:T(128)}, f32[1,16,4096]{2,1,0:T(8,128)S(1)}, ...), condition=%wide.region_23.24_spmd, body=%wide.region_6.23_spmd.sunk | while | flops 9961730 | bytes 8861801 | solution.py:83
  708.2 4.6 reverse_bitcast_fusion.1
  712.7 4.6 reverse_bitcast_fusion
  717.3 19.1 while.118
  741.2 256.5 %while.114 = (s32[]{:T(128)}, f32[1,16,4096]{2,1,0:T(8,128)S(1)}, f32[16,1,16,4096]{3,2,1,0:T(8,128)}, f32[16,1,16,4096]{3,2,1,0:T(8,128)}, f32[16,1,16,16]{3,2,...) while((s32[]{:T(128)}, f32[1,16,4096]{2,1,0:T(8,128)S(1)}, ...), condition=%wide.region_127.128_spmd, body=%wide.region_46.127_spmd.sunk | while | flops 29761284 | bytes 17177980 | solution.py:99
  997.9 4.9 convert_reduce_fusion
  1003.9 10.1 multiply_convert_fusion
  1016.2 11.4 fusion.206
  1029.8 3.7 fusion.200
  1037.2 14.4 fusion.194
  1051.7 8.1 pad_add_fusion
  1061.3 4.1 collective-permute-done.1
  1067.3 25.8 %fusion.175 = f32[2048,8192]{1,0:T(8,128)} fusion(bf16[256,4096]{1,0:T(8,128)(2,1)} %get-tuple-element.1527, bf16[256,4096]{1,0:T(8,128)(2,1)} %fusion.189, bf16[1,256,2048]{2,1,0:T(8,128)(2,1)S(1)} %copy-done.5, f32[2048]{0:T(1024)S(1)} %copy-done.18, f32[256]{0:T(256)S(1)} %copy-done.23), kind=kOutput, calls=%fused_computation.756 | convolution fusion | flops 8600420352 | bytes 72360960 | tf_op jit(solution)/shard_map/td,tc->dc/dot_general | solution.py:376
  1093.1 12.1 fusion.178
  1105.2 16.2 fusion.187
  1121.4 43.4 %all-reduce.73 = (f32[2048]{0:T(1024)S(1)}, f32[4096]{0:T(1024)S(1)}, f32[4096]{0:T(1024)S(1)}, f32[4096]{0:T(1024)S(1)}) all-reduce(f32[2048]{0:T(1024)S(1)} %get-tuple-element.932, f32[4096]{0:T(1024)S(1)} %get-tuple-element.927, f32[4096]{0:T(1024)S(1)} %get-tuple-element.1076, ...), channel_id=5, replica_groups=mesh['seq'=16,'fsdp'=2] {'seq','fsdp'}, use_global_device_ids=true, to_apply=%region_131.132.clone | all-reduce | flops 14336 | bytes 114688
  1167.2 3.5 fusion.186
  1172.3 124.8 %reduce-scatter.12.cloned.1.call-done = f32[128,128]{1,0:T(8,128)} async-done(((f32[4096,128]{1,0:T(8,128)}), f32[128,128]{1,0:T(8,128)}) %reduce-scatter.12.cloned.1.call-update) | async-done | bytes 65552 | tf_op jit(solution)/shard_map/reduce_scatter | solution.py:402
  1297.1 136.2 %reduce-scatter.10.cloned.1.call-done = f32[128,160]{0,1:T(8,128)} async-done(((f32[4096,160]{0,1:T(8,128)}), f32[128,160]{0,1:T(8,128)}) %reduce-scatter.10.cloned.1.call-update) | async-done | bytes 81936 | tf_op jit(solution)/shard_map/reduce_scatter | solution.py:401
  1433.3 364.0 %reduce-scatter.14.cloned.1.call-done = f32[128,2048]{1,0:T(8,128)} async-done(((f32[4096,2048]{1,0:T(8,128)}), f32[128,2048]{1,0:T(8,128)}) %reduce-scatter.14.cloned.1.call-update) | async-done | bytes 1048592 | tf_op jit(solution)/shard_map/reduce_scatter | solution.py:287
  1797.3 713.0 %reduce-scatter.8.cloned.1.call-done = f32[64,8192]{1,0:T(8,128)} async-done(((f32[2048,8192]{1,0:T(8,128)}), f32[64,8192]{1,0:T(8,128)}) %reduce-scatter.8.cloned.1.call-update) | async-done | bytes 2097168 | tf_op jit(solution)/shard_map/reduce_scatter | solution.py:375
  (1618 shorter events, 843.1 us)
Async XLA Ops:
  7.2 56.1 %all-gather.11.cloned.1.call-start = ((), (), s32[]{:S(2)}) async-start(), calls=%async_computation.5 | async-start | bytes 50331648 | tf_op jit(solution)/shard_map/all_gather | solution.py:174
  7.9 88.2 %all-gather.17.cloned.1.call-start = ((), (), s32[]{:S(2)}) async-start(), calls=%async_computation.8 | async-start | bytes 25165824 | tf_op jit(solution)/shard_map/all_gather | solution.py:156
  8.7 105.1 %all-gather.13.cloned.1.call-start = ((), (), s32[]{:S(2)}) async-start(), calls=%async_computation.6 | async-start | bytes 1966080 | tf_op jit(solution)/shard_map/all_gather | solution.py:152
  9.4 110.5 %all-gather.15.cloned.1.call-start = ((), (), s32[]{:S(2)}) async-start(), calls=%async_computation.7 | async-start | bytes 1572864 | tf_op jit(solution)/shard_map/all_gather | solution.py:153
  10.0 321.7 %all-gather.19.cloned.1.call-start = ((), (), s32[]{:S(2)}) async-start(), calls=%async_computation.13 | async-start | bytes 4456448 | tf_op jit(solution)/shard_map/all_gather | solution.py:12
  11.9 51.4 %copy-start.17 = (f32[2048]{0:T(1024)}, f32[2048]{0:T(1024)S(1)}, u32[]{:S(2)}) copy-start(f32[2048]{0:T(1024)S(1)} %convert_element_type.169) | copy-start | bytes 24580
  12.2 67.8 %copy-start.22 = (f32[256]{0:T(256)}, f32[256]{0:T(256)S(1)}, u32[]{:S(2)}) copy-start(f32[256]{0:T(256)S(1)} %add_rsqrt_fusion) | copy-start | bytes 3076
  80.1 16.0 copy-start.14
  80.2 15.9 collective-permute-start
  83.8 29.9 %copy-start.27 = (f32[4096,1]{0,1:T(1,128)}, f32[4096,1]{0,1:T(1,128)S(1)}, u32[]{:S(2)}) copy-start(f32[4096,1]{0,1:T(1,128)S(1)} %get-tuple-element.1537) | copy-start | bytes 49156
  83.9 29.9 %copy-start.29 = (f32[4096,1]{0,1:T(1,128)}, f32[4096,1]{0,1:T(1,128)S(1)}, u32[]{:S(2)}) copy-start(f32[4096,1]{0,1:T(1,128)S(1)} %get-tuple-element.1538) | copy-start | bytes 49156
  83.9 29.9 %copy-start.31 = (f32[4096,1]{0,1:T(1,128)}, f32[4096,1]{0,1:T(1,128)S(1)}, u32[]{:S(2)}) copy-start(f32[4096,1]{0,1:T(1,128)S(1)} %get-tuple-element.1539) | copy-start | bytes 49156
  83.9 29.9 %copy-start.33 = (f32[4096,1]{0,1:T(1,128)}, f32[4096,1]{0,1:T(1,128)S(1)}, u32[]{:S(2)}) copy-start(f32[4096,1]{0,1:T(1,128)S(1)} %get-tuple-element.1540) | copy-start | bytes 49156
  96.1 17.7 copy-start.40
  223.1 153.8 %all-gather.21.cloned.1.call-start = ((), (), s32[]{:S(2)}) async-start(), calls=%async_computation.14 | async-start | bytes 4456448 | tf_op jit(solution)/shard_map/all_gather | solution.py:12
  227.9 484.8 %all-gather.23.cloned.1.call-start = ((), (), s32[]{:S(2)}) async-start(), calls=%async_computation.15 | async-start | bytes 4456448 | tf_op jit(solution)/shard_map/all_gather | solution.py:12
  331.3 839.5 %reduce-scatter.16.cloned.1.call-start = ((), (), s32[]{:S(2)}) async-start(), calls=%async_computation.16 | async-start | bytes 2162688
  741.2 256.6 %copy-start.36 = (f32[256]{0:T(256)S(1)}, f32[256]{0:T(256)}, u32[]{:S(2)}) copy-start(f32[256]{0:T(256)} %copy-done.35) | copy-start | bytes 3076
  1003.9 12.2 copy-start.15
  1003.9 12.3 copy-start.16
  1003.9 12.3 copy-start.28
  1003.9 12.3 copy-start.30
  1003.9 12.3 copy-start.32
  1003.9 12.3 copy-start.34
  1003.9 12.3 copy-start.41
  1029.7 267.3 %reduce-scatter.12.cloned.1.call-start = ((), (), s32[]{:S(2)}) async-start(), calls=%async_computation.11 | async-start | bytes 2162688 | tf_op jit(solution)/shard_map/reduce_scatter | solution.py:402
  1033.5 399.7 %reduce-scatter.10.cloned.1.call-start = ((), (), s32[]{:S(2)}) async-start(), calls=%async_computation.10 | async-start | bytes 2703360 | tf_op jit(solution)/shard_map/reduce_scatter | solution.py:401
  1035.6 761.6 %reduce-scatter.14.cloned.1.call-start = ((), (), s32[]{:S(2)}) async-start(), calls=%async_computation.12 | async-start | bytes 34603008 | tf_op jit(solution)/shard_map/reduce_scatter | solution.py:287
  1051.6 1458.7 %reduce-scatter.8.cloned.1.call-start = ((), (), s32[]{:S(2)}) async-start(), calls=%async_computation.9 | async-start | bytes 69206016 | tf_op jit(solution)/shard_map/reduce_scatter | solution.py:375
  1059.9 5.6 collective-permute-start.1
  1105.2 16.2 copy-start.26
  1105.2 62.0 %copy-start.13 = (bf16[1,256,2048]{2,1,0:T(8,128)(2,1)S(1)}, bf16[1,256,2048]{2,1,0:T(8,128)(2,1)}, u32[]{:S(2)}) copy-start(bf16[1,256,2048]{2,1,0:T(8,128)(2,1)} %param.26) | copy-start | bytes 3145732
  (24 other events, 149.3 us)
Sparse Core Ops, SparseCore 0:
  9.6 53.6 all-gather.10
  64.8 31.2 all-gather.16
  97.7 10.5 all-gather.12
  109.7 10.1 all-gather.14
  223.2 75.6 all-gather.18
  302.2 74.6 all-gather.20
  380.2 74.6 all-gather.22
  1029.9 131.5 reduce-scatter.15
  1164.4 132.6 reduce-scatter.11
  1299.8 133.4 reduce-scatter.9
  1436.2 361.0 reduce-scatter.13
  1800.0 710.2 reduce-scatter.7
where the time goes:
time: 2530 us; the launch traced here: 2520 us
  waiting for transfers between devices  1450 us (57%)
  other arithmetic  529 us (21%)
  local copies, waits for them, and re-layouts  329 us (13%)
  matrix products  131 us (5%)
  blocking collectives  52.8 us (2%)
    reduce_scatter x1, waiting for transfers between devices, local(): lax.psum_scatter(jnp.einsum('td,tc->dc', lax.slice_in_dim(normed, 0, mode...  713 us
    reduce_scatter x1, waiting for transfers between devices, local(): lax.psum_scatter(jnp.einsum('ti,td->id', lax.slice_in_dim(branch, 0, inne...  364 us
    squeeze x208, local copies, waits for them, and re-layouts, run_blocks(): lax.scan(run_advance, (initial, jnp.ones_like(initial)), blocks)  183 us
    reduce_sum x288, other arithmetic, read_state(): return jnp.sum(current * query_now[:, :, None], axis=1)  141 us
    reduce_scatter x1, waiting for transfers between devices, local(): lax.psum_scatter(select_term, ('seq', 'fsdp'), scatter_dimension=0, tiled...  136 us
    reduce_scatter x1, waiting for transfers between devices, local(): lax.psum_scatter(beta_weight_term, ('seq', 'fsdp'), scatter_dimension=0,...  125 us
    reduce_sum x128, other arithmetic, decay_of(): return 1.0 - (key_now * key_now)[:, :, None] * rate_now[:, None, :]  119 us
    add x32, other arithmetic, step_state(): fading * current + key_now[:, :, None] * (rate_now * value_now)[:, None, :]  59.3 us
  transfers between devices with their start and end apart: 14, of which 9 were waited for; matrix products, arithmetic and copies ran while one was open for 23% of the time, Pallas kernels for 0%

commit v1 on v0

v1 whole, which is shorter than its diff:
```python
import functools

import jax
import jax.numpy as jnp
from jax import lax
from jax.experimental import pallas as pl
from jax.experimental.pallas import tpu as pltpu
from jax.sharding import PartitionSpec as P

f32 = jnp.float32
bf16 = jnp.bfloat16
epsilon = 1e-05
lanes = 128
group = 4
block_len = 32
both = ("seq", "fsdp")


def matmul(left, right):
    return jnp.dot(left, right, preferred_element_type=f32)


def matmul_nt(left, right):
    return lax.dot_general(left, right, (((1,), (1,)), ((), ())), preferred_element_type=f32)


def matmul_tn(left, right):
    return lax.dot_general(left, right, (((0,), (0,)), ((), ())), preferred_element_type=f32)


def swish_slope(value):
    logistic = jax.nn.sigmoid(value)
    return logistic * (1.0 + value * (1.0 - logistic))


def swap(value):
    return lax.ppermute(value, "fsdp", [(0, 1), (1, 0)])


def at(stacked, index):
    return lax.dynamic_index_in_dim(stacked, index, 0, keepdims=False)


def spread(ref, position, state):
    return jnp.broadcast_to(ref[0, position, pl.ds(state, 1), :], (8, lanes))


def summary_kernel(r_ref, v_ref, d_ref, k_ref, q_ref, k2_ref, p_ref, s_ref, g_ref):
    length, tiles = r_ref.shape[1], r_ref.shape[2]
    states = k_ref.shape[2]
    zero = jnp.zeros((8, lanes), f32)
    one = jnp.ones((8, lanes), f32)
    for tile in range(0, tiles, 8):
        cut = pl.ds(tile, 8)

        def body(position, carry):
            product, current, grads = (list(part) for part in carry)
            rate = r_ref[0, position, cut, :]
            fed = rate * v_ref[0, position, cut, :]
            grad = d_ref[0, position, cut, :]
            for i in range(states):
                fading = 1.0 - spread(k2_ref, position, i) * rate
                current[i] = fading * current[i] + spread(k_ref, position, i) * fed
                product[i] = product[i] * fading
                grads[i] = grads[i] + product[i] * (spread(q_ref, position, i) * grad)
            return (tuple(product), tuple(current), tuple(grads))

        product, current, grads = lax.fori_loop(
            0, length, body, ((one,) * states, (zero,) * states, (zero,) * states), unroll=4
        )
        for i in range(states):
            p_ref[0, i, cut, :] = product[i].astype(p_ref.dtype)
            s_ref[0, i, cut, :] = current[i].astype(s_ref.dtype)
            g_ref[0, i, cut, :] = grads[i].astype(g_ref.dtype)


def forward_kernel(r_ref, v_ref, k_ref, q_ref, k2_ref, init_ref, out_ref, start_ref):
    length, tiles = r_ref.shape[1], r_ref.shape[2]
    states = k_ref.shape[2]
    blocks = start_ref.shape[1]
    span = length // blocks
    for tile in range(0, tiles, 8):
        cut = pl.ds(tile, 8)

        def block(index, current):
            for i in range(states):
                start_ref[0, index, i, cut, :] = current[i]

            def body(step, current):
                current = list(current)
                position = index * span + step
                rate = r_ref[0, position, cut, :]
                fed = rate * v_ref[0, position, cut, :]
                total = None
                for i in range(states):
                    fading = 1.0 - spread(k2_ref, position, i) * rate
                    current[i] = fading * current[i] + spread(k_ref, position, i) * fed
                    term = spread(q_ref, position, i) * current[i]
                    total = term if total is None else total + term
                out_ref[0, position, cut, :] = total
                return tuple(current)

            return lax.fori_loop(0, span, body, current, unroll=4)

        initial = tuple(init_ref[0, i, cut, :] for i in range(states))
        lax.fori_loop(0, blocks, block, initial)


def backward_kernel(
    r_ref,
    v_ref,
    d_ref,
    k_ref,
    q_ref,
    k2_ref,
    start_ref,
    last_ref,
    dr_ref,
    dv_ref,
    dk_ref,
    dq_ref,
    hist,
):
    length, tiles = r_ref.shape[1], r_ref.shape[2]
    states = k_ref.shape[2]
    blocks = start_ref.shape[1]
    span = length // blocks
    cuts = [pl.ds(tile, 8) for tile in range(0, tiles, 8)]

    def block(lap, grads):
        index = blocks - 1 - lap
        base = index * span
        for cut in cuts:

            def ahead(step, current):
                current = list(current)
                position = base + step
                rate = r_ref[0, position, cut, :]
                fed = rate * v_ref[0, position, cut, :]
                for i in range(states):
                    fading = 1.0 - spread(k2_ref, position, i) * rate
                    current[i] = fading * current[i] + spread(k_ref, position, i) * fed
                    hist[step + 1, i, cut, :] = current[i]
                return tuple(current)

            initial = tuple(start_ref[0, index, i, cut, :] for i in range(states))
            for i in range(states):
                hist[0, i, cut, :] = initial[i]
            lax.fori_loop(0, span, ahead, initial, unroll=4)

        def back(lap_step, grads):
            grads = [list(part) for part in grads]
            step = span - 1 - lap_step
            position = base + step
            rates = [r_ref[0, position, cut, :] for cut in cuts]
            values = [v_ref[0, position, cut, :] for cut in cuts]
            outs = [d_ref[0, position, cut, :] for cut in cuts]
            d_rates = [None] * len(cuts)
            d_fed = [None] * len(cuts)
            for i in range(states):
                key = spread(k_ref, position, i)
                query = spread(q_ref, position, i)
                square = spread(k2_ref, position, i)
                key_term = None
                query_term = None
                for n, cut in enumerate(cuts):
                    grad = query * outs[n] + grads[n][i]
                    keyed = key * grad
                    held = key * hist[step, i, cut, :]
                    left = values[n] - held
                    rated = grad * rates[n]
                    part = keyed * left
                    d_rates[n] = part if i == 0 else d_rates[n] + part
                    d_fed[n] = keyed if i == 0 else d_fed[n] + keyed
                    part = rated * (left - held)
                    key_term = part if n == 0 else key_term + part
                    part = outs[n] * hist[step + 1, i, cut, :]
                    query_term = part if n == 0 else query_term + part
                    grads[n][i] = grad - square * rated
                dk_ref[0, position, pl.ds(i, 1), :] = jnp.sum(key_term, axis=0, keepdims=True)
                dq_ref[0, position, pl.ds(i, 1), :] = jnp.sum(query_term, axis=0, keepdims=True)
            for n, cut in enumerate(cuts):
                dr_ref[0, position, cut, :] = d_rates[n]
                dv_ref[0, position, cut, :] = rates[n] * d_fed[n]
            return tuple(tuple(part) for part in grads)

        return lax.fori_loop(0, span, back, grads)

    first = tuple(tuple(last_ref[0, i, cut, :] for i in range(states)) for cut in cuts)
    lax.fori_loop(0, blocks, block, first)


def per_sequence(kernel, name, operands, results, scratch, flops):
    sequences = operands[0].shape[0]

    def spec(array):
        rest = array.shape[1:]
        return pl.BlockSpec((1,) + rest, lambda n: (n,) + (0,) * len(rest))

    moved = sum(a.size * a.dtype.itemsize for a in (*operands, *results))
    return pl.pallas_call(
        kernel,
        grid=(sequences,),
        in_specs=[spec(a) for a in operands],
        out_specs=[spec(a) for a in results],
        out_shape=list(results),
        scratch_shapes=scratch,
        compiler_params=pltpu.CompilerParams(vmem_limit_bytes=56 * 2**20),
        cost_estimate=pl.CostEstimate(flops=flops, bytes_accessed=moved, transcendentals=0),
        name=name,
    )(*operands)


def exchange_states(product, last_state, summary):
    count = lax.axis_size("seq")
    shape = product.shape
    rows = product.size // lanes // count
    packed = jnp.stack([a.reshape(count, rows, lanes) for a in (product, last_state, summary)], 1)
    pieces = lax.all_to_all(packed, "seq", 0, 0).astype(f32)
    state = jnp.zeros((rows, lanes), f32)
    grad = jnp.zeros((rows, lanes), f32)
    states, grads = [], []
    for piece in range(count):
        states.append(state)
        state = pieces[piece, 0] * state + pieces[piece, 1]
        grads.append(grad)
        later = count - 1 - piece
        grad = pieces[later, 0] * grad + pieces[later, 2]
    sent = jnp.stack(
        [jnp.stack([a, b]) for a, b in zip(states, reversed(grads))]
    ).astype(bf16)
    got = lax.all_to_all(sent, "seq", 0, 0).astype(f32)
    return got[:, 0].reshape(shape), got[:, 1].reshape(shape)


def plane_gather(value):
    count = lax.axis_size("seq")
    return [value] + [
        lax.ppermute(value, "seq", [(s, s ^ d) for s in range(count)]) for d in range(1, group)
    ]


def plane_trade(chunk_for):
    count = lax.axis_size("seq")
    mine = lax.axis_index("seq") % group
    return [chunk_for(mine)] + [
        lax.ppermute(
            chunk_for(jnp.bitwise_xor(mine, d)), "seq", [(s, s ^ d) for s in range(count)]
        )
        for d in range(1, group)
    ]


def line_reduce(chunk_for, wanted):
    count = lax.axis_size("seq") // group
    mine = lax.axis_index("seq") // group

    def pairs(step, sign):
        found = []
        for o in range(count):
            target = o + sign * (count - 1 - step)
            if not (0 <= target < count):
                continue
            for p in range(group):
                for c in range(2):
                    if wanted(target, c):
                        source = (o * group + p) * 2 + c
                        found.append((source, source + sign * group * 2))
        return found

    total = chunk_for(mine)
    for sign in (1, -1):
        received = None
        for step in range(count - 1):
            links = pairs(step, sign)
            if not links:
                continue
            target = jnp.clip(mine + sign * (count - 1 - step), 0, count - 1)
            part = chunk_for(target)
            if received is not None:
                part = part + received.astype(f32)
            received = lax.ppermute(part.astype(bf16), both, links)
        total = total + received.astype(f32)
    return total


def owner_reduce(partial):
    half, rows, width = partial.shape
    core = lax.axis_index("fsdp")
    outer = lax.axis_index("seq") // group
    total = line_reduce(
        lambda target: at(partial, jnp.clip(target - core * half, 0, half - 1)),
        lambda target, c: target // half == c,
    )
    pieces = total.reshape(2, rows // 2, width)
    other = swap(at(pieces, 1 - core))
    return jnp.where(outer // half == core, at(pieces, core), other)


def local(
    tokens,
    cotangent,
    norm_gain,
    in_weight,
    conv_weight,
    conv_bias,
    select_weight,
    beta_weight,
    beta_bias,
    skip_gain,
    out_weight,
):
    core = lax.axis_index("fsdp")
    place = lax.axis_index("seq")
    count = lax.axis_size("seq")
    outer_count = count // group
    member = place % group
    length, model = tokens.shape[1], tokens.shape[2]
    half_model = in_weight.shape[0]
    half, taps = conv_weight.shape
    inner = 2 * half
    rank = beta_weight.shape[1]
    states = (select_weight.shape[1] - rank) // 2
    tiles = half // lanes
    rows = 2 * length
    reach = taps - 1

    own_tokens = tokens[0]
    other_tokens = swap(own_tokens)
    own_cot = cotangent[0]
    other_cot = swap(own_cot)
    gain_other = swap(norm_gain)
    low = jnp.where(core == 0, norm_gain, gain_other)
    high = jnp.where(core == 0, gain_other, norm_gain)
    gain_full = jnp.concatenate([low, high]).astype(f32)

    def columns(start):
        return lax.dynamic_slice(in_weight, (0, start), (half_model, half))

    inner_own = columns(core * half)
    gate_own = columns(inner + core * half)
    inner_got = swap(columns((1 - core) * half))
    gate_got = swap(columns(inner + (1 - core) * half))

    def normalise(values):
        wide = values.astype(f32)
        inverse = lax.rsqrt(jnp.mean(wide * wide, axis=1, keepdims=True) + epsilon)
        normal = wide * inverse
        return normal, inverse, (normal * gain_full).astype(bf16)

    normal, inverse, own_normed = normalise(own_tokens)
    other_normed = normalise(other_tokens)[2]
    normed = jnp.concatenate([own_normed, other_normed])
    cot = jnp.concatenate([own_cot, other_cot])
    normed_own = lax.dynamic_slice(normed, (0, core * half_model), (rows, half_model))
    normed_got = lax.dynamic_slice(normed, (0, (1 - core) * half_model), (rows, half_model))

    inner_pre = (matmul(normed_own, inner_own) + matmul(normed_got, inner_got)).astype(bf16)
    inner_pre = inner_pre.reshape(2, length, half)
    edges = lax.ppermute(
        inner_pre[:, length - reach :], "seq", [(s, s + 1) for s in range(count - 1)]
    )
    gate = (matmul(normed_own, gate_own) + matmul(normed_got, gate_got)).astype(bf16).astype(f32)
    d_branch = matmul_nt(cot, out_weight)

    def gathered(own):
        got = [a for a in plane_gather(own)]
        swapped = swap(jnp.stack(got[1:]))
        return got, swapped

    normed_parts, normed_swapped = gathered(own_normed)
    cot_parts, cot_swapped = gathered(own_cot)

    def all_rows(parts, swapped, other):
        pieces = []
        for d in range(group):
            pieces += [parts[d], other if d == 0 else swapped[d - 1]]
        return jnp.concatenate(pieces)

    normed_all = all_rows(normed_parts, normed_swapped, other_normed)
    cot_all = all_rows(cot_parts, cot_swapped, other_cot)

    extended = jnp.concatenate([edges, inner_pre], axis=1)
    conv_wide = conv_weight.astype(f32)
    conv_sum = conv_bias.astype(f32)
    for tap in range(taps):
        conv_sum = conv_sum + conv_wide[:, tap] * extended[:, tap : tap + length].astype(f32)
    conv_sum = conv_sum.reshape(rows, half)
    inner_act = jax.nn.silu(conv_sum).astype(bf16)
    selected = matmul(inner_act, select_weight)
    selected = selected + swap(selected.reshape(2, length, -1)[::-1]).reshape(rows, -1)
    low_rank = selected[:, :rank].astype(bf16)
    keys = selected[:, rank : rank + states]
    queries = selected[:, rank + states :]
    beta_gate = jax.nn.sigmoid(matmul_nt(low_rank, beta_weight) + beta_bias.astype(f32))
    key_norm = jnp.sum(keys * keys, axis=1, keepdims=True)
    denominator = 1.0 + beta_gate * key_norm
    rates = beta_gate / denominator
    values = inner_act.astype(f32)
    swish = jax.nn.silu(gate)
    d_recurrent = d_branch * swish

    def tiled(array):
        return array.reshape(2, length, tiles, lanes)

    def wide(array):
        return jnp.broadcast_to(
            array.reshape(2, length, states, 1), (2, length, states, lanes)
        )

    rate_t, value_t, grad_t = tiled(rates), tiled(values), tiled(d_recurrent)
    key_t, query_t, square_t = wide(keys), wide(queries), wide(keys * keys)
    size = rows * states * half
    state_shape = (2, states, tiles, lanes)
    product, last_state, summary = per_sequence(
        summary_kernel,
        "summary",
        (rate_t, value_t, grad_t, key_t, query_t, square_t),
        [jax.ShapeDtypeStruct(state_shape, bf16)] * 3,
        [],
        9 * size,
    )
    first_state, last_grad = exchange_states(product, last_state, summary)
    blocks = length // block_len
    recurrent, starts = per_sequence(
        forward_kernel,
        "forward",
        (rate_t, value_t, key_t, query_t, square_t, first_state),
        [
            jax.ShapeDtypeStruct((2, length, tiles, lanes), f32),
            jax.ShapeDtypeStruct((2, blocks, states, tiles, lanes), f32),
        ],
        [],
        7 * size,
    )
    skip_wide = skip_gain.astype(f32)
    skip_sum = recurrent.reshape(rows, half) + skip_wide * values
    branch = (skip_sum * swish).astype(bf16)
    d_gate = (d_branch * skip_sum * swish_slope(gate)).astype(bf16)

    owner_rows = 2 * half // count
    branch_split = branch.reshape(rows, outer_count // 2, group, owner_rows)

    def branch_chunk(p):
        return lax.dynamic_index_in_dim(branch_split, p, 2, keepdims=False).reshape(rows, -1)

    branch_all = jnp.concatenate(plane_trade(branch_chunk))
    out_partial = matmul_tn(branch_all, cot_all).reshape(outer_count // 2, owner_rows, model)
    out_grad = owner_reduce(out_partial)

    out_sum = matmul(branch, out_weight)
    layer_out = own_tokens.astype(f32) + (out_sum[:length] + swap(out_sum[length:]))
    layer_out = layer_out.astype(bf16)[None]

    def in_weight_part(grad_half):
        width = half // group

        def chunk(p):
            return lax.dynamic_slice(grad_half, (0, p * width), (rows, width))

        grad_all = jnp.concatenate(plane_trade(chunk))
        partial = matmul_tn(normed_all, grad_all).reshape(outer_count, -1, width)
        total = line_reduce(lambda target: at(partial, target), lambda target, c: True)
        pieces = total.reshape(group, -1, width)
        got = jnp.stack(plane_trade(lambda p: at(pieces, p).astype(bf16)))
        got = got.reshape(group, 2, -1, width)
        mine = lax.dynamic_index_in_dim(got, core, 1, keepdims=False)
        other = swap(lax.dynamic_index_in_dim(got, 1 - core, 1, keepdims=False))
        quarters = []
        for source in (jnp.where(core == 0, mine, other), jnp.where(core == 0, other, mine)):
            quarters += [at(source, jnp.bitwise_xor(member, q)) for q in range(group)]
        return jnp.concatenate(quarters, axis=1).astype(f32)

    gate_grad = in_weight_part(d_gate)
    d_rates, d_values, d_keys, d_queries = per_sequence(
        backward_kernel,
        "backward",
        (rate_t, value_t, grad_t, key_t, query_t, square_t, starts, last_grad),
        [
            jax.ShapeDtypeStruct((2, length, tiles, lanes), f32),
            jax.ShapeDtypeStruct((2, length, tiles, lanes), f32),
            jax.ShapeDtypeStruct((2, length, states, lanes), f32),
            jax.ShapeDtypeStruct((2, length, states, lanes), f32),
        ],
        [pltpu.VMEM((block_len + 1, states, tiles, lanes), f32)],
        23 * size,
    )
    d_rates = d_rates.reshape(rows, half)
    d_values = d_values.reshape(rows, half)
    squared_den = denominator * denominator
    d_norm = jnp.sum(d_rates * (-(beta_gate * beta_gate) / squared_den), axis=1, keepdims=True)
    d_keys = jnp.sum(d_keys, axis=3).reshape(rows, states) + 2.0 * keys * d_norm
    d_queries = jnp.sum(d_queries, axis=3).reshape(rows, states)
    d_logits = (d_rates / squared_den * beta_gate * (1.0 - beta_gate)).astype(bf16)
    d_selected = jnp.concatenate([matmul(d_logits, beta_weight), d_keys, d_queries], axis=1)
    d_selected = d_selected + swap(d_selected.reshape(2, length, -1)[::-1]).reshape(rows, -1)
    d_selected = d_selected.astype(bf16)
    d_inner = d_recurrent * skip_wide + d_values + matmul_nt(d_selected, select_weight)
    d_conv = (d_inner * swish_slope(conv_sum)).reshape(2, length, half)
    later = lax.ppermute(d_conv[:, :reach], "seq", [(s + 1, s) for s in range(count - 1)])
    d_extended = jnp.concatenate([d_conv, later], axis=1)
    d_inner_pre = sum(
        conv_wide[:, tap] * d_extended[:, reach - tap : reach - tap + length]
        for tap in range(taps)
    )
    d_inner_pre = d_inner_pre.reshape(rows, half).astype(bf16)
    inner_grad = in_weight_part(d_inner_pre)
    in_grad = jnp.concatenate([inner_grad, gate_grad], axis=1)

    vectors = [
        jnp.sum(d_conv * extended[:, tap : tap + length].astype(f32), axis=(0, 1))
        for tap in range(taps)
    ]
    vectors += [
        jnp.sum(d_conv, axis=(0, 1)),
        jnp.sum(d_logits.astype(f32), axis=0),
        jnp.sum(d_recurrent * values, axis=0),
    ]
    tail = jnp.stack(vectors, axis=1)
    pack = jnp.concatenate(
        [
            matmul_tn(inner_act, d_selected),
            matmul_tn(d_logits, low_rank),
            tail,
        ],
        axis=1,
    )
    width = pack.shape[1]
    pack = jnp.pad(pack, ((0, 0), (0, -width % lanes)))
    pack = pack.reshape(outer_count // 2, group, owner_rows, -1)
    pack_parts = plane_trade(
        lambda p: lax.dynamic_index_in_dim(pack, p, 1, keepdims=False).astype(bf16)
    )
    pack_sum = sum(a.astype(f32) for a in pack_parts)
    pack_own = owner_reduce(pack_sum)
    edge = select_weight.shape[1]
    select_grad = pack_own[:, :edge]
    beta_weight_grad = pack_own[:, edge : edge + rank]
    edge += rank
    conv_weight_grad = pack_own[:, edge : edge + taps]
    conv_bias_grad = pack_own[:, edge + taps]
    beta_bias_grad = pack_own[:, edge + taps + 1]
    skip_grad = pack_own[:, edge + taps + 2]

    d_normed_own = matmul_nt(d_inner_pre, inner_own) + matmul_nt(d_gate, gate_own)
    d_normed_got = matmul_nt(d_inner_pre, inner_got) + matmul_nt(d_gate, gate_got)
    left = jnp.where(core == 0, d_normed_own, d_normed_got)
    right = jnp.where(core == 0, d_normed_got, d_normed_own)
    d_normed = jnp.concatenate([left, right], axis=1)
    d_normed = d_normed[:length] + swap(d_normed[length:])
    gain_term = jnp.sum(d_normed * normal, axis=0)
    gain_parts = lax.all_to_all(gain_term.reshape(count, 1, -1), "seq", 0, 0)
    gain_sum = jnp.sum(gain_parts, axis=(0, 1)).reshape(2, -1)
    gain_grad = at(gain_sum, core) + swap(at(gain_sum, 1 - core))
    d_normal = d_normed * gain_full
    token_grad = inverse * (
        d_normal - normal * jnp.mean(normal * d_normal, axis=1, keepdims=True)
    ) + own_cot.astype(f32)

    return (
        layer_out,
        token_grad[None],
        gain_grad,
        in_grad,
        conv_weight_grad,
        conv_bias_grad,
        select_grad,
        beta_weight_grad,
        beta_bias_grad,
        skip_grad,
        out_grad,
    )


def solution(mesh):
    in_specs = (
        P("fsdp", "seq", None),
        P("fsdp", "seq", None),
        P("fsdp"),
        P("fsdp", None),
        P("fsdp", None),
        P("fsdp"),
        P("fsdp", None),
        P("fsdp", None),
        P("fsdp"),
        P("fsdp"),
        P("fsdp", None),
    )
    out_specs = (
        P("fsdp", "seq", None),
        P("fsdp", "seq", None),
        P(("seq", "fsdp")),
        P(("seq", "fsdp"), None),
        P(("seq", "fsdp"), None),
        P(("seq", "fsdp")),
        P(("seq", "fsdp"), None),
        P(("seq", "fsdp"), None),
        P(("seq", "fsdp")),
        P(("seq", "fsdp")),
        P(("seq", "fsdp"), None),
    )
    return jax.shard_map(local, mesh=mesh, in_specs=in_specs, out_specs=out_specs, check_vma=False)
```

time: 2530 us -> 724 us (0.29)
  waiting for transfers between devices: 1450 us -> 131 us
  other arithmetic: 529 us -> 93.3 us
  local copies, waits for them, and re-layouts: 329 us -> 118 us
  starting transfers between devices: 5.9 us -> 140 us
  Pallas kernels: 0 us -> 127 us
  blocking collectives: 52.8 us -> 0 us
  matrix products: 131 us -> 99.1 us
    reduce_scatter x4 -> x0, waiting for transfers between devices: 1340 us -> none  [the longest x1 713 us: local(): lax.psum_scatter(jnp.einsum('td,tc->dc', lax.slice_in_dim(normed, 0, mode...]
    reduce_sum x418 -> x9, other arithmetic: 265 us -> 24.6 us  [the longest x1 5.6 us: local(): jnp.sum(d_logits.astype(f32), axis=0)]
    squeeze x272 -> x5, local copies, waits for them, and re-layouts: 194 us -> 0.18 us  [the longest x3 0.13 us: at(): return lax.dynamic_index_in_dim(stacked, index, 0, keepdims=False)]
    pallas_call x0 -> x3, Pallas kernels: none -> 127 us  [per_sequence(): pl.pallas_call(kernel, grid=(sequences,), in_specs=[spec(a) for a in oper...]
    ppermute x2 -> x66, starting transfers between devices: 5.01 us -> 126 us  [the longest x24 53.2 us: line_reduce(): received = lax.ppermute(part.astype(bf16), both, links)]
    ppermute x2 -> x66, waiting for transfers between devices: 4.14 us -> 120 us  [the longest x6 62.7 us: plane_gather(): lax.ppermute(value, 'seq', [(s, s ^ d) for s in range(count)])]
    add x49 -> x8, other arithmetic: 113 us -> 6.21 us  [the longest x3 2.85 us: line_reduce(): total = total + received.astype(f32)]
    all_gather x7 -> x0, waiting for transfers between devices: 103 us -> none  [the longest x1 49.3 us: forward_pass(): lax.all_gather(in_weight, 'fsdp', axis=0, tiled=True)]
  transfers between devices with their start and end apart: 14 -> 69, of which waited for: 9 -> 19; matrix products, arithmetic and copies ran while one was open for 23% -> 32% of each run, Pallas kernels for 0% -> 0%
where the time goes in v1:
time: 724 us; the launch traced here: 712 us
  starting transfers between devices  140 us (19%)
  waiting for transfers between devices  131 us (18%)
  Pallas kernels  127 us (18%)
  local copies, waits for them, and re-layouts  118 us (16%)
  matrix products  99.1 us (14%)
  other arithmetic  93.3 us (13%)
    pallas_call x3, Pallas kernels, per_sequence(): pl.pallas_call(kernel, grid=(sequences,), in_specs=[spec(a) for a in oper...  127 us
    ppermute x6, waiting for transfers between devices, plane_gather(): lax.ppermute(value, 'seq', [(s, s ^ d) for s in range(count)])  62.7 us
    unnamed x162, local copies, waits for them, and re-layouts  59.2 us
    ppermute x24, starting transfers between devices, line_reduce(): received = lax.ppermute(part.astype(bf16), both, links)  53.2 us
    ppermute x24, waiting for transfers between devices, line_reduce(): received = lax.ppermute(part.astype(bf16), both, links)  43 us
    ppermute x16, starting transfers between devices, swap(): return lax.ppermute(value, 'fsdp', [(0, 1), (1, 0)])  42.8 us
    dot_general x7, matrix products, matmul_nt(): lax.dot_general(left, right, (((1,), (1,)), ((), ())), preferred_element_...  40.5 us
    dot_general x7, matrix products, matmul(): return jnp.dot(left, right, preferred_element_type=f32)  37.1 us
  transfers between devices with their start and end apart: 69, of which 19 were waited for; matrix products, arithmetic and copies ran while one was open for 32% of the time, Pallas kernels for 0%

profile of v1, /device:TPU:1, one launch (start us, length us, event | category | flops | bytes accessed | tf_op | source)
XLA Modules:
  0.0 711.7 jit_solution(12765075523401860464)
XLA Ops:
  12.2 8.5 %constant_dynamic-slice_fusion.19 = (bf16[1024,2048]{1,0:T(8,128)(2,1)}, bf16[1024,2048]{1,0:T(8,128)(2,1)}) fusion(bf16[1024,8192]{1,0:T(8,128)(2,1)} %param.14, s32[]{:T(128)S(6)} %select_n.227, s32[]{:T(128)S(6)} %select_n.229), kind=kLoop, calls=%fused_computation.331 | loop fusion | bytes 16777224 | tf_op jit(solution)/shard_map/dynamic_slice | solution.py:338
  28.1 22.6 %collective-permute-done.57 = bf16[256,2048]{1,0:T(8,128)(2,1)} collective-permute-done((bf16[256,2048]{1,0:T(8,128)(2,1)}, bf16[256,2048]{1,0:T(8,128)(2,1)}, u32[]{:S(2)}, u32[]{:S(2)}) %collective-permute-start.57) | collective-permute-done | bytes 1048608 | tf_op jit(solution)/shard_map/ppermute | solution.py:239
  52.0 15.8 %collective-permute-done.56 = bf16[256,2048]{1,0:T(8,128)(2,1)S(1)} collective-permute-done((bf16[256,2048]{1,0:T(8,128)(2,1)}, bf16[256,2048]{1,0:T(8,128)(2,1)S(1)}, u32[]{:S(2)}, u32[]{:S(2)}) %collective-permute-start.56) | collective-permute-done | bytes 1048608 | tf_op jit(solution)/shard_map/ppermute | solution.py:239
  76.0 6.7 fusion.43
  85.1 6.8 fusion.47
  93.1 7.3 %fusion.70 = f32[512,2048]{1,0:T(8,128)S(1)} fusion(bf16[2048,2048]{1,0:T(8,128)(2,1)} %param.21, bf16[256,2048]{1,0:T(8,128)(2,1)} %collective-permute-done.5, bf16[256,2048]{1,0:T(8,128)(2,1)S(1)} %bitcast.875), kind=kOutput, calls=%fused_computation.120 | convolution fusion | flops 4299161600 | bytes 14680064 | tf_op jit(solution)/shard_map/dot_general | solution.py:24
  100.4 20.5 %collective-permute-done.13 = bf16[256,2048]{1,0:T(8,128)(2,1)S(1)} collective-permute-done((bf16[256,2048]{1,0:T(8,128)(2,1)}, bf16[256,2048]{1,0:T(8,128)(2,1)S(1)}, u32[]{:S(2)}, u32[]{:S(2)}) %collective-permute-start.13) | collective-permute-done | bytes 1048608 | tf_op jit(solution)/shard_map/ppermute | solution.py:239
  122.9 6.0 add_convert_fusion.1
  138.7 6.0 add_convert_fusion
  182.7 28.7 %summary.1 = (bf16[2,16,16,128]{3,2,1,0:T(8,128)(2,1)}, bf16[2,16,16,128]{3,2,1,0:T(8,128)(2,1)}, bf16[2,16,16,128]{3,2,1,0:T(8,128)(2,1)}) custom-call(f32[2,256,16,128]{3,2,1,0:T(8,128)} %bitcast.832, f32[2,256,16,128]{3,2,1,0:T(8,128)} %fusion.67.v_ref, f32[2,256,16,128]{3,2,1,0:T(8,128)} %bitcast.841, f32[2,256,16,128]{3,2,1,0:T(8,128)} %broadcast_in_dim.17.k_ref, ...), custom_call_target="tpu_custom_call" | custom-call | flops 150994944 | bytes 25559040 | tf_op jit(solution)/shard_map/summary/pallas_call | solution.py:201
  213.2 5.9 all-to-all-start
  223.8 6.0 all-to-all-done
  254.3 24.2 %forward.1 = (f32[2,256,16,128]{3,2,1,0:T(8,128)}, f32[2,8,16,16,128]{4,3,2,1,0:T(8,128)}) custom-call(f32[2,256,16,128]{3,2,1,0:T(8,128)} %bitcast.833, f32[2,256,16,128]{3,2,1,0:T(8,128)} %fusion.67.v_ref, f32[2,256,16,128]{3,2,1,0:T(8,128)} %broadcast_in_dim.17.k_ref, f32[2,256,16,128]{3,2,1,0:T(8,128)} %broadcast_in_dim.19.q_ref, ...), custom_call_target="tpu_custom_call" | custom-call | flops 117440512 | bytes 27525120 | tf_op jit(solution)/shard_map/forward/pallas_call | solution.py:201
  278.5 5.5 fusion.23
  285.3 9.4 %fusion.242 = f32[512,2048]{1,0:T(8,128)} fusion(bf16[512,2048]{1,0:T(8,128)(2,1)S(1)} %get-tuple-element.128, bf16[2048,2048]{1,0:T(8,128)(2,1)} %param.21), kind=kOutput, calls=%fused_computation.470 | convolution fusion | flops 4294967296 | bytes 14680064 | tf_op jit(solution)/shard_map/dot_general | solution.py:20
  298.0 74.3 %backward.1 = (f32[2,256,16,128]{3,2,1,0:T(8,128)}, f32[2,256,16,128]{3,2,1,0:T(8,128)}, f32[2,256,16,128]{3,2,1,0:T(8,128)}, f32[2,256,16,128]{3,2,1,0:T(8,128)}) custom-call(f32[2,256,16,128]{3,2,1,0:T(8,128)} %bitcast.834, f32[2,256,16,128]{3,2,1,0:T(8,128)} %fusion.67.v_ref, f32[2,256,16,128]{3,2,1,0:T(8,128)} %bitcast.842, ...), custom_call_target="tpu_custom_call" | custom-call | flops 385875968 | bytes 44302336 | tf_op jit(solution)/shard_map/backward/pallas_call | solution.py:201
  380.8 5.6 convert_reduce_fusion
  397.8 6.6 fusion.41
  405.9 5.7 constant_dynamic-slice_fusion.3
  415.8 6.5 fusion.244
  441.0 9.8 %fusion.6 = (f32[2048]{0:T(1024)S(1)}, f32[2048]{0:T(1024)S(1)}, f32[2048]{0:T(1024)S(1)}, f32[512,2048]{1,0:T(8,128)S(1)}) fusion(bf16[2,256,2048]{2,1,0:T(8,128)(2,1)} %bitcast.859, bf16[2,3,2048]{2,1,0:T(4,128)(2,1)S(1)} %collective-permute-done.3, f32[2,256,2048]{2,1,0:T(8,128)} %copy-done.5, bf16[512,160]{1,0:T(8,128)(2,1)S(1)} %fusion.134, ...), kind=kOutput, calls=%fused_computation.19 | convolution fusion | flops 372238336 | bytes 21848064 | tf_op jit(solution)/shard_map/dot_general | solution.py:24
  474.4 7.6 %fusion.14 = bf16[2,256,2048]{2,1,0:T(8,128)(2,1)S(1)} fusion(f32[2,3,2048]{2,1,0:T(4,128)S(1)} %collective-permute-done.9, f32[2,256,2048]{2,1,0:T(8,128)} %bitcast.844, f32[2048]{0:T(1024)S(1)} %bitcast.921, f32[2048]{0:T(1024)S(1)} %bitcast.919, f32[2048]{0:T(1024)S(1)} %bitcast.917, f32[2048]{0:T(1024)S(1)} %bitcast.915), kind=kLoop, calls=%fused_computation.27 | loop fusion | flops 11534336 | bytes 6373376 | tf_op jit(solution)/shard_map/convert_element_type | solution.py:506
  496.9 6.0 fusion.90
  507.7 7.4 %fusion.82 = f32[2048,512]{1,0:T(8,128)S(1)} fusion(bf16[2048,2048]{1,0:T(8,128)(2,1)} %fusion.115, bf16[512,512]{1,0:T(8,128)(2,1)} %collective-permute-done.31, bf16[512,512]{1,0:T(8,128)(2,1)S(1)} %collective-permute-done.30, bf16[512,512]{1,0:T(8,128)(2,1)S(1)} %collective-permute-done.29, bf16[512,512]{1,0:T(8,128)(2,1)S(1)} %copy-done.40), kind=kOutput, calls=%fused_computation.132 | convolution fusion | flops 4303355904 | bytes 14680064 | tf_op jit(solution)/shard_map/dot_general | solution.py:28
  516.0 6.8 collective-permute-done.43
  529.6 9.5 %collective-permute-start.10 = (f32[256,2048]{1,0:T(8,128)}, f32[256,2048]{1,0:T(8,128)}, u32[]{:S(2)}, u32[]{:S(2)}) collective-permute-start(f32[256,2048]{1,0:T(8,128)} %pad_maximum_fusion.3), channel_id=1, source_target_pairs={{0,1},{1,0},{2,3},{3,2},{4,5},{5,4},{6,7},{7,6},{8,9},{9,8},{10,11... | collective-permute-start | bytes 6291464 | tf_op jit(solution)/shard_map/ppermute | solution.py:37
  563.6 19.0 %collective-permute-done.19 = bf16[512,512]{1,0:T(8,128)(2,1)S(1)} collective-permute-done((bf16[512,512]{1,0:T(8,128)(2,1)S(1)}, bf16[512,512]{1,0:T(8,128)(2,1)S(1)}, u32[]{:S(2)}, u32[]{:S(2)}) %collective-permute-start.19) | collective-permute-done | bytes 524320 | tf_op jit(solution)/shard_map/ppermute | solution.py:282
  592.9 6.9 collective-permute-done.33
  615.2 6.8 collective-permute-start.60
  638.5 5.7 fusion.63
  658.1 11.2 %collective-permute-done.24 = bf16[512,512]{1,0:T(8,128)(2,1)S(1)} collective-permute-done((bf16[512,512]{1,0:T(8,128)(2,1)S(1)}, bf16[512,512]{1,0:T(8,128)(2,1)S(1)}, u32[]{:S(2)}, u32[]{:S(2)}) %collective-permute-start.24) | collective-permute-done | bytes 524320 | tf_op jit(solution)/shard_map/ppermute | solution.py:282
  692.3 15.8 %collective-permute-start.65 = (f32[128,2048]{1,0:T(8,128)S(1)}, f32[128,2048]{1,0:T(8,128)S(1)}, u32[]{:S(2)}, u32[]{:S(2)}) collective-permute-start(f32[128,2048]{1,0:T(8,128)S(1)} %dynamic-slice_bitcast_fusion), channel_id=1, source_target_pairs={{0,1},{1,0},{2,3},{3,2},{4,5},{5,4},{6,7},{7,6},{8,9},{9,8},{10,11... | collective-permute-start | bytes 3145736 | tf_op jit(solution)/shard_map/ppermute | solution.py:37
  (431 shorter events, 318.1 us)
Async XLA Ops:
  0.7 71.4 %collective-permute-start.5 = (bf16[256,2048]{1,0:T(8,128)(2,1)}, bf16[256,2048]{1,0:T(8,128)(2,1)}, u32[]{:S(2)}, u32[]{:S(2)}) collective-permute-start(bf16[256,2048]{1,0:T(8,128)(2,1)} %bitcast.871), channel_id=1, source_target_pairs={{0,1},{1,0},{2,3},{3,2},{4,5},{5,4},{6,7},{7,6},{8,9},{9,8},{10,11... | collective-permute-start | bytes 3145736 | tf_op jit(solution)/shard_map/ppermute | solution.py:37
  0.8 26.4 %collective-permute-start.55 = (bf16[256,2048]{1,0:T(8,128)(2,1)}, bf16[256,2048]{1,0:T(8,128)(2,1)}, u32[]{:S(2)}, u32[]{:S(2)}) collective-permute-start(bf16[256,2048]{1,0:T(8,128)(2,1)} %bitcast.872), channel_id=1, source_target_pairs={{0,2},{2,0},{4,6},{6,4},{8,10},{10,8},{12,14},{14,12},{16,18},{18,... | collective-permute-start | bytes 3145736 | tf_op jit(solution)/shard_map/ppermute | solution.py:239
  3.5 47.3 %collective-permute-start.57 = (bf16[256,2048]{1,0:T(8,128)(2,1)}, bf16[256,2048]{1,0:T(8,128)(2,1)}, u32[]{:S(2)}, u32[]{:S(2)}) collective-permute-start(bf16[256,2048]{1,0:T(8,128)(2,1)} %bitcast.873), channel_id=1, source_target_pairs={{0,6},{2,4},{4,2},{6,0},{8,14},{10,12},{12,10},{14,8},{16,22},{18,... | collective-permute-start | bytes 3145736 | tf_op jit(solution)/shard_map/ppermute | solution.py:239
  20.8 47.0 %collective-permute-start.56 = (bf16[256,2048]{1,0:T(8,128)(2,1)}, bf16[256,2048]{1,0:T(8,128)(2,1)S(1)}, u32[]{:S(2)}, u32[]{:S(2)}) collective-permute-start(bf16[256,2048]{1,0:T(8,128)(2,1)} %bitcast.874), channel_id=1, source_target_pairs={{0,4},{2,6},{4,0},{6,2},{8,12},{10,14},{12,8},{14,10},{16,20},{18,... | collective-permute-start | bytes 3145736 | tf_op jit(solution)/shard_map/ppermute | solution.py:239
  22.5 100.4 %collective-permute-start.2 = (bf16[1024,2048]{1,0:T(8,128)(2,1)}, bf16[1024,2048]{1,0:T(8,128)(2,1)}, u32[]{:S(2)}, u32[]{:S(2)}) collective-permute-start(bf16[1024,2048]{1,0:T(8,128)(2,1)} %get-tuple-element.125), channel_id=1, source_target_pairs={{0,1},{1,0},{2,3},{3,2},{4,5},{5,4},{6,7},{7,6},{8,9},{9,8},{10,11... | collective-permute-start | bytes 12582920 | tf_op jit(solution)/shard_map/ppermute | solution.py:37
  27.2 111.5 %collective-permute-start.6 = (bf16[1024,2048]{1,0:T(8,128)(2,1)S(1)}, bf16[1024,2048]{1,0:T(8,128)(2,1)}, u32[]{:S(2)}, u32[]{:S(2)}) collective-permute-start(bf16[1024,2048]{1,0:T(8,128)(2,1)S(1)} %copy-done.26), channel_id=1, source_target_pairs={{0,1},{1,0},{2,3},{3,2},{4,5},{5,4},{6,7},{7,6},{8,9},{9,8},{10,11... | collective-permute-start | bytes 12582920 | tf_op jit(solution)/shard_map/ppermute | solution.py:37
  50.7 41.1 %collective-permute-start.12 = (bf16[256,2048]{1,0:T(8,128)(2,1)}, bf16[256,2048]{1,0:T(8,128)(2,1)S(1)}, u32[]{:S(2)}, u32[]{:S(2)}) collective-permute-start(bf16[256,2048]{1,0:T(8,128)(2,1)} %get-tuple-element.101), channel_id=1, source_target_pairs={{0,2},{2,0},{4,6},{6,4},{8,10},{10,8},{12,14},{14,12},{16,18},{18,... | collective-permute-start | bytes 3145736 | tf_op jit(solution)/shard_map/ppermute | solution.py:239
  67.7 32.6 %collective-permute-start.14 = (bf16[256,2048]{1,0:T(8,128)(2,1)}, bf16[256,2048]{1,0:T(8,128)(2,1)S(1)}, u32[]{:S(2)}, u32[]{:S(2)}) collective-permute-start(bf16[256,2048]{1,0:T(8,128)(2,1)} %get-tuple-element.101), channel_id=1, source_target_pairs={{0,6},{2,4},{4,2},{6,0},{8,14},{10,12},{12,10},{14,8},{16,22},{18,... | collective-permute-start | bytes 3145736 | tf_op jit(solution)/shard_map/ppermute | solution.py:239
  72.1 60.0 %collective-permute-start.58 = (bf16[3,256,2048]{2,1,0:T(8,128)(2,1)S(1)}, bf16[3,256,2048]{2,1,0:T(8,128)(2,1)S(1)}, u32[]{:S(2)}, u32[]{:S(2)}) collective-permute-start(bf16[3,256,2048]{2,1,0:T(8,128)(2,1)S(1)} %pad_maximum_fusion.2), channel_id=1, source_target_pairs={{0,1},{1,0},{2,3},{3,2},{4,5},{5,4},{6,7},{7,6},{8,9},{9,8},{10,11... | collective-permute-start | bytes 9437192 | tf_op jit(solution)/shard_map/ppermute | solution.py:37
  91.8 29.0 %collective-permute-start.13 = (bf16[256,2048]{1,0:T(8,128)(2,1)}, bf16[256,2048]{1,0:T(8,128)(2,1)S(1)}, u32[]{:S(2)}, u32[]{:S(2)}) collective-permute-start(bf16[256,2048]{1,0:T(8,128)(2,1)} %get-tuple-element.101), channel_id=1, source_target_pairs={{0,4},{2,6},{4,0},{6,2},{8,12},{10,14},{12,8},{14,10},{16,20},{18,... | collective-permute-start | bytes 3145736 | tf_op jit(solution)/shard_map/ppermute | solution.py:239
  121.2 23.5 %collective-permute-start.15 = (bf16[3,256,2048]{2,1,0:T(8,128)(2,1)S(1)}, bf16[3,256,2048]{2,1,0:T(8,128)(2,1)S(1)}, u32[]{:S(2)}, u32[]{:S(2)}) collective-permute-start(bf16[3,256,2048]{2,1,0:T(8,128)(2,1)S(1)} %pad_maximum_fusion.1), channel_id=1, source_target_pairs={{0,1},{1,0},{2,3},{3,2},{4,5},{5,4},{6,7},{7,6},{8,9},{9,8},{10,11... | collective-permute-start | bytes 9437192 | tf_op jit(solution)/shard_map/ppermute | solution.py:37
  394.4 44.1 %collective-permute-start.8 = (f32[2,256,160]{1,2,0:T(8,128)}, f32[2,256,160]{1,2,0:T(8,128)}, u32[]{:S(2)}, u32[]{:S(2)}) collective-permute-start(f32[2,256,160]{1,2,0:T(8,128)} %rev.7), channel_id=1, source_target_pairs={{0,1},{1,0},{2,3},{3,2},{4,5},{5,4},{6,7},{7,6},{8,9},{9,8},{10,11... | collective-permute-start | bytes 983048 | tf_op jit(solution)/shard_map/ppermute | solution.py:37
  405.9 228.6 %collective-permute-start.7 = (f32[256,2048]{1,0:T(8,128)}, f32[256,2048]{1,0:T(8,128)}, u32[]{:S(2)}, u32[]{:S(2)}) collective-permute-start(f32[256,2048]{1,0:T(8,128)} %slice.398), channel_id=1, source_target_pairs={{0,1},{1,0},{2,3},{3,2},{4,5},{5,4},{6,7},{7,6},{8,9},{9,8},{10,11... | collective-permute-start | bytes 6291464 | tf_op jit(solution)/shard_map/ppermute | solution.py:37
  415.1 79.9 %collective-permute-start.53 = (bf16[512,512]{0,1:T(8,128)(2,1)}, bf16[512,512]{0,1:T(8,128)(2,1)}, u32[]{:S(2)}, u32[]{:S(2)}) collective-permute-start(bf16[512,512]{0,1:T(8,128)(2,1)} %bitcast.181), channel_id=1, source_target_pairs={{0,4},{2,6},{4,0},{6,2},{8,12},{10,14},{12,8},{14,10},{16,20},{18,... | collective-permute-start | bytes 1572872 | tf_op jit(solution)/shard_map/ppermute | solution.py:247
  424.5 78.3 %collective-permute-start.31 = (bf16[512,512]{1,0:T(8,128)(2,1)}, bf16[512,512]{1,0:T(8,128)(2,1)}, u32[]{:S(2)}, u32[]{:S(2)}) collective-permute-start(bf16[512,512]{1,0:T(8,128)(2,1)} %get-tuple-element.150), channel_id=1, source_target_pairs={{0,6},{2,4},{4,2},{6,0},{8,14},{10,12},{12,10},{14,8},{16,22},{18,... | collective-permute-start | bytes 1572872 | tf_op jit(solution)/shard_map/ppermute | solution.py:247
  429.1 65.1 %collective-permute-start.54 = (bf16[512,512]{0,1:T(8,128)(2,1)}, bf16[512,512]{0,1:T(8,128)(2,1)}, u32[]{:S(2)}, u32[]{:S(2)}) collective-permute-start(bf16[512,512]{0,1:T(8,128)(2,1)} %bitcast.891), channel_id=1, source_target_pairs={{0,6},{2,4},{4,2},{6,0},{8,14},{10,12},{12,10},{14,8},{16,22},{18,... | collective-permute-start | bytes 1572872 | tf_op jit(solution)/shard_map/ppermute | solution.py:247
  451.7 21.8 %collective-permute-start.9 = (f32[2,3,2048]{2,1,0:T(4,128)S(1)}, f32[2,3,2048]{2,1,0:T(4,128)S(1)}, u32[]{:S(2)}, u32[]{:S(2)}) collective-permute-start(f32[2,3,2048]{2,1,0:T(4,128)S(1)} %slice.400), channel_id=1, source_target_pairs={{2,0},{4,2},{6,4},{8,6},{10,8},{12,10},{14,12},{16,14},{18,16},{20... | collective-permute-start | bytes 147464 | tf_op jit(solution)/shard_map/ppermute | solution.py:500
  473.5 22.4 %collective-permute-start.52 = (bf16[512,512]{0,1:T(8,128)(2,1)S(1)}, bf16[512,512]{0,1:T(8,128)(2,1)S(1)}, u32[]{:S(2)}, u32[]{:S(2)}) collective-permute-start(bf16[512,512]{0,1:T(8,128)(2,1)S(1)} %bitcast.890), channel_id=1, source_target_pairs={{0,2},{2,0},{4,6},{6,4},{8,10},{10,8},{12,14},{14,12},{16,18},{18,... | collective-permute-start | bytes 1572872 | tf_op jit(solution)/shard_map/ppermute | solution.py:247
  506.6 32.5 %collective-permute-start.18 = (bf16[512,512]{1,0:T(8,128)(2,1)S(1)}, bf16[512,512]{1,0:T(8,128)(2,1)S(1)}, u32[]{:S(2)}, u32[]{:S(2)}) collective-permute-start(bf16[512,512]{1,0:T(8,128)(2,1)S(1)} %get-tuple-element.154), channel_id=1, source_target_pairs={{0,6},{2,4},{4,2},{6,0},{8,14},{10,12},{12,10},{14,8},{16,22},{18,... | collective-permute-start | bytes 1572872 | tf_op jit(solution)/shard_map/ppermute | solution.py:247
  515.1 29.9 %collective-permute-start.17 = (bf16[512,512]{1,0:T(8,128)(2,1)S(1)}, bf16[512,512]{1,0:T(8,128)(2,1)S(1)}, u32[]{:S(2)}, u32[]{:S(2)}) collective-permute-start(bf16[512,512]{1,0:T(8,128)(2,1)S(1)} %get-tuple-element.155), channel_id=1, source_target_pairs={{0,4},{2,6},{4,0},{6,2},{8,12},{10,14},{12,8},{14,10},{16,20},{18,... | collective-permute-start | bytes 1572872 | tf_op jit(solution)/shard_map/ppermute | solution.py:247
  522.8 23.0 %collective-permute-start.16 = (bf16[512,512]{1,0:T(8,128)(2,1)S(1)}, bf16[512,512]{1,0:T(8,128)(2,1)S(1)}, u32[]{:S(2)}, u32[]{:S(2)}) collective-permute-start(bf16[512,512]{1,0:T(8,128)(2,1)S(1)} %get-tuple-element.156), channel_id=1, source_target_pairs={{0,2},{2,0},{4,6},{6,4},{8,10},{10,8},{12,14},{14,12},{16,18},{18,... | collective-permute-start | bytes 1572872 | tf_op jit(solution)/shard_map/ppermute | solution.py:247
  529.6 94.8 %collective-permute-start.10 = (f32[256,2048]{1,0:T(8,128)}, f32[256,2048]{1,0:T(8,128)}, u32[]{:S(2)}, u32[]{:S(2)}) collective-permute-start(f32[256,2048]{1,0:T(8,128)} %pad_maximum_fusion.3), channel_id=1, source_target_pairs={{0,1},{1,0},{2,3},{3,2},{4,5},{5,4},{6,7},{7,6},{8,9},{9,8},{10,11... | collective-permute-start | bytes 6291464 | tf_op jit(solution)/shard_map/ppermute | solution.py:37
  539.1 22.8 %collective-permute-start.32 = (bf16[512,512]{1,0:T(8,128)(2,1)S(1)}, bf16[512,512]{1,0:T(8,128)(2,1)S(1)}, u32[]{:S(2)}, u32[]{:S(2)}) collective-permute-start(bf16[512,512]{1,0:T(8,128)(2,1)S(1)} %get-tuple-element.137), channel_id=1, source_target_pairs={{0,8},{1,9},{2,10},{3,11},{4,12},{5,13},{6,14},{7,15}} | collective-permute-start | bytes 1572872 | tf_op jit(solution)/shard_map/ppermute | solution.py:282
  554.4 33.8 %collective-permute-start.59 = (bf16[256,2048]{1,0:T(8,128)(2,1)S(1)}, bf16[256,2048]{1,0:T(8,128)(2,1)S(1)}, u32[]{:S(2)}, u32[]{:S(2)}) collective-permute-start(bf16[256,2048]{1,0:T(8,128)(2,1)S(1)} %get-tuple-element.133), channel_id=1, source_target_pairs={{1,9},{3,11},{5,13},{7,15}} | collective-permute-start | bytes 3145736 | tf_op jit(solution)/shard_map/ppermute | solution.py:282
  558.0 24.6 %collective-permute-start.19 = (bf16[512,512]{1,0:T(8,128)(2,1)S(1)}, bf16[512,512]{1,0:T(8,128)(2,1)S(1)}, u32[]{:S(2)}, u32[]{:S(2)}) collective-permute-start(bf16[512,512]{1,0:T(8,128)(2,1)S(1)} %get-tuple-element.141), channel_id=1, source_target_pairs={{0,8},{1,9},{2,10},{3,11},{4,12},{5,13},{6,14},{7,15}} | collective-permute-start | bytes 1572872 | tf_op jit(solution)/shard_map/ppermute | solution.py:282
  562.8 20.6 %collective-permute-start.47 = (bf16[256,384]{1,0:T(8,128)(2,1)S(1)}, bf16[256,384]{1,0:T(8,128)(2,1)S(1)}, u32[]{:S(2)}, u32[]{:S(2)}) collective-permute-start(bf16[256,384]{1,0:T(8,128)(2,1)S(1)} %get-tuple-element.169), channel_id=1, source_target_pairs={{0,8},{2,10},{4,12},{6,14},{9,17},{11,19},{13,21},{15,23},{17,25},... | collective-permute-start | bytes 589832 | tf_op jit(solution)/shard_map/ppermute | solution.py:282
  605.8 41.4 %collective-permute-start.62 = (bf16[256,2048]{1,0:T(8,128)(2,1)}, bf16[256,2048]{1,0:T(8,128)(2,1)}, u32[]{:S(2)}, u32[]{:S(2)}) collective-permute-start(bf16[256,2048]{1,0:T(8,128)(2,1)} %get-tuple-element.134), channel_id=1, source_target_pairs={{24,16},{26,18},{28,20},{30,22}} | collective-permute-start | bytes 3145736 | tf_op jit(solution)/shard_map/ppermute | solution.py:282
  607.5 46.2 %collective-permute-start.34 = (bf16[512,512]{1,0:T(8,128)(2,1)S(1)}, bf16[512,512]{1,0:T(8,128)(2,1)}, u32[]{:S(2)}, u32[]{:S(2)}) collective-permute-start(bf16[512,512]{1,0:T(8,128)(2,1)S(1)} %get-tuple-element.135), channel_id=1, source_target_pairs={{0,8},{1,9},{2,10},{3,11},{4,12},{5,13},{6,14},{7,15},{8,16},{9,17... | collective-permute-start | bytes 1572872 | tf_op jit(solution)/shard_map/ppermute | solution.py:282
  615.2 33.3 %collective-permute-start.60 = (bf16[256,2048]{1,0:T(8,128)(2,1)}, bf16[256,2048]{1,0:T(8,128)(2,1)}, u32[]{:S(2)}, u32[]{:S(2)}) collective-permute-start(bf16[256,2048]{1,0:T(8,128)(2,1)} %fusion.100), channel_id=1, source_target_pairs={{1,9},{3,11},{5,13},{7,15},{9,17},{11,19},{13,21},{15,23}} | collective-permute-start | bytes 3145736 | tf_op jit(solution)/shard_map/ppermute | solution.py:282
  647.2 22.2 %collective-permute-start.24 = (bf16[512,512]{1,0:T(8,128)(2,1)S(1)}, bf16[512,512]{1,0:T(8,128)(2,1)S(1)}, u32[]{:S(2)}, u32[]{:S(2)}) collective-permute-start(bf16[512,512]{1,0:T(8,128)(2,1)S(1)} %fusion.124), channel_id=1, source_target_pairs={{8,0},{9,1},{10,2},{11,3},{12,4},{13,5},{14,6},{15,7},{16,8},{17,9... | collective-permute-start | bytes 1572872 | tf_op jit(solution)/shard_map/ppermute | solution.py:282
  648.5 25.9 %collective-permute-start.11 = (f32[64]{0:T(128)S(1)}, f32[64]{0:T(128)S(1)}, u32[]{:S(2)}, u32[]{:S(2)}) collective-permute-start(f32[64]{0:T(128)S(1)} %fusion.189), channel_id=1, source_target_pairs={{0,1},{1,0},{2,3},{3,2},{4,5},{5,4},{6,7},{7,6},{8,9},{9,8},{10,11... | collective-permute-start | bytes 776 | tf_op jit(solution)/shard_map/ppermute | solution.py:37
  653.7 36.7 %collective-permute-start.63 = (bf16[256,2048]{1,0:T(8,128)(2,1)S(1)}, bf16[256,2048]{1,0:T(8,128)(2,1)S(1)}, u32[]{:S(2)}, u32[]{:S(2)}) collective-permute-start(bf16[256,2048]{1,0:T(8,128)(2,1)S(1)} %get-tuple-element.132), channel_id=1, source_target_pairs={{16,8},{18,10},{20,12},{22,14},{24,16},{26,18},{28,20},{30,22}} | collective-permute-start | bytes 3145736 | tf_op jit(solution)/shard_map/ppermute | solution.py:282
  (97 other events, 1767.1 us)

commit v2 on v1

v2 whole, which is shorter than its diff:
```python
import functools

import jax
import jax.numpy as jnp
from jax import lax
from jax.experimental import pallas as pl
from jax.experimental.pallas import tpu as pltpu
from jax.sharding import PartitionSpec as P

f32 = jnp.float32
bf16 = jnp.bfloat16
epsilon = 1e-05
lanes = 128
group = 4
span = 16
batch = 8
narrow = 2
seq = ("outer", "member")


def matmul(left, right):
    return jnp.dot(left, right, preferred_element_type=f32)


def matmul_nt(left, right):
    return lax.dot_general(left, right, (((1,), (1,)), ((), ())), preferred_element_type=f32)


def matmul_tn(left, right):
    return lax.dot_general(left, right, (((0,), (0,)), ((), ())), preferred_element_type=f32)


def swish_slope(value):
    logistic = jax.nn.sigmoid(value)
    return logistic * (1.0 + value * (1.0 - logistic))


def together(*values):
    return lax.optimization_barrier(values)


def swap(value):
    return lax.ppermute(value, "fsdp", [(0, 1), (1, 0)])


def at(stacked, index):
    return lax.dynamic_index_in_dim(stacked, index, 0, keepdims=False)


def column(j):
    return pl.ds(j * lanes, lanes)


def eights(ref):
    return ref.reshape(ref.shape[0] // 8, 8, ref.shape[1])


def tall(ref, base, step, j):
    return jnp.broadcast_to(ref[base + step // 8, pl.ds(step % 8, 1), column(j)], (8, lanes))


def spread_columns(sel_ref, first, states, targets):
    length = sel_ref.shape[1]
    for i in range(states):
        value = jnp.broadcast_to(sel_ref[0, :, first + i : first + i + 1], (length, lanes))
        for target, apply in targets:
            target.reshape(length * states, lanes)[pl.ds(i, length, stride=states), :] = apply(
                value
            )


def gate_of(low_rank, weight_ref, bias_ref, j):
    logits = matmul_nt(low_rank, weight_ref[pl.ds(j * lanes, lanes), :])
    return jax.nn.sigmoid(logits + bias_ref[:, column(j)])


def key_sum(sel_ref, rank, states):
    keys = sel_ref[0, :, rank : rank + states]
    return jnp.sum(keys * keys, axis=1, keepdims=True)


def halves(ref, position, states):
    return [ref[position, pl.ds(h, 8), :] for h in range(0, states, 8)]


def summary_kernel(
    sel_ref, act_ref, gate_ref, db_ref, bw_ref, bb_ref, r_ref, f_ref, d_ref, sum_ref, kb, k2b, qb
):
    length, half = act_ref.shape[1], act_ref.shape[2]
    states = kb.shape[1]
    rank = bw_ref.shape[1]
    tiles = half // lanes
    spread_columns(sel_ref, rank, states, [(kb, lambda v: v), (k2b, lambda v: v * v)])
    spread_columns(sel_ref, rank + states, states, [(qb, lambda v: v)])
    norm = key_sum(sel_ref, rank, states)
    low_rank = sel_ref[0, :, :rank].astype(bf16)
    for j in range(tiles):
        beta = gate_of(low_rank, bw_ref, bb_ref, j)
        rate = beta / (1.0 + beta * norm)
        r_ref[0, :, column(j)] = rate
        f_ref[0, :, column(j)] = rate * act_ref[0, :, column(j)].astype(f32)
        gate = gate_ref[0, :, column(j)].astype(f32)
        d_ref[0, :, column(j)] = db_ref[0, :, column(j)] * (gate * jax.nn.sigmoid(gate))
    zero = jnp.zeros((8, lanes), f32)
    one = jnp.ones((8, lanes), f32)
    group = range(states // 8)
    rates, feds, outs = (eights(ref.at[0]) for ref in (r_ref, f_ref, d_ref))
    for first in range(0, tiles, batch):
        places = [(h, j) for j in range(first, first + batch) for h in group]

        def body(lap, carry):
            product, current, grads = (list(part) for part in carry)
            for step in range(8):
                position = pl.multiple_of(lap * 8, 8) + step
                key, square, query = (halves(ref, position, states) for ref in (kb, k2b, qb))
                for n, (h, j) in enumerate(places):
                    fading = 1.0 - square[h] * tall(rates, lap, step, j)
                    current[n] = fading * current[n] + key[h] * tall(feds, lap, step, j)
                    product[n] = product[n] * fading
                    grads[n] = grads[n] + product[n] * (query[h] * tall(outs, lap, step, j))
            return (tuple(product), tuple(current), tuple(grads))

        size = len(places)
        product, current, grads = lax.fori_loop(
            0, length // 8, body, ((one,) * size, (zero,) * size, (zero,) * size)
        )
        for kind, parts in enumerate((product, current, grads)):
            for n in range(0, size, states // 8):
                whole = jnp.concatenate(parts[n : n + states // 8])
                sum_ref[places[n][1], kind] = whole.astype(sum_ref.dtype)


def advance(rates, feds, key, square, base, step, current, places):
    for n, (h, j) in enumerate(places):
        fading = 1.0 - square[h] * tall(rates, base, step, j)
        current[n] = fading * current[n] + key[h] * tall(feds, base, step, j)


def keep(ref, step, states, places, parts):
    by_tile = {}
    for (h, j), part in zip(places, parts):
        by_tile.setdefault(j, []).append(part)
    for j, both in by_tile.items():
        ref[pl.ds(step * states, states), column(j)] = jnp.concatenate(both).astype(bf16)


def forward_kernel(
    sel_ref,
    r_ref,
    f_ref,
    init_ref,
    act_ref,
    gate_ref,
    db_ref,
    qd_ref,
    skip_ref,
    gate_out,
    branch_out,
    branch_ref,
    start_ref,
    term_ref,
    kb,
    k2b,
    state,
    hist,
    held,
):
    length, half = act_ref.shape[1], act_ref.shape[2]
    states = init_ref.shape[2]
    tiles = half // lanes
    rank = sel_ref.shape[2] - 2 * states
    parts = range(states // 8)
    spread_columns(sel_ref, rank, states, [(kb, lambda v: v), (k2b, lambda v: v * v)])
    for j in range(tiles):
        state[:, column(j)] = init_ref[j, 0].astype(f32)
    rates, feds = (eights(ref.at[0]) for ref in (r_ref, f_ref))

    def block(index, carry):
        base = pl.multiple_of(index * span, span)
        start_ref[0, index] = state[...]
        for first in range(0, tiles, batch):
            places = [(h, j) for j in range(first, first + batch) for h in parts]
            current = [state[pl.ds(h * 8, 8), column(j)] for h, j in places]
            for step in range(span):
                key, square = (halves(ref, base + step, states) for ref in (kb, k2b))
                advance(rates, feds, key, square, index * (span // 8), step, current, places)
                keep(hist, step, states, places, current)
            for n, (h, j) in enumerate(places):
                state[pl.ds(h * 8, 8), column(j)] = current[n]
        held[pl.ds(base, span), :] = matmul(qd_ref[0, pl.ds(base, span), :], hist[...])
        return carry

    lax.fori_loop(0, length // span, block, 0)
    width = half // group
    outer_half = branch_out.shape[0] // 2
    owned = branch_out.shape[2] // group
    for j in range(tiles):
        value = act_ref[0, :, column(j)].astype(f32)
        skip_sum = held[:, column(j)] + skip_ref[:, column(j)] * value
        gate = gate_ref[0, :, column(j)].astype(f32)
        logistic = jax.nn.sigmoid(gate)
        swish = gate * logistic
        d_branch = db_ref[0, :, column(j)]
        branch = (skip_sum * swish).astype(bf16)
        d_gate = (d_branch * skip_sum * (logistic * (1.0 + gate * (1.0 - logistic)))).astype(bf16)
        term_ref[0, :, column(j)] = jnp.sum(d_branch * swish * value, axis=0, keepdims=True)
        branch_ref[0, :, column(j)] = branch
        member, offset = divmod(j * lanes, width)
        gate_out[member, :, pl.ds(offset, lanes)] = d_gate
        for inside in range(0, lanes, owned):
            owner = (j * lanes + inside) // owned
            outer = owner % 2 * outer_half + owner // (2 * group)
            offset = owner // 2 % group * owned
            branch_out[outer, :, offset : offset + owned] = branch[:, inside : inside + owned]


def backward_kernel(
    sel_ref,
    r_ref,
    f_ref,
    d_ref,
    act_ref,
    start_ref,
    last_ref,
    kd_ref,
    bw_ref,
    bb_ref,
    skip_ref,
    dlog_ref,
    dsel_ref,
    base_ref,
    bias_ref,
    kb,
    k2b,
    qb,
    v_s,
    before,
    s_hist,
    g_hist,
    w_hist,
    grad_s,
    dr_s,
    dk_s,
    dq_s,
):
    length, half = act_ref.shape[1], act_ref.shape[2]
    states = last_ref.shape[2]
    tiles = half // lanes
    rank = bw_ref.shape[1]
    group = range(states // 8)
    blocks = length // span
    spread_columns(sel_ref, rank, states, [(kb, lambda v: v), (k2b, lambda v: v * v)])
    spread_columns(sel_ref, rank + states, states, [(qb, lambda v: v)])
    v_s[...] = act_ref[0].astype(f32)
    rates, feds, outs, values = (eights(ref) for ref in (r_ref.at[0], f_ref.at[0], d_ref.at[0], v_s))
    for j in range(tiles):
        grad_s[:, column(j)] = last_ref[j, 0].astype(f32)
    wide = span * states
    own = lax.broadcasted_iota(jnp.int32, (span, wide), 1) // states == lax.broadcasted_iota(
        jnp.int32, (span, wide), 0
    )

    def block(lap, carry):
        index = blocks - 1 - lap
        base = pl.multiple_of(index * span, span)
        eight = index * (span // 8)
        rows = pl.ds(base, span)
        diagonal = kd_ref[0, rows, :]
        d_query, d_key = None, None
        for first in range(0, tiles, narrow):
            places = [(h, j) for j in range(first, first + narrow) for h in group]
            cols = pl.ds(first * lanes, narrow * lanes)
            current = [start_ref[0, index, pl.ds(h * 8, 8), column(j)] for h, j in places]
            for step in range(span):
                for n, (h, j) in enumerate(places):
                    before[step, pl.ds(h * 8, 8), column(j)] = current[n]
                key, square = (halves(ref, base + step, states) for ref in (kb, k2b))
                advance(rates, feds, key, square, eight, step, current, places)
                keep(s_hist, step, states, places, current)
            part = matmul_nt(s_hist[:, cols], d_ref[0, rows, cols].astype(bf16))
            d_query = part if d_query is None else d_query + part
        for first in range(0, tiles, narrow):
            places = [(h, j) for j in range(first, first + narrow) for h in group]
            cols = pl.ds(first * lanes, narrow * lanes)
            grads = [grad_s[pl.ds(h * 8, 8), column(j)] for h, j in places]
            for step in reversed(range(span)):
                key, square, query = (halves(ref, base + step, states) for ref in (kb, k2b, qb))
                full, left = [], []
                for n, (h, j) in enumerate(places):
                    grad = grads[n] + query[h] * tall(outs, eight, step, j)
                    kept = key[h] * before[step, pl.ds(h * 8, 8), column(j)]
                    full.append(grad)
                    left.append(grad * (tall(values, eight, step, j) - kept))
                    grads[n] = grad * (1.0 - square[h] * tall(rates, eight, step, j))
                keep(g_hist, step, states, places, full)
                keep(w_hist, step, states, places, left)
            for n, (h, j) in enumerate(places):
                grad_s[pl.ds(h * 8, 8), column(j)] = grads[n]
            block_rates = r_ref[0, rows, cols]
            dr_s[rows, cols] = matmul(diagonal, w_hist[:, cols])
            base_ref[0, rows, cols] = block_rates * matmul(diagonal, g_hist[:, cols])
            part = matmul_nt(w_hist[:, cols], (2.0 * block_rates).astype(bf16)) - matmul_nt(
                g_hist[:, cols], f_ref[0, rows, cols].astype(bf16)
            )
            d_key = part if d_key is None else d_key + part
        dq_s[rows, :] = jnp.where(own, d_query.T, 0.0)
        dk_s[rows, :] = jnp.where(own, d_key.T, 0.0)
        return carry

    lax.fori_loop(0, blocks, block, 0)

    norm = key_sum(sel_ref, rank, states)
    low_rank = sel_ref[0, :, :rank].astype(bf16)
    d_norm = jnp.zeros((length, lanes), f32)
    for j in range(tiles):
        beta = gate_of(low_rank, bw_ref, bb_ref, j)
        inverse = 1.0 / (1.0 + beta * norm)
        rate = beta * inverse
        d_rate = dr_s[:, column(j)]
        d_norm = d_norm - d_rate * (rate * rate)
        d_logits = (d_rate * (inverse * inverse) * (beta * (1.0 - beta))).astype(bf16)
        dlog_ref[0, :, column(j)] = d_logits
        bias_ref[0, :, column(j)] = jnp.sum(d_logits.astype(f32), axis=0, keepdims=True)
        base_ref[0, :, column(j)] += d_ref[0, :, column(j)] * skip_ref[:, column(j)]
    d_norm = 2.0 * jnp.sum(d_norm, axis=1, keepdims=True)
    dsel_ref[0, :, :rank] = matmul(dlog_ref[0], bw_ref[...])

    def folded(ref):
        total = ref[:, :lanes]
        for first in range(lanes, wide, lanes):
            total = total + ref[:, first : first + lanes]
        size = lanes // 2
        while size >= states:
            total = total + pltpu.roll(total, size, 1)
            size //= 2
        return total[:, : 2 * states]

    place = lax.broadcasted_iota(jnp.int32, (length, 2 * states), 1)
    keys = sel_ref[0, :, rank:]
    dsel_ref[0, :, rank:] = jnp.where(place < states, folded(dk_s) + keys * d_norm, folded(dq_s))


def correlate_kernel(taps, split, d_ref, later_ref, w_ref, out_ref, held):
    length, half = d_ref.shape[1], d_ref.shape[2]
    width = half // split
    for j in range(half // lanes):
        held[:length, :] = d_ref[0, :, column(j)]
        held[length:, :] = later_ref[0, :, column(j)]
        total = None
        for tap in range(taps):
            part = w_ref[tap : tap + 1, column(j)] * held[pl.ds(taps - 1 - tap, length), :]
            total = part if total is None else total + part
        member, offset = divmod(j * lanes, width)
        out_ref[member, :, pl.ds(offset, lanes)] = total.astype(bf16)


def copy_kernel(core_ref, in_ref, out_ref):
    out_ref[...] = in_ref[...]


def other_columns(core, in_weight, gate):
    half_model, half = in_weight.shape[0], in_weight.shape[1] // 4
    wide = half // group
    first = 2 * group if gate else 0
    return pl.pallas_call(
        copy_kernel,
        grid_spec=pltpu.PrefetchScalarGridSpec(
            num_scalar_prefetch=1,
            grid=(group,),
            in_specs=[
                pl.BlockSpec(
                    (half_model, wide), lambda n, core: (0, first + group * (1 - core[0]) + n)
                )
            ],
            out_specs=pl.BlockSpec((half_model, wide), lambda n, core: (0, n)),
        ),
        out_shape=shape(half_model, half, dtype=bf16),
        name="columns",
    )(core, in_weight)


def whole_kernel(transposed, left_ref, right_ref, out_ref):
    product = matmul_nt if transposed else matmul
    out_ref[...] = product(left_ref[...], right_ref[...])


def run_product(left, right, transposed, micros):
    rows, depth = left.shape
    columns = right.shape[0 if transposed else 1]
    wide = 4 * lanes
    right_spec = (
        pl.BlockSpec((wide, depth), lambda n: (n, 0))
        if transposed
        else pl.BlockSpec((depth, wide), lambda n: (0, n))
    )
    return pl.pallas_call(
        functools.partial(whole_kernel, transposed),
        grid=(columns // wide,),
        in_specs=[pl.BlockSpec((rows, depth), lambda n: (0, 0)), right_spec],
        out_specs=pl.BlockSpec((rows, wide), lambda n: (0, n)),
        out_shape=shape(rows, columns),
        compiler_params=pltpu.CompilerParams(vmem_limit_bytes=40 * 2**20),
        cost_estimate=pl.CostEstimate(
            flops=int(micros * 1.15e9), bytes_accessed=1 << 20, transcendentals=0
        ),
        name="product",
    )(left, right)


def project_kernel(core_ref, x_ref, own_ref, got_ref, out_ref):
    size = own_ref.shape[0]
    mine = pl.multiple_of(core_ref[0] * size, size)
    other = pl.multiple_of((1 - core_ref[0]) * size, size)
    out_ref[...] = (
        matmul(x_ref[:, pl.ds(mine, size)], own_ref[...])
        + matmul(x_ref[:, pl.ds(other, size)], got_ref[...])
    ).astype(out_ref.dtype)


def run_project(core, normed, in_weight, got, gate, micros):
    rows, model = normed.shape
    half_model, half = got.shape
    wide = half // group
    first = 2 * group if gate else 0
    return pl.pallas_call(
        project_kernel,
        grid_spec=pltpu.PrefetchScalarGridSpec(
            num_scalar_prefetch=1,
            grid=(group,),
            in_specs=[
                pl.BlockSpec((rows, model), lambda n, core: (0, 0)),
                pl.BlockSpec((half_model, wide), lambda n, core: (0, first + group * core[0] + n)),
                pl.BlockSpec((half_model, wide), lambda n, core: (0, n)),
            ],
            out_specs=pl.BlockSpec((rows, wide), lambda n, core: (0, n)),
        ),
        out_shape=shape(rows, half, dtype=bf16),
        compiler_params=pltpu.CompilerParams(vmem_limit_bytes=40 * 2**20),
        cost_estimate=pl.CostEstimate(
            flops=int(micros * 1.15e9), bytes_accessed=2 * half_model * half * 2, transcendentals=0
        ),
        name="project",
    )(core, normed, in_weight, got)


def normed_kernel(
    core_ref,
    inner_ref,
    gate_ref,
    inner_own,
    gate_own,
    inner_got,
    gate_got,
    kept_ref,
    sent_ref,
    inner_flat,
    gate_flat,
    total,
):
    lap = pl.program_id(0)
    length = kept_ref.shape[0]
    wide = inner_ref.shape[2]

    @pl.when(lap == 0)
    def _():
        for n in range(group):
            inner_flat[:, pl.ds(n * wide, wide)] = inner_ref[n]
            gate_flat[:, pl.ds(n * wide, wide)] = gate_ref[n]

    @pl.when(lap < group)
    def _():
        total[...] = matmul_nt(inner_flat[...], inner_own[...]) + matmul_nt(
            gate_flat[...], gate_own[...]
        )

    @pl.when(lap >= group)
    def _():
        total[...] = matmul_nt(inner_flat[...], inner_got[...]) + matmul_nt(
            gate_flat[...], gate_got[...]
        )

    kept_ref[...] = total[pl.ds(pl.multiple_of(core_ref[0] * length, length), length), :]
    sent_ref[...] = total[pl.ds(pl.multiple_of((1 - core_ref[0]) * length, length), length), :]


def run_normed(core, inner_split, gate_split, in_weight, inner_got, gate_got, micros):
    _, rows, wide = inner_split.shape
    half_model, half = inner_got.shape
    high = half_model // group
    result = shape(rows // 2, 2 * half_model)
    whole = pl.BlockSpec((group, rows, wide), lambda n, core: (0, 0, 0))

    def own(offset):
        return pl.BlockSpec(
            (high, half), lambda n, core: (jnp.minimum(n, group - 1), offset + core[0])
        )

    got = pl.BlockSpec((high, half), lambda n, core: (jnp.maximum(n - group, 0), 0))
    out = pl.BlockSpec(
        (rows // 2, high),
        lambda n, core: (0, jnp.where(n < group, n + group * core[0], n - group * core[0])),
    )
    return pl.pallas_call(
        normed_kernel,
        grid_spec=pltpu.PrefetchScalarGridSpec(
            num_scalar_prefetch=1,
            grid=(2 * group,),
            in_specs=[whole, whole, own(0), own(2), got, got],
            out_specs=[out] * 2,
            scratch_shapes=[
                pltpu.VMEM((rows, half), bf16),
                pltpu.VMEM((rows, half), bf16),
                pltpu.VMEM((rows, high), f32),
            ],
        ),
        out_shape=[result] * 2,
        compiler_params=pltpu.CompilerParams(vmem_limit_bytes=50 * 2**20),
        cost_estimate=pl.CostEstimate(
            flops=int(micros * 1.15e9), bytes_accessed=1 << 20, transcendentals=0
        ),
        name="normed",
    )(core, inner_split, gate_split, in_weight, in_weight, inner_got, gate_got)


def pack_kernel(sel_ref, low_ref, act_ref, log_ref, vec_ref, out_ref):
    half = act_ref.shape[1]
    rows = out_ref.shape[3]
    first, second = sel_ref.shape[0], low_ref.shape[0]
    step = 2 * lanes
    tail = out_ref.shape[2] - first - second
    for start in range(0, half, step):
        cols = pl.ds(start, step)
        parts = (
            matmul(sel_ref[...], act_ref[:, cols]).astype(bf16),
            matmul(low_ref[...], log_ref[:, cols]).astype(bf16),
            vec_ref[:tail, cols].astype(bf16),
        )
        size = min(rows, step)
        for inside in range(0, step, size):
            outer, rest = divmod(start + inside, group * rows)
            member, offset = divmod(rest, rows)
            row = 0
            for part in parts:
                out_ref[member, outer, row : row + part.shape[0], offset : offset + size] = part[
                    :, inside : inside + size
                ]
                row += part.shape[0]


def run_pack(selected, low_rank, act, logits, vectors, outer_half, rows, micros):
    height = selected.shape[0] + low_rank.shape[0] + vectors.shape[0]
    operands = (selected, low_rank, act, logits, vectors)
    return pl.pallas_call(
        pack_kernel,
        out_shape=shape(group, outer_half, height, rows, dtype=bf16),
        in_specs=[pl.BlockSpec(memory_space=pltpu.VMEM)] * 5,
        out_specs=pl.BlockSpec(memory_space=pltpu.VMEM),
        compiler_params=pltpu.CompilerParams(vmem_limit_bytes=40 * 2**20),
        cost_estimate=pl.CostEstimate(
            flops=int(micros * 1.15e9), bytes_accessed=1 << 20, transcendentals=0
        ),
        name="pack",
    )(*operands)


def sequence_spec(array):
    rest = array.shape[1:]
    return pl.BlockSpec((1,) + rest, lambda n: (n,) + (0,) * len(rest))


def whole_spec(array):
    zeros = (0,) * array.ndim
    return pl.BlockSpec(array.shape, lambda n: zeros)


def per_sequence(
    kernel, name, operands, shared, results, scratch, micros, out_specs=None, in_specs=None
):
    sequences = operands[0].shape[0]
    moved = sum(a.size * a.dtype.itemsize for a in (*operands, *shared, *results))
    return pl.pallas_call(
        kernel,
        grid=(sequences,),
        in_specs=[(in_specs or {}).get(i, sequence_spec(a)) for i, a in enumerate(operands)]
        + [whole_spec(a) for a in shared],
        out_specs=out_specs or [sequence_spec(a) for a in results],
        out_shape=list(results),
        scratch_shapes=scratch,
        compiler_params=pltpu.CompilerParams(vmem_limit_bytes=58 * 2**20),
        cost_estimate=pl.CostEstimate(
            flops=int(micros * 1.15e9), bytes_accessed=moved, transcendentals=0
        ),
        name=name,
    )(*operands, *shared)


def shape(*dims, dtype=f32):
    return jax.ShapeDtypeStruct(dims, dtype)


def block_diagonal(array):
    length, states = array.shape[1], array.shape[2]
    wide = span * states
    own = jnp.arange(wide)[None, :] // states == jnp.arange(length)[:, None] % span
    return jnp.where(own, jnp.tile(array, (1, 1, span)), 0.0).astype(bf16)


def run_summary(selected, inner_act, gate, d_branch, beta_weight, beta_bias, states):
    count, length, half = inner_act.shape
    natural = shape(count, length, half)
    tiles = half // lanes
    results = [natural] * 3 + [shape(tiles, 3, count * states, lanes, dtype=bf16)]
    specs = [sequence_spec(a) for a in results]
    specs[3] = pl.BlockSpec((tiles, 3, states, lanes), lambda n: (0, 0, n, 0))
    kept = pltpu.VMEM((length, states, lanes), f32)
    return per_sequence(
        summary_kernel,
        "summary",
        (selected, inner_act, gate, d_branch),
        (beta_weight, beta_bias),
        results,
        [kept] * 3,
        25,
        specs,
    )


def run_forward(selected, rates, fed, chain, act, gate, d_branch, skip, outer_count):
    count, length, half = rates.shape
    states = chain.shape[2] // count
    queries = selected[:, :, selected.shape[2] - states :]
    kept = pltpu.VMEM((length, states, lanes), f32)
    results = [
        shape(group, count * length, half // group, dtype=bf16),
        shape(outer_count, count * length, half // outer_count, dtype=bf16),
        shape(count, length, half, dtype=bf16),
        shape(count, length // span, states, half),
        shape(count, 1, half),
    ]
    specs = [sequence_spec(a) for a in results]
    specs[0] = pl.BlockSpec((group, length, half // group), lambda n: (0, n, 0))
    specs[1] = pl.BlockSpec((outer_count, length, half // outer_count), lambda n: (0, n, 0))
    return per_sequence(
        forward_kernel,
        "forward",
        (selected, rates, fed, chain, act, gate, d_branch, block_diagonal(queries)),
        (skip,),
        results,
        [kept] * 2
        + [
            pltpu.VMEM((states, half), f32),
            pltpu.VMEM((span * states, half), bf16),
            pltpu.VMEM((length, half), f32),
        ],
        20,
        specs,
        {3: pl.BlockSpec((half // lanes, 1, states, lanes), lambda n: (0, 0, n, 0))},
    )


def run_backward(
    sequence, into, selected, rates, fed, grads, act, starts, chain, beta_weight, beta_bias, skip
):
    count, length, half = rates.shape
    states = chain.shape[2] // count
    rank = beta_weight.shape[1]
    keys = selected[:, :, rank : rank + states]
    kept = pltpu.VMEM((length, states, lanes), f32)
    natural = pltpu.VMEM((length, half), f32)
    hist = pltpu.VMEM((span * states, half), bf16)
    folded = pltpu.VMEM((length, span * states), f32)
    operands = (selected, rates, fed, grads, act, starts, chain, block_diagonal(keys))
    shared = (beta_weight, beta_bias, skip)
    results = [
        shape(count, length, half, dtype=bf16),
        shape(count, length, selected.shape[2]),
        shape(count, length, half),
        shape(count, 1, half),
    ]

    def spec(array):
        rest = array.shape[1:]
        return pl.BlockSpec((1,) + rest, lambda n: (sequence,) + (0,) * len(rest))

    def kernel(*refs):
        backward_kernel(*refs[len(into) :])

    moved = sum(a.size * a.dtype.itemsize for a in (*operands, *results)) // count
    return pl.pallas_call(
        kernel,
        grid=(1,),
        in_specs=[pl.BlockSpec(memory_space=pl.ANY) for _ in into]
        + [spec(a) for a in operands[:6]]
        + [pl.BlockSpec((half // lanes, 1, states, lanes), lambda n: (0, 1, sequence, 0))]
        + [spec(a) for a in operands[7:]]
        + [whole_spec(a) for a in shared],
        out_specs=[spec(a) for a in results],
        out_shape=results,
        scratch_shapes=[kept] * 3
        + [natural, pltpu.VMEM((span, states, half), f32)]
        + [hist] * 3
        + [pltpu.VMEM((states, half), f32), natural]
        + [folded] * 2,
        input_output_aliases={n: n for n in range(len(into))},
        compiler_params=pltpu.CompilerParams(vmem_limit_bytes=58 * 2**20),
        cost_estimate=pl.CostEstimate(
            flops=int(34 * 1.15e9), bytes_accessed=moved, transcendentals=0
        ),
        name="backward",
    )(*into, *operands, *shared)


def run_correlate(d_conv, later, weights, taps):
    count, length, half = d_conv.shape
    results = [shape(group, count * length, half // group, dtype=bf16)]
    specs = [pl.BlockSpec((group, length, half // group), lambda n: (0, n, 0))]
    later = jnp.pad(later, ((0, 0), (0, 8 - later.shape[1]), (0, 0)))
    return per_sequence(
        functools.partial(correlate_kernel, taps, group),
        "correlate",
        (d_conv, later),
        (weights,),
        results,
        [pltpu.VMEM((length + 8, lanes), f32)],
        4,
        specs,
    )[0]


def chain_kernel(pieces_ref, out_ref):
    count = pieces_ref.shape[0]
    state = jnp.zeros(pieces_ref.shape[2:], f32)
    grad = jnp.zeros(pieces_ref.shape[2:], f32)
    for piece in range(count):
        later = count - 1 - piece
        out_ref[piece, 0] = state.astype(bf16)
        out_ref[later, 1] = grad.astype(bf16)
        state = pieces_ref[piece, 0].astype(f32) * state + pieces_ref[piece, 1].astype(f32)
        grad = pieces_ref[later, 0].astype(f32) * grad + pieces_ref[later, 2].astype(f32)


def exchange_states(sums):
    count = lax.axis_size(seq)
    tiles, kinds, rows, _ = sums.shape
    share = tiles * rows // count
    if share < rows:
        sums = sums.reshape(tiles, kinds, rows // share, share, lanes).swapaxes(1, 2)
    pieces = lax.all_to_all(sums.reshape(count, kinds, share, lanes), seq, 0, 0)
    vmem = pl.BlockSpec(memory_space=pltpu.VMEM)
    sent = pl.pallas_call(
        chain_kernel,
        out_shape=shape(count, 2, share, lanes, dtype=bf16),
        in_specs=[vmem],
        out_specs=vmem,
        name="chain",
    )(pieces)
    got = lax.all_to_all(sent, seq, 0, 0)
    if share < rows:
        got = got.reshape(tiles, rows // share, 2, share, lanes).swapaxes(1, 2)
    return got.reshape(tiles, 2, rows, lanes)


def shifted(value, steps):
    count = lax.axis_size(seq)
    pairs = [(s, s + steps) for s in range(count) if 0 <= s + steps < count]
    return lax.ppermute(value, seq, pairs)


def plane_trade(chunks):
    mine = lax.axis_index("member")
    got = [at(chunks, mine)]
    for d in range(1, group):
        pairs = [(m, m ^ d) for m in range(group)]
        got.append(lax.ppermute(at(chunks, jnp.bitwise_xor(mine, d)), "member", pairs))
    return got


def line_step(partial, bit, axis="outer"):
    count = lax.axis_size(axis)
    mine = (lax.axis_index(axis) // bit) % 2
    split = partial.reshape((-1, 2) + partial.shape[1:])
    sent = lax.dynamic_index_in_dim(split, 1 - mine, 1, keepdims=False).astype(bf16)
    kept = lax.dynamic_index_in_dim(split, mine, 1, keepdims=False)
    got = lax.ppermute(sent, axis, [(o, o ^ bit) for o in range(count)])
    return kept + got.astype(f32)


def line_reduce(partial, bit, axis="outer"):
    while partial.shape[0] > 1:
        partial = line_step(partial, bit, axis)
        bit *= 2
    return partial[0]


def to_owner(rows):
    half = lax.axis_size("outer") // 2
    core = lax.axis_index("fsdp")
    pairs = []
    for o in range(2 * half):
        c = 1 - o // half
        pairs.append((o * 2 + c, (o ^ half) * 2 + 1 - c))
    got = lax.ppermute(rows.astype(bf16), ("outer", "fsdp"), pairs).astype(f32)
    return jnp.where(lax.axis_index("outer") // half == core, rows, got)


def owner_sum(partial):
    partial = line_reduce(partial, 1)
    half = lax.axis_size("outer") // 2
    pairs = []
    for o in range(2 * half):
        c = 1 - o // half
        pairs.append((o * 2 + c, (o ^ half) * 2 + c))
    return partial + lax.ppermute(partial.astype(bf16), ("outer", "fsdp"), pairs).astype(f32)


def owner_part(total, axis):
    core = lax.axis_index("fsdp")
    outer = lax.axis_index("outer")
    half = lax.axis_size("outer") // 2
    size = total.shape[axis] // 2
    mine = lax.dynamic_slice_in_dim(total, core * size, size, axis)
    other = swap(lax.dynamic_slice_in_dim(total, (1 - core) * size, size, axis))
    return jnp.where(outer // half == core, mine, other)


def local(
    tokens,
    cotangent,
    norm_gain,
    in_weight,
    conv_weight,
    conv_bias,
    select_weight,
    beta_weight,
    beta_bias,
    skip_gain,
    out_weight,
):
    core = lax.axis_index("fsdp")
    count = lax.axis_size(seq)
    outer_count = lax.axis_size("outer")
    member = lax.axis_index("member")
    length, model = tokens.shape[1], tokens.shape[2]
    half_model = in_weight.shape[0]
    half, taps = conv_weight.shape
    inner = 2 * half
    rank = beta_weight.shape[1]
    states = (select_weight.shape[1] - rank) // 2
    rows = 2 * length
    reach = taps - 1

    def ordered(mine, other):
        return jnp.where(core == 0, mine, other), jnp.where(core == 0, other, mine)

    own_tokens = tokens[0]
    own_cot = cotangent[0]
    x = jnp.concatenate(ordered(own_tokens, swap(own_tokens)))
    cot = jnp.concatenate(ordered(own_cot, swap(own_cot)))
    gain_full = jnp.concatenate(ordered(norm_gain, swap(norm_gain))).astype(f32)

    core_index = core.astype(jnp.int32).reshape(1)
    inner_got = swap(other_columns(core_index, in_weight, False))
    gate_got = swap(other_columns(core_index, in_weight, True))

    def normalise(values):
        wide = values.astype(f32)
        inverse = lax.rsqrt(jnp.mean(wide * wide, axis=1, keepdims=True) + epsilon)
        normal = wide * inverse
        return normal, inverse, (normal * gain_full).astype(bf16)

    normal, inverse, own_normed = normalise(own_tokens)
    normed = normalise(x)[2]
    normed_all = lax.all_gather(own_normed, ("member", "fsdp"), tiled=True)
    cot_all = lax.all_gather(own_cot, ("outer", "fsdp"), tiled=True)
    d_branch = run_product(cot, out_weight, True, 5)
    inner_pre = run_project(core_index, normed, in_weight, inner_got, False, 5)
    inner_pre = inner_pre.reshape(2, length, half)
    edges = shifted(inner_pre[:, length - reach :], 1)
    gate = run_project(core_index, normed, in_weight, gate_got, True, 5).reshape(2, length, half)
    extended = jnp.concatenate([edges, inner_pre], axis=1)
    conv_wide = conv_weight.astype(f32)
    conv_sum = conv_bias.astype(f32)
    for tap in range(taps):
        conv_sum = conv_sum + conv_wide[:, tap] * extended[:, tap : tap + length].astype(f32)
    conv_sum = conv_sum.reshape(rows, half)
    inner_act = jax.nn.silu(conv_sum).astype(bf16)
    selected = matmul(inner_act, select_weight)
    selected = selected + swap(selected)
    low_rank = selected[:, :rank].astype(bf16)
    beta_shift = beta_bias.astype(f32)[None]
    skip_wide = skip_gain.astype(f32)[None]
    width = half // group
    owner_rows = 2 * half // count
    selected = selected.reshape(2, length, -1)
    act_rows = inner_act.reshape(2, length, half)
    d_branch = d_branch.reshape(2, length, half)
    rates, fed, d_recurrent, sums = run_summary(
        selected, act_rows, gate, d_branch, beta_weight, beta_shift, states
    )
    chain = exchange_states(sums)
    early, branch_split, branch, starts, skip_term = run_forward(
        selected, rates, fed, chain, act_rows, gate, d_branch, skip_wide, outer_count
    )
    early, branch_split, normed_all, cot_all = together(
        early, branch_split, normed_all, cot_all
    )
    branch = branch.reshape(rows, half)

    traded = plane_trade(early)
    branch_all = lax.all_to_all(branch_split, "outer", 0, 0).reshape(outer_count * rows, -1)
    def ordered_members(pieces):
        stacked = jnp.stack(pieces)
        return jnp.concatenate([at(stacked, jnp.bitwise_xor(member, m)) for m in range(group)])

    def in_weight_partial(grad_all):
        return matmul_tn(normed_all, grad_all).reshape(outer_count, -1, width)

    def in_weight_rows(inner_part, gate_part):
        pieces = jnp.concatenate([inner_part, gate_part], axis=1).reshape(group, -1, 2 * width)
        got = lax.all_to_all(pieces, "member", 0, 0).reshape(group, 2, -1, 2 * width)
        mine = lax.dynamic_index_in_dim(got, core, 1, keepdims=False)
        other = swap(lax.dynamic_index_in_dim(got, 1 - core, 1, keepdims=False))
        low, high = ordered(mine, other)
        found = [source[q, :, :width] for source in (low, high) for q in range(group)]
        found += [source[q, :, width:] for source in (low, high) for q in range(group)]
        return jnp.concatenate(found, axis=1).astype(f32)

    operands = (
        selected,
        rates,
        fed,
        d_recurrent,
        act_rows,
        starts,
        chain,
        beta_weight,
        beta_shift,
        skip_wide,
    )
    first_part = list(run_backward(0, (), *operands))
    *traded, first_part[1] = together(*traded, first_part[1])
    early_all = ordered_members(traded)
    gate_partial, *first_part = together(in_weight_partial(early_all), *first_part)
    gate_mid = line_step(gate_partial, 1)
    d_logits, d_selected, d_base, bias_term = run_backward(1, tuple(first_part), *operands)
    d_selected, branch_all, gate_mid = together(d_selected, branch_all, gate_mid)
    d_logits = d_logits.reshape(rows, half)
    d_selected = d_selected.reshape(rows, -1)
    d_selected = d_selected + swap(d_selected)
    d_selected = d_selected.astype(bf16)
    d_inner = d_base.reshape(rows, half) + matmul_nt(d_selected, select_weight)
    d_conv = (d_inner * swish_slope(conv_sum)).reshape(2, length, half)
    later = shifted(d_conv[:, :reach], -1)
    split = run_correlate(d_conv, later, conv_wide.T, taps)
    split, early, branch = together(split, early, branch)
    inner_all = lax.all_to_all(split, "member", 0, 0).reshape(group * rows, width)
    kept, sent = run_normed(core_index, split, early, in_weight, inner_got, gate_got, 10)
    gate_part = line_reduce(gate_mid, 2)
    inner_all, gate_part, kept, sent, branch_all = together(
        inner_all, gate_part, kept, sent, branch_all
    )
    inner_partial = in_weight_partial(inner_all)
    out_partial = matmul_tn(branch_all, cot_all).reshape(group, -1, model)

    out_sum = run_product(branch, out_weight, False, 5)
    out_sum = out_sum.reshape(2, length, model)
    layer_out = own_tokens.astype(f32) + (at(out_sum, core) + swap(at(out_sum, 1 - core)))
    layer_out = layer_out.astype(bf16)[None]

    d_normed = kept + swap(sent)
    gain_term = jnp.sum(d_normed * normal, axis=0)
    gain_term = gain_term.reshape(2, -1)
    gain_term = at(gain_term, core) + swap(at(gain_term, 1 - core))
    d_normal = d_normed * gain_full
    token_grad = inverse * (
        d_normal - normal * jnp.mean(normal * d_normal, axis=1, keepdims=True)
    ) + own_cot.astype(f32)

    vectors = [
        jnp.sum(d_conv * extended[:, tap : tap + length].astype(f32), axis=(0, 1))
        for tap in range(taps)
    ]
    owned = half // count
    vectors += [
        jnp.sum(d_conv, axis=(0, 1)),
        jnp.sum(bias_term, axis=(0, 1)),
        jnp.sum(skip_term, axis=(0, 1)),
        jnp.pad(gain_term.reshape(count, -1), ((0, 0), (0, owned - model // 2 // count))).reshape(-1),
    ]
    vectors = jnp.stack(vectors)
    vectors = jnp.pad(vectors, ((0, -vectors.shape[0] % 16), (0, 0)))
    pack = run_pack(
        d_selected.T, low_rank.T, inner_act, d_logits, vectors, outer_count // 2, owner_rows, 1
    )

    inner_mid = line_step(inner_partial, 1)
    pack_all = lax.all_to_all(pack, "member", 0, 0)
    out_total = line_reduce(out_partial, 1, "member")
    inner_mid, pack_all, out_total = together(inner_mid, pack_all, out_total)
    inner_part = line_reduce(inner_mid, 2)
    pack_own = owner_part(owner_sum(jnp.sum(pack_all.astype(f32), axis=0)), 1).T
    out_grad = to_owner(out_total)
    in_grad = in_weight_rows(inner_part.astype(bf16), gate_part.astype(bf16))
    edge = select_weight.shape[1]
    select_grad = pack_own[:, :edge]
    beta_weight_grad = pack_own[:, edge : edge + rank]
    edge += rank
    conv_weight_grad = pack_own[:, edge : edge + taps]
    conv_bias_grad = pack_own[:, edge + taps]
    beta_bias_grad = pack_own[:, edge + taps + 1]
    skip_grad = pack_own[:, edge + taps + 2]
    gain_grad = pack_own[: model // 2 // count, edge + taps + 3]

    return (
        layer_out,
        token_grad[None],
        gain_grad,
        in_grad,
        conv_weight_grad,
        conv_bias_grad,
        select_grad,
        beta_weight_grad,
        beta_bias_grad,
        skip_grad,
        out_grad,
    )


def solution(mesh):
    devices = mesh.devices
    parts = jax.sharding.Mesh(
        devices.reshape(devices.shape[0] // group, group, devices.shape[1]),
        ("outer", "member", "fsdp"),
    )
    everything = ("outer", "member", "fsdp")
    tokens = P("fsdp", seq, None)
    vector, matrix = P("fsdp"), P("fsdp", None)
    owned, owned_rows = P(everything), P(everything, None)
    in_specs = (
        tokens,
        tokens,
        vector,
        matrix,
        matrix,
        vector,
        matrix,
        matrix,
        vector,
        vector,
        matrix,
    )
    out_specs = (
        tokens,
        tokens,
        owned,
        owned_rows,
        owned_rows,
        owned,
        owned_rows,
        owned_rows,
        owned,
        owned,
        owned_rows,
    )
    return jax.shard_map(
        local, mesh=parts, in_specs=in_specs, out_specs=out_specs, check_vma=False
    )
```

time: 724 us -> 491 us (0.68)
  local copies, waits for them, and re-layouts: 118 us -> 34.5 us
  Pallas kernels: 127 us -> 200 us
  matrix products: 99.1 us -> 26.5 us
  starting transfers between devices: 140 us -> 82.8 us
  other arithmetic: 93.3 us -> 43.8 us
  waiting for transfers between devices: 131 us -> 82.5 us
  between operations: 2.62 us -> 15.4 us
    pallas_call x3 -> x14, Pallas kernels: 127 us -> 200 us  [the longest x3 70.7 us: per_sequence(): pl.pallas_call(kernel, grid=(sequences,), in_specs=[(in_specs or {}).get(...]
    ppermute x50 -> x14, waiting for transfers between devices: 119 us -> 51.6 us  [the longest x7 34.4 us: line_step(): got = lax.ppermute(sent, axis, [(o, o ^ bit) for o in range(count)])]
    ppermute x50 -> x14, starting transfers between devices: 82.9 us -> 20.6 us  [the longest x7 8.07 us: line_step(): got = lax.ppermute(sent, axis, [(o, o ^ bit) for o in range(count)])]
    unnamed x162 -> x110, local copies, waits for them, and re-layouts: 59.2 us -> 13.1 us
    dot_general x7 -> x1, matrix products: 37.1 us -> 0.84 us  [matmul(): return jnp.dot(left, right, preferred_element_type=f32)]
    dot_general x7 -> x1, matrix products: 40.5 us -> 6.24 us  [matmul_nt(): lax.dot_general(left, right, (((1,), (1,)), ((), ())), preferred_element_...]
    all_to_all x3 -> x6, starting transfers between devices: 14.6 us -> 40.3 us  [the longest x1 15.6 us: local(): lax.all_to_all(split, 'member', 0, 0).reshape(group * rows, width)]
    convert_element_type x19 -> x10, other arithmetic: 32.2 us -> 9.89 us  [the longest x2 5.42 us: local(): inner_act = jax.nn.silu(conv_sum).astype(bf16)]
  transfers between devices with their start and end apart: 69 -> 34, of which waited for: 19 -> 13; matrix products, arithmetic and copies ran while one was open for 32% -> 16% of each run, Pallas kernels for 0% -> 41%
where the time goes in v2:
time: 491 us; the launch traced here: 485 us
  Pallas kernels  200 us (41%)
  starting transfers between devices  82.8 us (17%)
  waiting for transfers between devices  82.5 us (17%)
  other arithmetic  43.8 us (9%)
  local copies, waits for them, and re-layouts  34.5 us (7%)
  matrix products  26.5 us (5%)
  between operations  15.4 us (3%)
    pallas_call x3, Pallas kernels, per_sequence(): pl.pallas_call(kernel, grid=(sequences,), in_specs=[(in_specs or {}).get(...  70.7 us
    pallas_call x2, Pallas kernels, run_backward(): pl.pallas_call(kernel, grid=(1,), in_specs=[pl.BlockSpec(memory_space=pl....  70.2 us
    ppermute x7, waiting for transfers between devices, line_step(): got = lax.ppermute(sent, axis, [(o, o ^ bit) for o in range(count)])  34.4 us
    ppermute x12, starting transfers between devices, swap(): return lax.ppermute(value, 'fsdp', [(0, 1), (1, 0)])  21.8 us
    dot_general x3, matrix products, matmul_tn(): lax.dot_general(left, right, (((0,), (0,)), ((), ())), preferred_element_...  19.5 us
    pallas_call x1, Pallas kernels, run_normed(): pl.pallas_call(normed_kernel, grid_spec=pltpu.PrefetchScalarGridSpec(num_...  16.8 us
    all_to_all x1, starting transfers between devices, local(): lax.all_to_all(split, 'member', 0, 0).reshape(group * rows, width)  15.6 us
    pallas_call x2, Pallas kernels, run_product(): pl.pallas_call(functools.partial(whole_kernel, transposed), grid=(columns...  15.3 us
  transfers between devices with their start and end apart: 34, of which 13 were waited for; matrix products, arithmetic and copies ran while one was open for 16% of the time, Pallas kernels for 41%

profile of v2, /device:TPU:1, one launch (start us, length us, event | category | flops | bytes accessed | tf_op | source)
XLA Modules:
  0.0 485.4 jit_solution(18058151636725919400)
XLA Ops:
  11.7 4.9 %columns.2 = bf16[1024,2048]{1,0:T(8,128)(2,1)} custom-call(s32[1]{0:T(128)} %bitcast.2.core_ref, bf16[1024,8192]{1,0:T(8,128)(2,1)} %gate_own.1), custom_call_target="tpu_custom_call" | custom-call | tf_op jit(solution)/shard_map/columns/pallas_call | solution.py:365
  17.7 5.0 %columns.3 = bf16[1024,2048]{1,0:T(8,128)(2,1)} custom-call(s32[1]{0:T(128)} %bitcast.2.core_ref, bf16[1024,8192]{1,0:T(8,128)(2,1)} %gate_own.1), custom_call_target="tpu_custom_call" | custom-call | tf_op jit(solution)/shard_map/columns/pallas_call | solution.py:365
  32.7 7.1 %project.2 = bf16[512,2048]{1,0:T(8,128)(2,1)S(1)} custom-call(s32[1]{0:T(128)} %bitcast.2.core_ref, bf16[512,2048]{1,0:T(8,128)(2,1)S(1)} %fusion.2.x_ref, bf16[1024,8192]{1,0:T(8,128)(2,1)} %gate_own.1, bf16[1024,2048]{1,0:T(8,128)(2,1)} %collective-permute-done.2.got_ref.inner_got), custom_call_target="tpu_custom_call" | custom-call | flops 5750000128 | bytes 8388608 | tf_op jit(solution)/shard_map/project/pallas_call | solution.py:425
  39.8 5.3 %collective-permute-start.3 = (bf16[2,3,2048]{2,1,0:T(4,128)(2,1)S(1)}, bf16[2,3,2048]{2,1,0:T(4,128)(2,1)S(1)}, u32[]{:S(2)}, u32[]{:S(2)}) collective-permute-start(bf16[2,3,2048]{2,1,0:T(4,128)(2,1)S(1)} %slice.146), channel_id=1, source_target_pairs={{0,2},{2,4},{4,6},{6,8},{8,10},{10,12},{12,14},{14,16},{16,18},{18... | collective-permute-start | bytes 73736 | tf_op jit(solution)/shard_map/ppermute | solution.py:766
  45.1 7.3 %product.2 = f32[512,2048]{1,0:T(8,128)S(1)} custom-call(bf16[512,2048]{1,0:T(8,128)(2,1)S(1)} %pad_maximum_fusion.2.left_ref, bf16[2048,2048]{1,0:T(8,128)(2,1)} %right_ref.3), custom_call_target="tpu_custom_call" | custom-call | flops 5750000128 | bytes 1048576 | tf_op jit(solution)/shard_map/product/pallas_call | solution.py:396
  61.7 7.3 %project.3 = bf16[512,2048]{1,0:T(8,128)(2,1)S(1)} custom-call(s32[1]{0:T(128)} %bitcast.2.core_ref, bf16[512,2048]{1,0:T(8,128)(2,1)S(1)} %fusion.2.x_ref, bf16[1024,8192]{1,0:T(8,128)(2,1)} %gate_own.1, bf16[1024,2048]{1,0:T(8,128)(2,1)S(1)} %collective-permute-done.5.got_ref.gate_got), custom_call_target="tpu_custom_call" | custom-call | flops 5750000128 | bytes 8388608 | tf_op jit(solution)/shard_map/project/pallas_call | solution.py:425
  71.6 35.8 %summary.1 = (f32[2,256,2048]{2,1,0:T(8,128)}, f32[2,256,2048]{2,1,0:T(8,128)}, f32[2,256,2048]{2,1,0:T(8,128)}, bf16[16,3,32,128]{3,2,1,0:T(8,128)(2,1)}) custom-call(f32[2,256,160]{2,1,0:T(8,128)} %copy.53.sel_ref.refs_0_.refs_4_, bf16[2,256,2048]{2,1,0:T(8,128)(2,1)} %get-tuple-element.145.act_ref.refs_4_.refs_8_, bf16[2,256,2048]{2,1,0:T(8,128)(2,1)} %bitcast.240, ...), custom_call_target="tpu_custom_call" | custom-call | flops 28750000128 | bytes 22224896 | tf_op jit(solution)/shard_map/summary/pallas_call | solution.py:581
  107.5 6.1 %all-to-all-start = ((bf16[16,3,32,128]{3,2,1,0:T(8,128)(2,1)}), bf16[16,3,32,128]{3,2,1,0:T(8,128)(2,1)S(1)}, u32[]{:S(2)}, u32[]{:S(2)}) async-start(bf16[16,3,32,128]{3,2,1,0:T(8,128)(2,1)} %get-tuple-element.60), calls=%async_computation | async-start | bytes 786432 | tf_op jit(solution)/shard_map/all_to_all | solution.py:748
  114.2 10.1 %all-to-all-done.pieces_ref = bf16[16,3,32,128]{3,2,1,0:T(8,128)(2,1)S(1)} async-done(((bf16[16,3,32,128]{3,2,1,0:T(8,128)(2,1)}), bf16[16,3,32,128]{3,2,1,0:T(8,128)(2,1)S(1)}, u32[]{:S(2)}, u32[]{:S(2)}) %all-to-all-start) | async-done | bytes 393248 | tf_op jit(solution)/shard_map/all_to_all | solution.py:748
  126.9 5.1 %all-to-all-start.1 = ((bf16[16,2,32,128]{3,2,1,0:T(8,128)(2,1)}), bf16[16,2,32,128]{3,2,1,0:T(8,128)(2,1)S(1)}, u32[]{:S(2)}, u32[]{:S(2)}) async-start(bf16[16,2,32,128]{3,2,1,0:T(8,128)(2,1)} %chain.1), calls=%async_computation.1 | async-start | bytes 524288 | tf_op jit(solution)/shard_map/all_to_all | solution.py:757
  134.1 5.5 %all-to-all-done.1.init_ref.refs_6_.refs_10_ = bf16[16,2,32,128]{3,2,1,0:T(8,128)(2,1)S(1)} async-done(((bf16[16,2,32,128]{3,2,1,0:T(8,128)(2,1)}), bf16[16,2,32,128]{3,2,1,0:T(8,128)(2,1)S(1)}, u32[]{:S(2)}, u32[]{:S(2)}) %all-to-all-start.1) | async-done | bytes 262176 | tf_op jit(solution)/shard_map/all_to_all | solution.py:757
  140.3 29.8 %forward.1 = (bf16[4,512,512]{2,1,0:T(8,128)(2,1)}, bf16[4,512,512]{2,1,0:T(8,128)(2,1)}, bf16[2,256,2048]{2,1,0:T(8,128)(2,1)}, f32[2,16,16,2048]{3,2,1,0:T(8,128)}, f32[2,1,2048]{2,1,0:T(1,128)}) custom-call(f32[2,256,160]{2,1,0:T(8,128)} %copy.53.sel_ref.refs_0_.refs_4_, f32[2,256,2048]{2,1,0:T(8,128)} %get-tuple-element.58.r_ref.refs_1_.refs_5_, ...), custom_call_target="tpu_custom_call" | custom-call | flops 23000000512 | bytes 28139520 | tf_op jit(solution)/shard_map/forward/pallas_call | solution.py:581
  175.3 35.1 %backward.2 = (bf16[2,256,2048]{2,1,0:T(8,128)(2,1)}, f32[2,256,160]{2,1,0:T(8,128)}, f32[2,256,2048]{2,1,0:T(8,128)}, f32[2,1,2048]{2,1,0:T(1,128)}) custom-call(f32[2,256,160]{2,1,0:T(8,128)} %copy.53.sel_ref.refs_0_.refs_4_, f32[2,256,2048]{2,1,0:T(8,128)} %get-tuple-element.58.r_ref.refs_1_.refs_5_, ...), custom_call_target="tpu_custom_call" | custom-call | flops 39099998208 | bytes 13180928 | tf_op jit(solution)/shard_map/backward/pallas_call | solution.py:689
  210.4 4.9 %all-to-all-start.2 = ((bf16[4,512,512]{2,1,0:T(8,128)(2,1)}), bf16[4,512,512]{2,1,0:T(8,128)(2,1)}, u32[]{:S(2)}, u32[]{:S(2)}) async-start(bf16[4,512,512]{2,1,0:T(8,128)(2,1)} %get-tuple-element.82), calls=%async_computation.2 | async-start | bytes 4194304 | tf_op jit(solution)/shard_map/all_to_all | solution.py:910
  218.8 4.8 fusion.32
  225.3 35.1 %backward.3 = (bf16[2,256,2048]{2,1,0:T(8,128)(2,1)}, f32[2,256,160]{2,1,0:T(8,128)}, f32[2,256,2048]{2,1,0:T(8,128)}, f32[2,1,2048]{2,1,0:T(1,128)}) custom-call(bf16[2,256,2048]{2,1,0:T(8,128)(2,1)} %get-tuple-element.76.refs_0_, ...), custom_call_target="tpu_custom_call", output_to_operand_aliasing={{0}: (0, {}), {1}: (1, {}), {2}: (2, {}), {3}: (3, {})} | custom-call | flops 39099998208 | bytes 13180928 | tf_op jit(solution)/shard_map/backward/pallas_call | solution.py:689
  260.4 12.0 %collective-permute-done.10 = bf16[2,512,512]{2,1,0:T(8,128)(2,1)} collective-permute-done((bf16[2,512,512]{2,1,0:T(8,128)(2,1)S(1)}, bf16[2,512,512]{2,1,0:T(8,128)(2,1)}, u32[]{:S(2)}, u32[]{:S(2)}) %collective-permute-start.10) | collective-permute-done | bytes 1048608 | tf_op jit(solution)/shard_map/ppermute | solution.py:784
  285.5 6.2 %fusion.9 = (f32[2048]{0:T(1024)S(1)}, f32[2048]{0:T(1024)S(1)}, f32[2048]{0:T(1024)S(1)}, f32[512,2048]{1,0:T(8,128)S(1)}) fusion(bf16[2,256,2048]{2,1,0:T(8,128)(2,1)S(1)} %bitcast.236, bf16[2,3,2048]{2,1,0:T(4,128)(2,1)S(1)} %copy-done.37, f32[2,256,2048]{2,1,0:T(8,128)} %copy-done.17, bf16[512,160]{0,1:T(8,128)(2,1)S(1)} %add_convert_fusion.1, ...), kind=kOutput, calls=%fused_computation.17 | convolution fusion | flops 363849728 | bytes 15548416 | tf_op jit(solution)/shard_map/dot_general | solution.py:26
  297.8 5.1 %correlate.1.inner_ref = bf16[4,512,512]{2,1,0:T(8,128)(2,1)} custom-call(f32[2,256,2048]{2,1,0:T(8,128)} %bitcast.249, f32[2,8,2048]{2,1,0:T(8,128)} %pad.12.later_ref, f32[4,2048]{1,0:T(4,128)} %convert_bitcast_fusion.w_ref), custom_call_target="tpu_custom_call" | custom-call | flops 4600000000 | bytes 6455296 | tf_op jit(solution)/shard_map/correlate/pallas_call | solution.py:581
  302.9 15.6 %all-to-all-start.3 = ((bf16[4,512,512]{2,1,0:T(8,128)(2,1)}), bf16[4,512,512]{2,1,0:T(8,128)(2,1)S(1)}, u32[]{:S(2)}, u32[]{:S(2)}) async-start(bf16[4,512,512]{2,1,0:T(8,128)(2,1)} %correlate.1.inner_ref), calls=%async_computation.3 | async-start | bytes 4194304 | tf_op jit(solution)/shard_map/all_to_all | solution.py:956
  318.5 16.8 %normed.1 = (f32[256,2048]{1,0:T(8,128)S(1)}, f32[256,2048]{1,0:T(8,128)}) custom-call(s32[1]{0:T(128)} %bitcast.2.core_ref, bf16[4,512,512]{2,1,0:T(8,128)(2,1)} %correlate.1.inner_ref, bf16[4,512,512]{2,1,0:T(8,128)(2,1)} %get-tuple-element.89.gate_ref, bf16[1024,8192]{1,0:T(8,128)(2,1)} %gate_own.1, bf16[1024,8192]{1,0:T(8,128)(2,1)} %gate_own.1, ...), custom_call_target="tpu_custom_call" | custom-call | flops 11500000256 | bytes 1048576 | tf_op jit(solution)/shard_map/normed/pallas_call | solution.py:503
  335.3 8.0 %product.3 = f32[512,2048]{1,0:T(8,128)S(1)} custom-call(bf16[512,2048]{1,0:T(8,128)(2,1)S(1)} %bitcast.245, bf16[2048,2048]{1,0:T(8,128)(2,1)} %right_ref.3), custom_call_target="tpu_custom_call" | custom-call | flops 5750000128 | bytes 1048576 | tf_op jit(solution)/shard_map/product/pallas_call | solution.py:396
  347.3 7.7 %fusion.71 = f32[512,2048]{1,0:T(8,128)S(1)} fusion(bf16[2048,512]{1,0:T(8,128)(2,1)} %bitcast.30, bf16[2048,2048]{1,0:T(8,128)(2,1)} %bitcast.284), kind=kOutput, calls=%fused_computation.170 | convolution fusion | flops 4294967296 | bytes 14680064 | tf_op jit(solution)/shard_map/dot_general | solution.py:30
  358.3 6.9 %fusion.70 = f32[2048,512]{1,0:T(8,128)S(1)} fusion(bf16[2048,2048]{1,0:T(8,128)(2,1)} %all-gather.4.cloned.1.call-done, bf16[2048,512]{1,0:T(8,128)(2,1)S(1)} %bitcast.257), kind=kOutput, calls=%fused_computation.169 | convolution fusion | flops 4294967296 | bytes 14680064 | tf_op jit(solution)/shard_map/dot_general | solution.py:30
  367.1 12.0 %collective-permute-done.18 = bf16[2,128,2048]{2,1,0:T(8,128)(2,1)S(1)} collective-permute-done((bf16[2,128,2048]{2,1,0:T(8,128)(2,1)S(1)}, bf16[2,128,2048]{2,1,0:T(8,128)(2,1)S(1)}, u32[]{:S(2)}, u32[]{:S(2)}) %collective-permute-start.18) | collective-permute-done | bytes 1048608 | tf_op jit(solution)/shard_map/ppermute | solution.py:784
  400.8 5.5 %collective-permute-done.19 = bf16[1,128,2048]{2,1,0:T(8,128)(2,1)} collective-permute-done((bf16[1,128,2048]{2,1,0:T(8,128)(2,1)}, bf16[1,128,2048]{2,1,0:T(8,128)(2,1)}, u32[]{:S(2)}, u32[]{:S(2)}) %collective-permute-start.19) | collective-permute-done | bytes 524320 | tf_op jit(solution)/shard_map/ppermute | solution.py:784
  408.5 4.7 all-to-all-done.4
  416.4 4.9 %collective-permute-done.20 = bf16[1,304,256]{2,1,0:T(8,128)(2,1)S(1)} collective-permute-done((bf16[1,304,256]{2,1,0:T(8,128)(2,1)}, bf16[1,304,256]{2,1,0:T(8,128)(2,1)S(1)}, u32[]{:S(2)}, u32[]{:S(2)}) %collective-permute-start.20) | collective-permute-done | bytes 155680 | tf_op jit(solution)/shard_map/ppermute | solution.py:784
  422.6 10.6 %collective-permute-done.21 = bf16[304,256]{1,0:T(8,128)(2,1)S(1)} collective-permute-done((bf16[304,256]{1,0:T(8,128)(2,1)S(1)}, bf16[304,256]{1,0:T(8,128)(2,1)S(1)}, u32[]{:S(2)}, u32[]{:S(2)}) %collective-permute-start.21) | collective-permute-done | bytes 155680 | tf_op jit(solution)/shard_map/ppermute | solution.py:813
  434.0 12.9 %collective-permute-start.22 = (f32[304,128]{1,0:T(8,128)}, f32[304,128]{1,0:T(8,128)S(1)}, u32[]{:S(2)}, u32[]{:S(2)}) collective-permute-start(f32[304,128]{1,0:T(8,128)} %constant_dynamic-slice_fusion), channel_id=1, source_target_pairs={{0,1},{1,0},{2,3},{3,2},{4,5},{5,4},{6,7},{7,6},{8,9},{9,8},{10,11... | collective-permute-start | bytes 466952 | tf_op jit(solution)/shard_map/ppermute | solution.py:43
  452.8 6.6 %fusion.28 = (f32[1,256,2048]{2,1,0:T(8,128)}, bf16[1,256,2048]{2,1,0:T(8,128)(2,1)}) fusion(f32[256]{0:T(256)S(1)} %broadcast_multiply_fusion, f32[2048]{0:T(1024)S(1)} %copy-done.34, f32[256]{0:T(256)S(1)} %copy-done.39, bf16[1,256,2048]{2,1,0:T(8,128)(2,1)} %param.12, bf16[1,256,2048]{2,1,0:T(8,128)(2,1)} %param.11, f32[256,2048]{1,0:T(8,128)S(1)} %copy-done.8, ...), kind=kLoop, calls=%fused_computation.48 | loop fusion | flops 6291456 | bytes 13641732 | tf_op jit(solution)/shard_map/broadcast_in_dim | solution.py:1016
  462.0 4.6 all-to-all-done.5
  (251 shorter events, 120.6 us)
Async XLA Ops:
  7.2 162.9 %all-gather.6.cloned.1.call-start = ((), (), s32[]{:S(2)}) async-start(), calls=%async_computation.7 | async-start | bytes 9437184 | tf_op jit(solution)/shard_map/all_gather | solution.py:874
  7.9 162.2 %all-gather.4.cloned.1.call-start = ((), (), s32[]{:S(2)}) async-start(), calls=%async_computation.6 | async-start | bytes 9437184 | tf_op jit(solution)/shard_map/all_gather | solution.py:873
  16.6 16.0 %collective-permute-start.2 = (bf16[1024,2048]{1,0:T(8,128)(2,1)}, bf16[1024,2048]{1,0:T(8,128)(2,1)}, u32[]{:S(2)}, u32[]{:S(2)}) collective-permute-start(bf16[1024,2048]{1,0:T(8,128)(2,1)} %columns.2), channel_id=1, source_target_pairs={{0,1},{1,0},{2,3},{3,2},{4,5},{5,4},{6,7},{7,6},{8,9},{9,8},{10,11... | collective-permute-start | bytes 12582920 | tf_op jit(solution)/shard_map/ppermute | solution.py:43
  17.1 8.4 %collective-permute-start = (bf16[256,2048]{1,0:T(8,128)(2,1)S(1)}, bf16[256,2048]{1,0:T(8,128)(2,1)}, u32[]{:S(2)}, u32[]{:S(2)}) collective-permute-start(bf16[256,2048]{1,0:T(8,128)(2,1)S(1)} %bitcast.246), channel_id=1, source_target_pairs={{0,1},{1,0},{2,3},{3,2},{4,5},{5,4},{6,7},{7,6},{8,9},{9,8},{10,11... | collective-permute-start | bytes 3145736 | tf_op jit(solution)/shard_map/ppermute | solution.py:43
  17.1 12.8 %collective-permute-start.6 = (bf16[256,2048]{1,0:T(8,128)(2,1)S(1)}, bf16[256,2048]{1,0:T(8,128)(2,1)}, u32[]{:S(2)}, u32[]{:S(2)}) collective-permute-start(bf16[256,2048]{1,0:T(8,128)(2,1)S(1)} %bitcast.247), channel_id=1, source_target_pairs={{0,1},{1,0},{2,3},{3,2},{4,5},{5,4},{6,7},{7,6},{8,9},{9,8},{10,11... | collective-permute-start | bytes 3145736 | tf_op jit(solution)/shard_map/ppermute | solution.py:43
  22.7 39.0 %collective-permute-start.5 = (bf16[1024,2048]{1,0:T(8,128)(2,1)}, bf16[1024,2048]{1,0:T(8,128)(2,1)S(1)}, u32[]{:S(2)}, u32[]{:S(2)}) collective-permute-start(bf16[1024,2048]{1,0:T(8,128)(2,1)} %columns.3), channel_id=1, source_target_pairs={{0,1},{1,0},{2,3},{3,2},{4,5},{5,4},{6,7},{7,6},{8,9},{9,8},{10,11... | collective-permute-start | bytes 12582920 | tf_op jit(solution)/shard_map/ppermute | solution.py:43
  39.8 12.6 %collective-permute-start.3 = (bf16[2,3,2048]{2,1,0:T(4,128)(2,1)S(1)}, bf16[2,3,2048]{2,1,0:T(4,128)(2,1)S(1)}, u32[]{:S(2)}, u32[]{:S(2)}) collective-permute-start(bf16[2,3,2048]{2,1,0:T(4,128)(2,1)S(1)} %slice.146), channel_id=1, source_target_pairs={{0,2},{2,4},{4,6},{6,8},{8,10},{10,12},{12,14},{14,16},{16,18},{18... | collective-permute-start | bytes 73736 | tf_op jit(solution)/shard_map/ppermute | solution.py:766
  61.0 9.3 %collective-permute-start.4 = (f32[512,160]{0,1:T(8,128)S(1)}, f32[512,160]{0,1:T(8,128)S(1)}, u32[]{:S(2)}, u32[]{:S(2)}) collective-permute-start(f32[512,160]{0,1:T(8,128)S(1)} %fusion.69), channel_id=1, source_target_pairs={{0,1},{1,0},{2,3},{3,2},{4,5},{5,4},{6,7},{7,6},{8,9},{9,8},{10,11... | collective-permute-start | bytes 983048 | tf_op jit(solution)/shard_map/ppermute | solution.py:43
  107.5 16.9 %all-to-all-start = ((bf16[16,3,32,128]{3,2,1,0:T(8,128)(2,1)}), bf16[16,3,32,128]{3,2,1,0:T(8,128)(2,1)S(1)}, u32[]{:S(2)}, u32[]{:S(2)}) async-start(bf16[16,3,32,128]{3,2,1,0:T(8,128)(2,1)} %get-tuple-element.60), calls=%async_computation | async-start | bytes 786432 | tf_op jit(solution)/shard_map/all_to_all | solution.py:748
  126.9 12.7 %all-to-all-start.1 = ((bf16[16,2,32,128]{3,2,1,0:T(8,128)(2,1)}), bf16[16,2,32,128]{3,2,1,0:T(8,128)(2,1)S(1)}, u32[]{:S(2)}, u32[]{:S(2)}) async-start(bf16[16,2,32,128]{3,2,1,0:T(8,128)(2,1)} %chain.1), calls=%async_computation.1 | async-start | bytes 524288 | tf_op jit(solution)/shard_map/all_to_all | solution.py:757
  172.7 42.6 %collective-permute-start.7 = (bf16[512,512]{1,0:T(8,128)(2,1)}, bf16[512,512]{1,0:T(8,128)(2,1)S(1)}, u32[]{:S(2)}, u32[]{:S(2)}) collective-permute-start(bf16[512,512]{1,0:T(8,128)(2,1)} %get-tuple-element.153), channel_id=1, source_target_pairs={{0,2},{2,0},{4,6},{6,4},{1,3},{3,1},{5,7},{7,5},{8,10},{10,8},{12,... | collective-permute-start | bytes 1572872 | tf_op jit(solution)/shard_map/ppermute | solution.py:774
  173.6 41.6 %collective-permute-start.8 = (bf16[512,512]{1,0:T(8,128)(2,1)S(1)}, bf16[512,512]{1,0:T(8,128)(2,1)S(1)}, u32[]{:S(2)}, u32[]{:S(2)}) collective-permute-start(bf16[512,512]{1,0:T(8,128)(2,1)S(1)} %get-tuple-element.152), channel_id=1, source_target_pairs={{0,4},{2,6},{4,0},{6,2},{1,5},{3,7},{5,1},{7,3},{8,12},{10,14},{12... | collective-permute-start | bytes 1572872 | tf_op jit(solution)/shard_map/ppermute | solution.py:774
  173.7 41.6 %collective-permute-start.9 = (bf16[512,512]{1,0:T(8,128)(2,1)S(1)}, bf16[512,512]{1,0:T(8,128)(2,1)}, u32[]{:S(2)}, u32[]{:S(2)}) collective-permute-start(bf16[512,512]{1,0:T(8,128)(2,1)S(1)} %get-tuple-element.151), channel_id=1, source_target_pairs={{0,6},{2,4},{4,2},{6,0},{1,7},{3,5},{5,3},{7,1},{8,14},{10,12},{12... | collective-permute-start | bytes 1572872 | tf_op jit(solution)/shard_map/ppermute | solution.py:774
  210.4 64.9 %all-to-all-start.2 = ((bf16[4,512,512]{2,1,0:T(8,128)(2,1)}), bf16[4,512,512]{2,1,0:T(8,128)(2,1)}, u32[]{:S(2)}, u32[]{:S(2)}) async-start(bf16[4,512,512]{2,1,0:T(8,128)(2,1)} %get-tuple-element.82), calls=%async_computation.2 | async-start | bytes 4194304 | tf_op jit(solution)/shard_map/all_to_all | solution.py:910
  223.8 48.6 %collective-permute-start.10 = (bf16[2,512,512]{2,1,0:T(8,128)(2,1)S(1)}, bf16[2,512,512]{2,1,0:T(8,128)(2,1)}, u32[]{:S(2)}, u32[]{:S(2)}) collective-permute-start(bf16[2,512,512]{2,1,0:T(8,128)(2,1)S(1)} %fusion.41), channel_id=1, source_target_pairs={{0,8},{8,0},{16,24},{24,16},{1,9},{9,1},{17,25},{25,17},{2,10},{10... | collective-permute-start | bytes 3145736 | tf_op jit(solution)/shard_map/ppermute | solution.py:784
  276.6 7.8 %collective-permute-start.11 = (f32[512,160]{0,1:T(8,128)S(1)}, f32[512,160]{0,1:T(8,128)}, u32[]{:S(2)}, u32[]{:S(2)}) collective-permute-start(f32[512,160]{0,1:T(8,128)S(1)} %copy.62), channel_id=1, source_target_pairs={{0,1},{1,0},{2,3},{3,2},{4,5},{5,4},{6,7},{7,6},{8,9},{9,8},{10,11... | collective-permute-start | bytes 983048 | tf_op jit(solution)/shard_map/ppermute | solution.py:43
  282.3 63.1 %collective-permute-start.14 = (bf16[1,512,512]{2,1,0:T(8,128)(2,1)}, bf16[1,512,512]{2,1,0:T(8,128)(2,1)}, u32[]{:S(2)}, u32[]{:S(2)}) collective-permute-start(bf16[1,512,512]{2,1,0:T(8,128)(2,1)} %dynamic-slice_convert_fusion.3), channel_id=1, source_target_pairs={{0,16},{8,24},{16,0},{24,8},{1,17},{9,25},{17,1},{25,9},{2,18},{10... | collective-permute-start | bytes 1572872 | tf_op jit(solution)/shard_map/ppermute | solution.py:784
  291.7 5.4 %collective-permute-start.12 = (f32[2,3,2048]{2,1,0:T(4,128)S(1)}, f32[2,3,2048]{2,1,0:T(4,128)S(1)}, u32[]{:S(2)}, u32[]{:S(2)}) collective-permute-start(f32[2,3,2048]{2,1,0:T(4,128)S(1)} %slice.156), channel_id=1, source_target_pairs={{2,0},{4,2},{6,4},{8,6},{10,8},{12,10},{14,12},{16,14},{18,16},{20... | collective-permute-start | bytes 147464 | tf_op jit(solution)/shard_map/ppermute | solution.py:766
  302.9 44.5 %all-to-all-start.3 = ((bf16[4,512,512]{2,1,0:T(8,128)(2,1)}), bf16[4,512,512]{2,1,0:T(8,128)(2,1)S(1)}, u32[]{:S(2)}, u32[]{:S(2)}) async-start(bf16[4,512,512]{2,1,0:T(8,128)(2,1)} %correlate.1.inner_ref), calls=%async_computation.3 | async-start | bytes 4194304 | tf_op jit(solution)/shard_map/all_to_all | solution.py:956
  355.2 23.9 %collective-permute-start.18 = (bf16[2,128,2048]{2,1,0:T(8,128)(2,1)S(1)}, bf16[2,128,2048]{2,1,0:T(8,128)(2,1)S(1)}, u32[]{:S(2)}, u32[]{:S(2)}) collective-permute-start(bf16[2,128,2048]{2,1,0:T(8,128)(2,1)S(1)} %fusion.42), channel_id=1, source_target_pairs={{0,2},{2,0},{4,6},{6,4},{1,3},{3,1},{5,7},{7,5},{8,10},{10,8},{12,... | collective-permute-start | bytes 3145736 | tf_op jit(solution)/shard_map/ppermute | solution.py:784
  356.8 23.9 %collective-permute-start.15 = (f32[256,2048]{1,0:T(8,128)S(1)}, f32[256,2048]{1,0:T(8,128)S(1)}, u32[]{:S(2)}, u32[]{:S(2)}) collective-permute-start(f32[256,2048]{1,0:T(8,128)S(1)} %copy-done.46), channel_id=1, source_target_pairs={{0,1},{1,0},{2,3},{3,2},{4,5},{5,4},{6,7},{7,6},{8,9},{9,8},{10,11... | collective-permute-start | bytes 6291464 | tf_op jit(solution)/shard_map/ppermute | solution.py:43
  366.5 32.6 %collective-permute-start.16 = (bf16[2,512,512]{2,1,0:T(8,128)(2,1)}, bf16[2,512,512]{2,1,0:T(8,128)(2,1)}, u32[]{:S(2)}, u32[]{:S(2)}) collective-permute-start(bf16[2,512,512]{2,1,0:T(8,128)(2,1)} %fusion.40), channel_id=1, source_target_pairs={{0,8},{8,0},{16,24},{24,16},{1,9},{9,1},{17,25},{25,17},{2,10},{10... | collective-permute-start | bytes 3145736 | tf_op jit(solution)/shard_map/ppermute | solution.py:784
  386.0 20.3 %collective-permute-start.19 = (bf16[1,128,2048]{2,1,0:T(8,128)(2,1)}, bf16[1,128,2048]{2,1,0:T(8,128)(2,1)}, u32[]{:S(2)}, u32[]{:S(2)}) collective-permute-start(bf16[1,128,2048]{2,1,0:T(8,128)(2,1)} %dynamic-slice_convert_fusion.2), channel_id=1, source_target_pairs={{0,4},{2,6},{4,0},{6,2},{1,5},{3,7},{5,1},{7,3},{8,12},{10,14},{12... | collective-permute-start | bytes 1572872 | tf_op jit(solution)/shard_map/ppermute | solution.py:784
  391.2 22.0 %all-to-all-start.4 = ((bf16[4,2,304,256]{3,2,1,0:T(8,128)(2,1)}), bf16[4,2,304,256]{3,2,1,0:T(8,128)(2,1)}, u32[]{:S(2)}, u32[]{:S(2)}) async-start(bf16[4,2,304,256]{3,2,1,0:T(8,128)(2,1)} %copy-done.9), calls=%async_computation.4 | async-start | bytes 2490368 | tf_op jit(solution)/shard_map/all_to_all | solution.py:997
  398.8 54.0 %collective-permute-start.13 = (f32[256,2048]{1,0:T(8,128)}, f32[256,2048]{1,0:T(8,128)}, u32[]{:S(2)}, u32[]{:S(2)}) collective-permute-start(f32[256,2048]{1,0:T(8,128)} %dynamic-slice_bitcast_fusion), channel_id=1, source_target_pairs={{0,1},{1,0},{2,3},{3,2},{4,5},{5,4},{6,7},{7,6},{8,9},{9,8},{10,11... | collective-permute-start | bytes 6291464 | tf_op jit(solution)/shard_map/ppermute | solution.py:43
  415.4 5.8 %collective-permute-start.20 = (bf16[1,304,256]{2,1,0:T(8,128)(2,1)}, bf16[1,304,256]{2,1,0:T(8,128)(2,1)S(1)}, u32[]{:S(2)}, u32[]{:S(2)}) collective-permute-start(bf16[1,304,256]{2,1,0:T(8,128)(2,1)} %dynamic-slice_convert_fusion.4), channel_id=1, source_target_pairs={{0,8},{8,0},{16,24},{24,16},{1,9},{9,1},{17,25},{25,17},{2,10},{10... | collective-permute-start | bytes 466952 | tf_op jit(solution)/shard_map/ppermute | solution.py:784
  416.3 30.7 %collective-permute-start.23 = (bf16[1,512,512]{2,1,0:T(8,128)(2,1)S(1)}, bf16[1,512,512]{2,1,0:T(8,128)(2,1)S(1)}, u32[]{:S(2)}, u32[]{:S(2)}) collective-permute-start(bf16[1,512,512]{2,1,0:T(8,128)(2,1)S(1)} %dynamic-slice_convert_fusion.1), channel_id=1, source_target_pairs={{0,16},{8,24},{16,0},{24,8},{1,17},{9,25},{17,1},{25,9},{2,18},{10... | collective-permute-start | bytes 1572872 | tf_op jit(solution)/shard_map/ppermute | solution.py:784
  421.3 11.9 %collective-permute-start.21 = (bf16[304,256]{1,0:T(8,128)(2,1)S(1)}, bf16[304,256]{1,0:T(8,128)(2,1)S(1)}, u32[]{:S(2)}, u32[]{:S(2)}) collective-permute-start(bf16[304,256]{1,0:T(8,128)(2,1)S(1)} %bitcast_convert_fusion.2), channel_id=1, source_target_pairs={{1,17},{9,25},{16,0},{24,8},{3,19},{11,27},{18,2},{26,10},{5,21},{... | collective-permute-start | bytes 466952 | tf_op jit(solution)/shard_map/ppermute | solution.py:813
  434.0 27.5 %collective-permute-start.22 = (f32[304,128]{1,0:T(8,128)}, f32[304,128]{1,0:T(8,128)S(1)}, u32[]{:S(2)}, u32[]{:S(2)}) collective-permute-start(f32[304,128]{1,0:T(8,128)} %constant_dynamic-slice_fusion), channel_id=1, source_target_pairs={{0,1},{1,0},{2,3},{3,2},{4,5},{5,4},{6,7},{7,6},{8,9},{9,8},{10,11... | collective-permute-start | bytes 466952 | tf_op jit(solution)/shard_map/ppermute | solution.py:43
  448.3 18.4 %all-to-all-start.5 = ((bf16[4,128,1024]{2,1,0:T(8,128)(2,1)}), bf16[4,128,1024]{2,1,0:T(8,128)(2,1)}, u32[]{:S(2)}, u32[]{:S(2)}) async-start(bf16[4,128,1024]{2,1,0:T(8,128)(2,1)} %bitcast.250), calls=%async_computation.5 | async-start | bytes 2097152 | tf_op jit(solution)/shard_map/all_to_all | solution.py:920
  459.4 14.9 %collective-permute-start.25 = (bf16[128,2048]{1,0:T(8,128)(2,1)S(1)}, bf16[128,2048]{1,0:T(8,128)(2,1)S(1)}, u32[]{:S(2)}, u32[]{:S(2)}) collective-permute-start(bf16[128,2048]{1,0:T(8,128)(2,1)S(1)} %convert_element_type.204), channel_id=1, source_target_pairs={{1,16},{9,24},{16,1},{24,9},{3,18},{11,26},{18,3},{26,11},{5,20},{... | collective-permute-start | bytes 1572872 | tf_op jit(solution)/shard_map/ppermute | solution.py:802
  467.7 7.7 %collective-permute-start.24 = (bf16[4,64,1024]{2,1,0:T(8,128)(2,1)S(1)}, bf16[4,64,1024]{2,1,0:T(8,128)(2,1)}, u32[]{:S(2)}, u32[]{:S(2)}) collective-permute-start(bf16[4,64,1024]{2,1,0:T(8,128)(2,1)S(1)} %dynamic-slice_bitcast_fusion.1), channel_id=1, source_target_pairs={{0,1},{1,0},{2,3},{3,2},{4,5},{5,4},{6,7},{7,6},{8,9},{9,8},{10,11... | collective-permute-start | bytes 1572872 | tf_op jit(solution)/shard_map/ppermute | solution.py:43
  (49 other events, 492.1 us)
Sparse Core Ops, SparseCore 0:
  9.6 84.5 all-gather.5
  96.7 59.7 all-gather.3

commit v3 on v2

--- a/solution.py
+++ b/solution.py
@@ -940,10 +940,12 @@
     first_part = list(run_backward(0, (), *operands))
     *traded, first_part[1] = together(*traded, first_part[1])
     early_all = ordered_members(traded)
-    gate_partial, *first_part = together(in_weight_partial(early_all), *first_part)
+    gate_partial, branch_all, *first_part = together(
+        in_weight_partial(early_all), branch_all, *first_part
+    )
     gate_mid = line_step(gate_partial, 1)
     d_logits, d_selected, d_base, bias_term = run_backward(1, tuple(first_part), *operands)
-    d_selected, branch_all, gate_mid = together(d_selected, branch_all, gate_mid)
+    d_selected, gate_mid = together(d_selected, gate_mid)
     d_logits = d_logits.reshape(rows, half)
     d_selected = d_selected.reshape(rows, -1)
     d_selected = d_selected + swap(d_selected)
@@ -952,14 +954,12 @@
     d_conv = (d_inner * swish_slope(conv_sum)).reshape(2, length, half)
     later = shifted(d_conv[:, :reach], -1)
     split = run_correlate(d_conv, later, conv_wide.T, taps)
-    split, early, branch = together(split, early, branch)
+    split, early = together(split, early)
     inner_all = lax.all_to_all(split, "member", 0, 0).reshape(group * rows, width)
     kept, sent = run_normed(core_index, split, early, in_weight, inner_got, gate_got, 10)
     gate_part = line_reduce(gate_mid, 2)
-    inner_all, gate_part, kept, sent, branch_all = together(
-        inner_all, gate_part, kept, sent, branch_all
-    )
-    inner_partial = in_weight_partial(inner_all)
+    inner_all, gate_part, kept, sent = together(inner_all, gate_part, kept, sent)
+    inner_partial, branch_all, branch = together(in_weight_partial(inner_all), branch_all, branch)
     out_partial = matmul_tn(branch_all, cot_all).reshape(group, -1, model)
 
     out_sum = run_product(branch, out_weight, False, 5)
@@ -995,9 +995,11 @@
 
     inner_mid = line_step(inner_partial, 1)
     pack_all = lax.all_to_all(pack, "member", 0, 0)
-    out_total = line_reduce(out_partial, 1, "member")
-    inner_mid, pack_all, out_total = together(inner_mid, pack_all, out_total)
+    out_mid = line_step(out_partial, 1, "member")
+    inner_mid, out_mid = together(inner_mid, out_mid)
     inner_part = line_reduce(inner_mid, 2)
+    out_total = line_reduce(out_mid, 2, "member")
+    inner_part, out_total, pack_all = together(inner_part, out_total, pack_all)
     pack_own = owner_part(owner_sum(jnp.sum(pack_all.astype(f32), axis=0)), 1).T
     out_grad = to_owner(out_total)
     in_grad = in_weight_rows(inner_part.astype(bf16), gate_part.astype(bf16))

time: 491 us -> 465 us (0.947)
  starting transfers between devices: 82.8 us -> 62.9 us
  waiting for transfers between devices: 82.5 us -> 70.6 us
    ppermute x12, starting transfers between devices: 21.8 us -> 10.3 us  [swap(): return lax.ppermute(value, 'fsdp', [(0, 1), (1, 0)])]
    all_to_all x1, starting transfers between devices: 15.6 us -> 4.83 us  [local(): lax.all_to_all(split, 'member', 0, 0).reshape(group * rows, width)]
    ppermute x1, waiting for transfers between devices: 10.6 us -> 0.01 us  [owner_sum(): lax.ppermute(partial.astype(bf16), ('outer', 'fsdp'), pairs).astype(f32)]
    unnamed x110 -> x114, local copies, waits for them, and re-layouts: 13.1 us -> 12.6 us
  transfers between devices with their start and end apart: 34 -> 34, of which waited for: 13 -> 14; matrix products, arithmetic and copies ran while one was open for 16% -> 17% of each run, Pallas kernels for 41% -> 42%
where the time goes in v3:
time: 465 us; the launch traced here: 460 us
  Pallas kernels  199 us (43%)
  waiting for transfers between devices  70.6 us (15%)
  starting transfers between devices  62.9 us (14%)
  other arithmetic  46.8 us (10%)
  local copies, waits for them, and re-layouts  35.8 us (8%)
  matrix products  29.3 us (6%)
  between operations  15.4 us (3%)
    pallas_call x3, Pallas kernels, per_sequence(): pl.pallas_call(kernel, grid=(sequences,), in_specs=[(in_specs or {}).get(...  70.7 us
    pallas_call x2, Pallas kernels, run_backward(): pl.pallas_call(kernel, grid=(1,), in_specs=[pl.BlockSpec(memory_space=pl....  70.3 us
    ppermute x7, waiting for transfers between devices, line_step(): got = lax.ppermute(sent, axis, [(o, o ^ bit) for o in range(count)])  31.3 us
    dot_general x3, matrix products, matmul_tn(): lax.dot_general(left, right, (((0,), (0,)), ((), ())), preferred_element_...  22.2 us
    pallas_call x1, Pallas kernels, run_normed(): pl.pallas_call(normed_kernel, grid_spec=pltpu.PrefetchScalarGridSpec(num_...  16.7 us
    pallas_call x2, Pallas kernels, run_product(): pl.pallas_call(functools.partial(whole_kernel, transposed), grid=(columns...  14.8 us
    pallas_call x2, Pallas kernels, run_project(): pl.pallas_call(project_kernel, grid_spec=pltpu.PrefetchScalarGridSpec(num...  14.4 us
    unnamed x114, local copies, waits for them, and re-layouts  12.6 us
  transfers between devices with their start and end apart: 34, of which 14 were waited for; matrix products, arithmetic and copies ran while one was open for 17% of the time, Pallas kernels for 42%

profile of v3, /device:TPU:1, one launch (start us, length us, event | category | flops | bytes accessed | tf_op | source)
XLA Modules:
  0.0 460.1 jit_solution(3823727879903369145)
XLA Ops:
  11.7 4.9 %columns.2 = bf16[1024,2048]{1,0:T(8,128)(2,1)} custom-call(s32[1]{0:T(128)} %bitcast.2.core_ref, bf16[1024,8192]{1,0:T(8,128)(2,1)} %gate_own.1), custom_call_target="tpu_custom_call" | custom-call | tf_op jit(solution)/shard_map/columns/pallas_call | solution.py:365
  17.6 5.0 %columns.3 = bf16[1024,2048]{1,0:T(8,128)(2,1)} custom-call(s32[1]{0:T(128)} %bitcast.2.core_ref, bf16[1024,8192]{1,0:T(8,128)(2,1)} %gate_own.1), custom_call_target="tpu_custom_call" | custom-call | tf_op jit(solution)/shard_map/columns/pallas_call | solution.py:365
  32.6 7.1 %project.2 = bf16[512,2048]{1,0:T(8,128)(2,1)S(1)} custom-call(s32[1]{0:T(128)} %bitcast.2.core_ref, bf16[512,2048]{1,0:T(8,128)(2,1)S(1)} %fusion.2.x_ref, bf16[1024,8192]{1,0:T(8,128)(2,1)} %gate_own.1, bf16[1024,2048]{1,0:T(8,128)(2,1)} %collective-permute-done.2.got_ref.inner_got), custom_call_target="tpu_custom_call" | custom-call | flops 5750000128 | bytes 8388608 | tf_op jit(solution)/shard_map/project/pallas_call | solution.py:425
  39.8 5.0 %collective-permute-start.3 = (bf16[2,3,2048]{2,1,0:T(4,128)(2,1)S(1)}, bf16[2,3,2048]{2,1,0:T(4,128)(2,1)S(1)}, u32[]{:S(2)}, u32[]{:S(2)}) collective-permute-start(bf16[2,3,2048]{2,1,0:T(4,128)(2,1)S(1)} %slice.146), channel_id=1, source_target_pairs={{0,2},{2,4},{4,6},{6,8},{8,10},{10,12},{12,14},{14,16},{16,18},{18... | collective-permute-start | bytes 73736 | tf_op jit(solution)/shard_map/ppermute | solution.py:766
  44.8 7.3 %product.2 = f32[512,2048]{1,0:T(8,128)S(1)} custom-call(bf16[512,2048]{1,0:T(8,128)(2,1)S(1)} %pad_maximum_fusion.2.left_ref, bf16[2048,2048]{1,0:T(8,128)(2,1)} %right_ref.3), custom_call_target="tpu_custom_call" | custom-call | flops 5750000128 | bytes 1048576 | tf_op jit(solution)/shard_map/product/pallas_call | solution.py:396
  52.2 4.3 multiply_convert_fusion
  61.5 7.3 %project.3 = bf16[512,2048]{1,0:T(8,128)(2,1)S(1)} custom-call(s32[1]{0:T(128)} %bitcast.2.core_ref, bf16[512,2048]{1,0:T(8,128)(2,1)S(1)} %fusion.2.x_ref, bf16[1024,8192]{1,0:T(8,128)(2,1)} %gate_own.1, bf16[1024,2048]{1,0:T(8,128)(2,1)S(1)} %collective-permute-done.5.got_ref.gate_got), custom_call_target="tpu_custom_call" | custom-call | flops 5750000128 | bytes 8388608 | tf_op jit(solution)/shard_map/project/pallas_call | solution.py:425
  71.4 35.8 %summary.1 = (f32[2,256,2048]{2,1,0:T(8,128)}, f32[2,256,2048]{2,1,0:T(8,128)}, f32[2,256,2048]{2,1,0:T(8,128)}, bf16[16,3,32,128]{3,2,1,0:T(8,128)(2,1)}) custom-call(f32[2,256,160]{2,1,0:T(8,128)} %copy.54.sel_ref.refs_0_.refs_4_, bf16[2,256,2048]{2,1,0:T(8,128)(2,1)} %get-tuple-element.151.act_ref.refs_4_.refs_8_, bf16[2,256,2048]{2,1,0:T(8,128)(2,1)} %bitcast.245, ...), custom_call_target="tpu_custom_call" | custom-call | flops 28750000128 | bytes 22224896 | tf_op jit(solution)/shard_map/summary/pallas_call | solution.py:581
  107.2 6.0 %all-to-all-start = ((bf16[16,3,32,128]{3,2,1,0:T(8,128)(2,1)}), bf16[16,3,32,128]{3,2,1,0:T(8,128)(2,1)S(1)}, u32[]{:S(2)}, u32[]{:S(2)}) async-start(bf16[16,3,32,128]{3,2,1,0:T(8,128)(2,1)} %get-tuple-element.63), calls=%async_computation | async-start | bytes 786432 | tf_op jit(solution)/shard_map/all_to_all | solution.py:748
  113.3 10.8 %all-to-all-done.pieces_ref = bf16[16,3,32,128]{3,2,1,0:T(8,128)(2,1)S(1)} async-done(((bf16[16,3,32,128]{3,2,1,0:T(8,128)(2,1)}), bf16[16,3,32,128]{3,2,1,0:T(8,128)(2,1)S(1)}, u32[]{:S(2)}, u32[]{:S(2)}) %all-to-all-start) | async-done | bytes 393248 | tf_op jit(solution)/shard_map/all_to_all | solution.py:748
  126.6 5.4 %all-to-all-start.1 = ((bf16[16,2,32,128]{3,2,1,0:T(8,128)(2,1)}), bf16[16,2,32,128]{3,2,1,0:T(8,128)(2,1)S(1)}, u32[]{:S(2)}, u32[]{:S(2)}) async-start(bf16[16,2,32,128]{3,2,1,0:T(8,128)(2,1)} %chain.1), calls=%async_computation.1 | async-start | bytes 524288 | tf_op jit(solution)/shard_map/all_to_all | solution.py:757
  134.0 5.6 %all-to-all-done.1.init_ref.refs_6_.refs_10_ = bf16[16,2,32,128]{3,2,1,0:T(8,128)(2,1)S(1)} async-done(((bf16[16,2,32,128]{3,2,1,0:T(8,128)(2,1)}), bf16[16,2,32,128]{3,2,1,0:T(8,128)(2,1)S(1)}, u32[]{:S(2)}, u32[]{:S(2)}) %all-to-all-start.1) | async-done | bytes 262176 | tf_op jit(solution)/shard_map/all_to_all | solution.py:757
  140.3 29.8 %forward.1 = (bf16[4,512,512]{2,1,0:T(8,128)(2,1)}, bf16[4,512,512]{2,1,0:T(8,128)(2,1)}, bf16[2,256,2048]{2,1,0:T(8,128)(2,1)}, f32[2,16,16,2048]{3,2,1,0:T(8,128)}, f32[2,1,2048]{2,1,0:T(1,128)}) custom-call(f32[2,256,160]{2,1,0:T(8,128)} %copy.54.sel_ref.refs_0_.refs_4_, f32[2,256,2048]{2,1,0:T(8,128)} %get-tuple-element.61.r_ref.refs_1_.refs_5_, ...), custom_call_target="tpu_custom_call" | custom-call | flops 23000000512 | bytes 28139520 | tf_op jit(solution)/shard_map/forward/pallas_call | solution.py:581
  175.5 4.3 all-to-all-start.2
  179.9 35.1 %backward.2 = (bf16[2,256,2048]{2,1,0:T(8,128)(2,1)}, f32[2,256,160]{2,1,0:T(8,128)}, f32[2,256,2048]{2,1,0:T(8,128)}, f32[2,1,2048]{2,1,0:T(1,128)}) custom-call(f32[2,256,160]{2,1,0:T(8,128)} %copy.54.sel_ref.refs_0_.refs_4_, f32[2,256,2048]{2,1,0:T(8,128)} %get-tuple-element.61.r_ref.refs_1_.refs_5_, ...), custom_call_target="tpu_custom_call" | custom-call | flops 39099998208 | bytes 13180928 | tf_op jit(solution)/shard_map/backward/pallas_call | solution.py:689
  216.7 9.8 %fusion.32 = f32[2048,512]{1,0:T(8,128)} fusion(bf16[2048,2048]{1,0:T(8,128)(2,1)} %all-gather.4.cloned.1.call-done, bf16[512,512]{1,0:T(8,128)(2,1)S(1)} %get-tuple-element.154, bf16[512,512]{1,0:T(8,128)(2,1)S(1)} %get-tuple-element.155, bf16[512,512]{1,0:T(8,128)(2,1)S(1)} %get-tuple-element.156, bf16[512,512]{1,0:T(8,128)(2,1)S(1)} %get-tuple-element.153), kind=kOutput, calls=%fused_computation.56 | convolution fusion | flops 4303355904 | bytes 14680064 | tf_op jit(solution)/shard_map/dot_general | solution.py:30
  230.5 35.2 %backward.3 = (bf16[2,256,2048]{2,1,0:T(8,128)(2,1)}, f32[2,256,160]{2,1,0:T(8,128)}, f32[2,256,2048]{2,1,0:T(8,128)}, f32[2,1,2048]{2,1,0:T(1,128)}) custom-call(bf16[2,256,2048]{2,1,0:T(8,128)(2,1)} %get-tuple-element.80.refs_0_, ...), custom_call_target="tpu_custom_call", output_to_operand_aliasing={{0}: (0, {}), {1}: (1, {}), {2}: (2, {}), {3}: (3, {})} | custom-call | flops 39099998208 | bytes 13180928 | tf_op jit(solution)/shard_map/backward/pallas_call | solution.py:689
  275.8 6.3 %fusion.9 = (f32[2048]{0:T(1024)S(1)}, f32[2048]{0:T(1024)S(1)}, f32[2048]{0:T(1024)S(1)}, f32[512,2048]{1,0:T(8,128)S(1)}) fusion(bf16[2,256,2048]{2,1,0:T(8,128)(2,1)S(1)} %bitcast.241, bf16[2,3,2048]{2,1,0:T(4,128)(2,1)S(1)} %copy-done.39, f32[2,256,2048]{2,1,0:T(8,128)} %copy-done.17, bf16[512,160]{0,1:T(8,128)(2,1)S(1)} %add_convert_fusion, ...), kind=kOutput, calls=%fused_computation.17 | convolution fusion | flops 363849728 | bytes 15548416 | tf_op jit(solution)/shard_map/dot_general | solution.py:26
  289.9 5.1 %correlate.1.inner_ref = bf16[4,512,512]{2,1,0:T(8,128)(2,1)} custom-call(f32[2,256,2048]{2,1,0:T(8,128)} %bitcast.254, f32[2,8,2048]{2,1,0:T(8,128)} %pad.12.later_ref, f32[4,2048]{1,0:T(4,128)} %convert_bitcast_fusion.w_ref), custom_call_target="tpu_custom_call" | custom-call | flops 4600000000 | bytes 6455296 | tf_op jit(solution)/shard_map/correlate/pallas_call | solution.py:581
  294.9 4.8 %all-to-all-start.3 = ((bf16[4,512,512]{2,1,0:T(8,128)(2,1)}), bf16[4,512,512]{2,1,0:T(8,128)(2,1)}, u32[]{:S(2)}, u32[]{:S(2)}) async-start(bf16[4,512,512]{2,1,0:T(8,128)(2,1)} %correlate.1.inner_ref), calls=%async_computation.3 | async-start | bytes 4194304 | tf_op jit(solution)/shard_map/all_to_all | solution.py:958
  304.3 16.7 %normed.1 = (f32[256,2048]{1,0:T(8,128)S(1)}, f32[256,2048]{1,0:T(8,128)}) custom-call(s32[1]{0:T(128)} %bitcast.2.core_ref, bf16[4,512,512]{2,1,0:T(8,128)(2,1)} %correlate.1.inner_ref, bf16[4,512,512]{2,1,0:T(8,128)(2,1)} %get-tuple-element.90.gate_ref, bf16[1024,8192]{1,0:T(8,128)(2,1)} %gate_own.1, bf16[1024,8192]{1,0:T(8,128)(2,1)} %gate_own.1, ...), custom_call_target="tpu_custom_call" | custom-call | flops 11500000256 | bytes 1048576 | tf_op jit(solution)/shard_map/normed/pallas_call | solution.py:503
  322.3 5.9 %collective-permute-done.13 = bf16[1,512,512]{2,1,0:T(8,128)(2,1)S(1)} collective-permute-done((bf16[1,512,512]{2,1,0:T(8,128)(2,1)S(1)}, bf16[1,512,512]{2,1,0:T(8,128)(2,1)S(1)}, u32[]{:S(2)}, u32[]{:S(2)}) %collective-permute-start.13) | collective-permute-done | bytes 524320 | tf_op jit(solution)/shard_map/ppermute | solution.py:784
  329.8 7.9 %fusion.69 = f32[2048,512]{1,0:T(8,128)S(1)} fusion(bf16[2048,2048]{1,0:T(8,128)(2,1)} %all-gather.4.cloned.1.call-done, bf16[2048,512]{1,0:T(8,128)(2,1)} %bitcast.37), kind=kOutput, calls=%fused_computation.168 | convolution fusion | flops 4294967296 | bytes 14680064 | tf_op jit(solution)/shard_map/dot_general | solution.py:30
  338.8 4.6 fusion.70
  346.7 7.4 %product.3 = f32[512,2048]{1,0:T(8,128)S(1)} custom-call(bf16[512,2048]{1,0:T(8,128)(2,1)S(1)} %bitcast.250, bf16[2048,2048]{1,0:T(8,128)(2,1)} %right_ref.3), custom_call_target="tpu_custom_call" | custom-call | flops 5750000128 | bytes 1048576 | tf_op jit(solution)/shard_map/product/pallas_call | solution.py:396
  354.2 9.8 %collective-permute-done.16 = bf16[2,512,512]{2,1,0:T(8,128)(2,1)} collective-permute-done((bf16[2,512,512]{2,1,0:T(8,128)(2,1)}, bf16[2,512,512]{2,1,0:T(8,128)(2,1)}, u32[]{:S(2)}, u32[]{:S(2)}) %collective-permute-start.16) | collective-permute-done | bytes 1048608 | tf_op jit(solution)/shard_map/ppermute | solution.py:784
  365.6 4.1 collective-permute-done.17
  393.1 6.8 %collective-permute-done.18 = bf16[1,512,512]{2,1,0:T(8,128)(2,1)} collective-permute-done((bf16[1,512,512]{2,1,0:T(8,128)(2,1)}, bf16[1,512,512]{2,1,0:T(8,128)(2,1)}, u32[]{:S(2)}, u32[]{:S(2)}) %collective-permute-start.18) | collective-permute-done | bytes 524320 | tf_op jit(solution)/shard_map/ppermute | solution.py:784
  408.2 4.7 %collective-permute-done.21 = bf16[1,304,256]{2,1,0:T(8,128)(2,1)S(1)} collective-permute-done((bf16[1,304,256]{2,1,0:T(8,128)(2,1)S(1)}, bf16[1,304,256]{2,1,0:T(8,128)(2,1)S(1)}, u32[]{:S(2)}, u32[]{:S(2)}) %collective-permute-start.21) | collective-permute-done | bytes 155680 | tf_op jit(solution)/shard_map/ppermute | solution.py:784
  418.3 4.4 all-to-all-start.5
  426.1 6.5 %fusion.28 = (f32[1,256,2048]{2,1,0:T(8,128)}, bf16[1,256,2048]{2,1,0:T(8,128)(2,1)}) fusion(f32[256]{0:T(256)S(1)} %broadcast_multiply_fusion, f32[2048]{0:T(1024)S(1)} %copy-done.35, f32[256]{0:T(256)S(1)} %copy-done.41, bf16[1,256,2048]{2,1,0:T(8,128)(2,1)} %param.12, bf16[1,256,2048]{2,1,0:T(8,128)(2,1)} %param.11, f32[256,2048]{1,0:T(8,128)S(1)} %copy-done.8, ...), kind=kLoop, calls=%fused_computation.48 | loop fusion | flops 6291456 | bytes 13641732 | tf_op jit(solution)/shard_map/broadcast_in_dim | solution.py:1018
  441.0 7.9 %collective-permute-done.25 = bf16[128,2048]{1,0:T(8,128)(2,1)S(1)} collective-permute-done((bf16[128,2048]{1,0:T(8,128)(2,1)S(1)}, bf16[128,2048]{1,0:T(8,128)(2,1)S(1)}, u32[]{:S(2)}, u32[]{:S(2)}) %collective-permute-start.25) | collective-permute-done | bytes 524320 | tf_op jit(solution)/shard_map/ppermute | solution.py:802
  (256 shorter events, 123.2 us)
Async XLA Ops:
  7.2 162.9 %all-gather.6.cloned.1.call-start = ((), (), s32[]{:S(2)}) async-start(), calls=%async_computation.7 | async-start | bytes 9437184 | tf_op jit(solution)/shard_map/all_gather | solution.py:874
  7.9 162.2 %all-gather.4.cloned.1.call-start = ((), (), s32[]{:S(2)}) async-start(), calls=%async_computation.6 | async-start | bytes 9437184 | tf_op jit(solution)/shard_map/all_gather | solution.py:873
  16.6 16.0 %collective-permute-start.2 = (bf16[1024,2048]{1,0:T(8,128)(2,1)}, bf16[1024,2048]{1,0:T(8,128)(2,1)}, u32[]{:S(2)}, u32[]{:S(2)}) collective-permute-start(bf16[1024,2048]{1,0:T(8,128)(2,1)} %columns.2), channel_id=1, source_target_pairs={{0,1},{1,0},{2,3},{3,2},{4,5},{5,4},{6,7},{7,6},{8,9},{9,8},{10,11... | collective-permute-start | bytes 12582920 | tf_op jit(solution)/shard_map/ppermute | solution.py:43
  17.0 8.4 %collective-permute-start = (bf16[256,2048]{1,0:T(8,128)(2,1)S(1)}, bf16[256,2048]{1,0:T(8,128)(2,1)}, u32[]{:S(2)}, u32[]{:S(2)}) collective-permute-start(bf16[256,2048]{1,0:T(8,128)(2,1)S(1)} %bitcast.251), channel_id=1, source_target_pairs={{0,1},{1,0},{2,3},{3,2},{4,5},{5,4},{6,7},{7,6},{8,9},{9,8},{10,11... | collective-permute-start | bytes 3145736 | tf_op jit(solution)/shard_map/ppermute | solution.py:43
  17.1 12.8 %collective-permute-start.6 = (bf16[256,2048]{1,0:T(8,128)(2,1)S(1)}, bf16[256,2048]{1,0:T(8,128)(2,1)}, u32[]{:S(2)}, u32[]{:S(2)}) collective-permute-start(bf16[256,2048]{1,0:T(8,128)(2,1)S(1)} %bitcast.252), channel_id=1, source_target_pairs={{0,1},{1,0},{2,3},{3,2},{4,5},{5,4},{6,7},{7,6},{8,9},{9,8},{10,11... | collective-permute-start | bytes 3145736 | tf_op jit(solution)/shard_map/ppermute | solution.py:43
  22.7 38.8 %collective-permute-start.5 = (bf16[1024,2048]{1,0:T(8,128)(2,1)}, bf16[1024,2048]{1,0:T(8,128)(2,1)S(1)}, u32[]{:S(2)}, u32[]{:S(2)}) collective-permute-start(bf16[1024,2048]{1,0:T(8,128)(2,1)} %columns.3), channel_id=1, source_target_pairs={{0,1},{1,0},{2,3},{3,2},{4,5},{5,4},{6,7},{7,6},{8,9},{9,8},{10,11... | collective-permute-start | bytes 12582920 | tf_op jit(solution)/shard_map/ppermute | solution.py:43
  39.8 12.4 %collective-permute-start.3 = (bf16[2,3,2048]{2,1,0:T(4,128)(2,1)S(1)}, bf16[2,3,2048]{2,1,0:T(4,128)(2,1)S(1)}, u32[]{:S(2)}, u32[]{:S(2)}) collective-permute-start(bf16[2,3,2048]{2,1,0:T(4,128)(2,1)S(1)} %slice.146), channel_id=1, source_target_pairs={{0,2},{2,4},{4,6},{6,8},{8,10},{10,12},{12,14},{14,16},{16,18},{18... | collective-permute-start | bytes 73736 | tf_op jit(solution)/shard_map/ppermute | solution.py:766
  60.8 9.3 %collective-permute-start.4 = (f32[512,160]{0,1:T(8,128)S(1)}, f32[512,160]{0,1:T(8,128)S(1)}, u32[]{:S(2)}, u32[]{:S(2)}) collective-permute-start(f32[512,160]{0,1:T(8,128)S(1)} %fusion.68), channel_id=1, source_target_pairs={{0,1},{1,0},{2,3},{3,2},{4,5},{5,4},{6,7},{7,6},{8,9},{9,8},{10,11... | collective-permute-start | bytes 983048 | tf_op jit(solution)/shard_map/ppermute | solution.py:43
  107.2 16.8 %all-to-all-start = ((bf16[16,3,32,128]{3,2,1,0:T(8,128)(2,1)}), bf16[16,3,32,128]{3,2,1,0:T(8,128)(2,1)S(1)}, u32[]{:S(2)}, u32[]{:S(2)}) async-start(bf16[16,3,32,128]{3,2,1,0:T(8,128)(2,1)} %get-tuple-element.63), calls=%async_computation | async-start | bytes 786432 | tf_op jit(solution)/shard_map/all_to_all | solution.py:748
  126.6 13.0 %all-to-all-start.1 = ((bf16[16,2,32,128]{3,2,1,0:T(8,128)(2,1)}), bf16[16,2,32,128]{3,2,1,0:T(8,128)(2,1)S(1)}, u32[]{:S(2)}, u32[]{:S(2)}) async-start(bf16[16,2,32,128]{3,2,1,0:T(8,128)(2,1)} %chain.1), calls=%async_computation.1 | async-start | bytes 524288 | tf_op jit(solution)/shard_map/all_to_all | solution.py:757
  172.9 42.1 %collective-permute-start.7 = (bf16[512,512]{1,0:T(8,128)(2,1)}, bf16[512,512]{1,0:T(8,128)(2,1)}, u32[]{:S(2)}, u32[]{:S(2)}) collective-permute-start(bf16[512,512]{1,0:T(8,128)(2,1)} %get-tuple-element.159), channel_id=1, source_target_pairs={{0,2},{2,0},{4,6},{6,4},{1,3},{3,1},{5,7},{7,5},{8,10},{10,8},{12,... | collective-permute-start | bytes 1572872 | tf_op jit(solution)/shard_map/ppermute | solution.py:774
  173.9 41.1 %collective-permute-start.8 = (bf16[512,512]{1,0:T(8,128)(2,1)}, bf16[512,512]{1,0:T(8,128)(2,1)}, u32[]{:S(2)}, u32[]{:S(2)}) collective-permute-start(bf16[512,512]{1,0:T(8,128)(2,1)} %get-tuple-element.158), channel_id=1, source_target_pairs={{0,4},{2,6},{4,0},{6,2},{1,5},{3,7},{5,1},{7,3},{8,12},{10,14},{12... | collective-permute-start | bytes 1572872 | tf_op jit(solution)/shard_map/ppermute | solution.py:774
  173.9 41.1 %collective-permute-start.9 = (bf16[512,512]{1,0:T(8,128)(2,1)}, bf16[512,512]{1,0:T(8,128)(2,1)}, u32[]{:S(2)}, u32[]{:S(2)}) collective-permute-start(bf16[512,512]{1,0:T(8,128)(2,1)} %get-tuple-element.157), channel_id=1, source_target_pairs={{0,6},{2,4},{4,2},{6,0},{1,7},{3,5},{5,3},{7,1},{8,14},{10,12},{12... | collective-permute-start | bytes 1572872 | tf_op jit(solution)/shard_map/ppermute | solution.py:774
  175.5 52.0 %all-to-all-start.2 = ((bf16[4,512,512]{2,1,0:T(8,128)(2,1)}), bf16[4,512,512]{2,1,0:T(8,128)(2,1)S(1)}, u32[]{:S(2)}, u32[]{:S(2)}) async-start(bf16[4,512,512]{2,1,0:T(8,128)(2,1)} %get-tuple-element.75), calls=%async_computation.2 | async-start | bytes 4194304 | tf_op jit(solution)/shard_map/all_to_all | solution.py:910
  230.0 35.7 %collective-permute-start.10 = (bf16[2,512,512]{2,1,0:T(8,128)(2,1)S(1)}, bf16[2,512,512]{2,1,0:T(8,128)(2,1)S(1)}, u32[]{:S(2)}, u32[]{:S(2)}) collective-permute-start(bf16[2,512,512]{2,1,0:T(8,128)(2,1)S(1)} %fusion.40), channel_id=1, source_target_pairs={{0,8},{8,0},{16,24},{24,16},{1,9},{9,1},{17,25},{25,17},{2,10},{10... | collective-permute-start | bytes 3145736 | tf_op jit(solution)/shard_map/ppermute | solution.py:784
  270.4 5.3 %collective-permute-start.11 = (f32[512,160]{0,1:T(8,128)S(1)}, f32[512,160]{0,1:T(8,128)S(1)}, u32[]{:S(2)}, u32[]{:S(2)}) collective-permute-start(f32[512,160]{0,1:T(8,128)S(1)} %copy.64), channel_id=1, source_target_pairs={{0,1},{1,0},{2,3},{3,2},{4,5},{5,4},{6,7},{7,6},{8,9},{9,8},{10,11... | collective-permute-start | bytes 983048 | tf_op jit(solution)/shard_map/ppermute | solution.py:43
  284.2 5.0 %collective-permute-start.12 = (f32[2,3,2048]{2,1,0:T(4,128)S(1)}, f32[2,3,2048]{2,1,0:T(4,128)S(1)}, u32[]{:S(2)}, u32[]{:S(2)}) collective-permute-start(f32[2,3,2048]{2,1,0:T(4,128)S(1)} %slice.156), channel_id=1, source_target_pairs={{2,0},{4,2},{6,4},{8,6},{10,8},{12,10},{14,12},{16,14},{18,16},{20... | collective-permute-start | bytes 147464 | tf_op jit(solution)/shard_map/ppermute | solution.py:766
  294.9 34.2 %all-to-all-start.3 = ((bf16[4,512,512]{2,1,0:T(8,128)(2,1)}), bf16[4,512,512]{2,1,0:T(8,128)(2,1)}, u32[]{:S(2)}, u32[]{:S(2)}) async-start(bf16[4,512,512]{2,1,0:T(8,128)(2,1)} %correlate.1.inner_ref), calls=%async_computation.3 | async-start | bytes 4194304 | tf_op jit(solution)/shard_map/all_to_all | solution.py:958
  302.1 26.0 %collective-permute-start.13 = (bf16[1,512,512]{2,1,0:T(8,128)(2,1)S(1)}, bf16[1,512,512]{2,1,0:T(8,128)(2,1)S(1)}, u32[]{:S(2)}, u32[]{:S(2)}) collective-permute-start(bf16[1,512,512]{2,1,0:T(8,128)(2,1)S(1)} %dynamic-slice_convert_fusion.2), channel_id=1, source_target_pairs={{0,16},{8,24},{16,0},{24,8},{1,17},{9,25},{17,1},{25,9},{2,18},{10... | collective-permute-start | bytes 1572872 | tf_op jit(solution)/shard_map/ppermute | solution.py:784
  329.2 47.2 %collective-permute-start.15 = (f32[256,2048]{1,0:T(8,128)}, f32[256,2048]{1,0:T(8,128)S(1)}, u32[]{:S(2)}, u32[]{:S(2)}) collective-permute-start(f32[256,2048]{1,0:T(8,128)} %get-tuple-element.98), channel_id=1, source_target_pairs={{0,1},{1,0},{2,3},{3,2},{4,5},{5,4},{6,7},{7,6},{8,9},{9,8},{10,11... | collective-permute-start | bytes 6291464 | tf_op jit(solution)/shard_map/ppermute | solution.py:43
  338.8 25.2 %collective-permute-start.16 = (bf16[2,512,512]{2,1,0:T(8,128)(2,1)}, bf16[2,512,512]{2,1,0:T(8,128)(2,1)}, u32[]{:S(2)}, u32[]{:S(2)}) collective-permute-start(bf16[2,512,512]{2,1,0:T(8,128)(2,1)} %fusion.41), channel_id=1, source_target_pairs={{0,8},{8,0},{16,24},{24,16},{1,9},{9,1},{17,25},{25,17},{2,10},{10... | collective-permute-start | bytes 3145736 | tf_op jit(solution)/shard_map/ppermute | solution.py:784
  344.5 25.2 %collective-permute-start.17 = (bf16[2,128,2048]{2,1,0:T(8,128)(2,1)}, bf16[2,128,2048]{2,1,0:T(8,128)(2,1)}, u32[]{:S(2)}, u32[]{:S(2)}) collective-permute-start(bf16[2,128,2048]{2,1,0:T(8,128)(2,1)} %fusion.42), channel_id=1, source_target_pairs={{0,2},{2,0},{4,6},{6,4},{1,3},{3,1},{5,7},{7,5},{8,10},{10,8},{12,... | collective-permute-start | bytes 3145736 | tf_op jit(solution)/shard_map/ppermute | solution.py:784
  373.5 26.4 %collective-permute-start.18 = (bf16[1,512,512]{2,1,0:T(8,128)(2,1)}, bf16[1,512,512]{2,1,0:T(8,128)(2,1)}, u32[]{:S(2)}, u32[]{:S(2)}) collective-permute-start(bf16[1,512,512]{2,1,0:T(8,128)(2,1)} %dynamic-slice_convert_fusion.1), channel_id=1, source_target_pairs={{0,16},{8,24},{16,0},{24,8},{1,17},{9,25},{17,1},{25,9},{2,18},{10... | collective-permute-start | bytes 1572872 | tf_op jit(solution)/shard_map/ppermute | solution.py:784
  380.8 21.2 %collective-permute-start.19 = (bf16[1,128,2048]{2,1,0:T(8,128)(2,1)}, bf16[1,128,2048]{2,1,0:T(8,128)(2,1)}, u32[]{:S(2)}, u32[]{:S(2)}) collective-permute-start(bf16[1,128,2048]{2,1,0:T(8,128)(2,1)} %dynamic-slice_convert_fusion), channel_id=1, source_target_pairs={{0,4},{2,6},{4,0},{6,2},{1,5},{3,7},{5,1},{7,3},{8,12},{10,14},{12... | collective-permute-start | bytes 1572872 | tf_op jit(solution)/shard_map/ppermute | solution.py:784
  386.0 21.9 %all-to-all-start.4 = ((bf16[4,2,304,256]{3,2,1,0:T(8,128)(2,1)}), bf16[4,2,304,256]{3,2,1,0:T(8,128)(2,1)S(1)}, u32[]{:S(2)}, u32[]{:S(2)}) async-start(bf16[4,2,304,256]{3,2,1,0:T(8,128)(2,1)} %copy-done.9), calls=%async_computation.4 | async-start | bytes 2490368 | tf_op jit(solution)/shard_map/all_to_all | solution.py:997
  392.8 33.2 %collective-permute-start.14 = (f32[256,2048]{1,0:T(8,128)}, f32[256,2048]{1,0:T(8,128)}, u32[]{:S(2)}, u32[]{:S(2)}) collective-permute-start(f32[256,2048]{1,0:T(8,128)} %dynamic-slice_bitcast_fusion), channel_id=1, source_target_pairs={{0,1},{1,0},{2,3},{3,2},{4,5},{5,4},{6,7},{7,6},{8,9},{9,8},{10,11... | collective-permute-start | bytes 6291464 | tf_op jit(solution)/shard_map/ppermute | solution.py:43
  408.1 4.8 %collective-permute-start.21 = (bf16[1,304,256]{2,1,0:T(8,128)(2,1)S(1)}, bf16[1,304,256]{2,1,0:T(8,128)(2,1)S(1)}, u32[]{:S(2)}, u32[]{:S(2)}) collective-permute-start(bf16[1,304,256]{2,1,0:T(8,128)(2,1)S(1)} %dynamic-slice_convert_fusion.3), channel_id=1, source_target_pairs={{0,8},{8,0},{16,24},{24,16},{1,9},{9,1},{17,25},{25,17},{2,10},{10... | collective-permute-start | bytes 466952 | tf_op jit(solution)/shard_map/ppermute | solution.py:784
  413.6 9.1 %collective-permute-start.22 = (bf16[304,256]{1,0:T(8,128)(2,1)}, bf16[304,256]{1,0:T(8,128)(2,1)}, u32[]{:S(2)}, u32[]{:S(2)}) collective-permute-start(bf16[304,256]{1,0:T(8,128)(2,1)} %bitcast_convert_fusion.3), channel_id=1, source_target_pairs={{1,17},{9,25},{16,0},{24,8},{3,19},{11,27},{18,2},{26,10},{5,21},{... | collective-permute-start | bytes 466952 | tf_op jit(solution)/shard_map/ppermute | solution.py:813
  418.3 18.9 %all-to-all-start.5 = ((bf16[4,128,1024]{2,1,0:T(8,128)(2,1)}), bf16[4,128,1024]{2,1,0:T(8,128)(2,1)}, u32[]{:S(2)}, u32[]{:S(2)}) async-start(bf16[4,128,1024]{2,1,0:T(8,128)(2,1)} %bitcast.255), calls=%async_computation.5 | async-start | bytes 2097152 | tf_op jit(solution)/shard_map/all_to_all | solution.py:920
  423.7 13.0 %collective-permute-start.23 = (f32[304,128]{1,0:T(8,128)S(1)}, f32[304,128]{1,0:T(8,128)S(1)}, u32[]{:S(2)}, u32[]{:S(2)}) collective-permute-start(f32[304,128]{1,0:T(8,128)S(1)} %constant_dynamic-slice_fusion), channel_id=1, source_target_pairs={{0,1},{1,0},{2,3},{3,2},{4,5},{5,4},{6,7},{7,6},{8,9},{9,8},{10,11... | collective-permute-start | bytes 466952 | tf_op jit(solution)/shard_map/ppermute | solution.py:43
  432.6 16.3 %collective-permute-start.25 = (bf16[128,2048]{1,0:T(8,128)(2,1)S(1)}, bf16[128,2048]{1,0:T(8,128)(2,1)S(1)}, u32[]{:S(2)}, u32[]{:S(2)}) collective-permute-start(bf16[128,2048]{1,0:T(8,128)(2,1)S(1)} %convert_element_type.200), channel_id=1, source_target_pairs={{1,16},{9,24},{16,1},{24,9},{3,18},{11,26},{18,3},{26,11},{5,20},{... | collective-permute-start | bytes 1572872 | tf_op jit(solution)/shard_map/ppermute | solution.py:802
  438.3 11.6 %collective-permute-start.24 = (bf16[4,64,1024]{2,1,0:T(8,128)(2,1)S(1)}, bf16[4,64,1024]{2,1,0:T(8,128)(2,1)}, u32[]{:S(2)}, u32[]{:S(2)}) collective-permute-start(bf16[4,64,1024]{2,1,0:T(8,128)(2,1)S(1)} %dynamic-slice_bitcast_fusion.1), channel_id=1, source_target_pairs={{0,1},{1,0},{2,3},{3,2},{4,5},{5,4},{6,7},{7,6},{8,9},{9,8},{10,11... | collective-permute-start | bytes 1572872 | tf_op jit(solution)/shard_map/ppermute | solution.py:43
  (51 other events, 496.3 us)
Sparse Core Ops, SparseCore 0:
  9.6 84.5 all-gather.5
  96.7 59.7 all-gather.3

commit v4 on v3

--- a/solution.py
+++ b/solution.py
@@ -375,6 +375,9 @@
             out_specs=pl.BlockSpec((half_model, wide), lambda n, core: (0, n)),
         ),
         out_shape=shape(half_model, half, dtype=bf16),
+        cost_estimate=pl.CostEstimate(
+            flops=int(5 * 1.15e9), bytes_accessed=4 * half_model * half, transcendentals=0
+        ),
         name="columns",
     )(core, in_weight)
 
@@ -775,13 +778,18 @@
     return got
 
 
-def line_step(partial, bit, axis="outer"):
+def line_trade(partial, bit, axis="outer"):
     count = lax.axis_size(axis)
     mine = (lax.axis_index(axis) // bit) % 2
     split = partial.reshape((-1, 2) + partial.shape[1:])
     sent = lax.dynamic_index_in_dim(split, 1 - mine, 1, keepdims=False).astype(bf16)
     kept = lax.dynamic_index_in_dim(split, mine, 1, keepdims=False)
     got = lax.ppermute(sent, axis, [(o, o ^ bit) for o in range(count)])
+    return kept, got
+
+
+def line_step(partial, bit, axis="outer"):
+    kept, got = line_trade(partial, bit, axis)
     return kept + got.astype(f32)
 
 
@@ -943,9 +951,9 @@
     gate_partial, branch_all, *first_part = together(
         in_weight_partial(early_all), branch_all, *first_part
     )
-    gate_mid = line_step(gate_partial, 1)
+    gate_kept, gate_got_sum = line_trade(gate_partial, 1)
     d_logits, d_selected, d_base, bias_term = run_backward(1, tuple(first_part), *operands)
-    d_selected, gate_mid = together(d_selected, gate_mid)
+    d_selected, gate_got_sum = together(d_selected, gate_got_sum)
     d_logits = d_logits.reshape(rows, half)
     d_selected = d_selected.reshape(rows, -1)
     d_selected = d_selected + swap(d_selected)
@@ -957,7 +965,8 @@
     split, early = together(split, early)
     inner_all = lax.all_to_all(split, "member", 0, 0).reshape(group * rows, width)
     kept, sent = run_normed(core_index, split, early, in_weight, inner_got, gate_got, 10)
-    gate_part = line_reduce(gate_mid, 2)
+    split, gate_got_sum = together(split, gate_got_sum)
+    gate_part = line_reduce(gate_kept + gate_got_sum.astype(f32), 2)
     inner_all, gate_part, kept, sent = together(inner_all, gate_part, kept, sent)
     inner_partial, branch_all, branch = together(in_weight_partial(inner_all), branch_all, branch)
     out_partial = matmul_tn(branch_all, cot_all).reshape(group, -1, model)
@@ -994,12 +1003,13 @@
     )
 
     inner_mid = line_step(inner_partial, 1)
+    out_kept, out_got = line_trade(out_partial, 1, "member")
+    pack, out_got = together(pack, out_got)
+    out_mid = out_kept + out_got.astype(f32)
     pack_all = lax.all_to_all(pack, "member", 0, 0)
-    out_mid = line_step(out_partial, 1, "member")
-    inner_mid, out_mid = together(inner_mid, out_mid)
     inner_part = line_reduce(inner_mid, 2)
     out_total = line_reduce(out_mid, 2, "member")
-    inner_part, out_total, pack_all = together(inner_part, out_total, pack_all)
+    inner_part, pack_all = together(inner_part, pack_all)
     pack_own = owner_part(owner_sum(jnp.sum(pack_all.astype(f32), axis=0)), 1).T
     out_grad = to_owner(out_total)
     in_grad = in_weight_rows(inner_part.astype(bf16), gate_part.astype(bf16))

time: 465 us -> 449 us (0.966)
  waiting for transfers between devices: 70.6 us -> 57.1 us
  local copies, waits for them, and re-layouts: 35.8 us -> 28.7 us
    ppermute x1, waiting for transfers between devices: 7.91 us -> 0.01 us  [to_owner(): got = lax.ppermute(rows.astype(bf16), ('outer', 'fsdp'), pairs).astype(f32)]
    add x3 -> x1, other arithmetic: 7.94 us -> 1.65 us  [line_step(): return kept + got.astype(f32)]
    unnamed x114 -> x112, local copies, waits for them, and re-layouts: 12.6 us -> 12.2 us
  transfers between devices with their start and end apart: 34 -> 34, of which waited for: 14 -> 11; matrix products, arithmetic and copies ran while one was open for 17% -> 17% of each run, Pallas kernels for 42% -> 44%
where the time goes in v4:
time: 449 us; the launch traced here: 443 us
  Pallas kernels  199 us (44%)
  starting transfers between devices  64.8 us (14%)
  waiting for transfers between devices  57.1 us (13%)
  other arithmetic  46.6 us (10%)
  matrix products  31.4 us (7%)
  local copies, waits for them, and re-layouts  28.7 us (6%)
  between operations  15.5 us (3%)
    pallas_call x3, Pallas kernels, per_sequence(): pl.pallas_call(kernel, grid=(sequences,), in_specs=[(in_specs or {}).get(...  70.7 us
    pallas_call x2, Pallas kernels, run_backward(): pl.pallas_call(kernel, grid=(1,), in_specs=[pl.BlockSpec(memory_space=pl....  70.4 us
    ppermute x7, waiting for transfers between devices, line_trade(): got = lax.ppermute(sent, axis, [(o, o ^ bit) for o in range(count)])  26.8 us
    dot_general x3, matrix products, matmul_tn(): lax.dot_general(left, right, (((0,), (0,)), ((), ())), preferred_element_...  24.3 us
    pallas_call x1, Pallas kernels, run_normed(): pl.pallas_call(normed_kernel, grid_spec=pltpu.PrefetchScalarGridSpec(num_...  16.7 us
    pallas_call x2, Pallas kernels, run_product(): pl.pallas_call(functools.partial(whole_kernel, transposed), grid=(columns...  14.5 us
    pallas_call x2, Pallas kernels, run_project(): pl.pallas_call(project_kernel, grid_spec=pltpu.PrefetchScalarGridSpec(num...  14.4 us
    ppermute x12, starting transfers between devices, swap(): return lax.ppermute(value, 'fsdp', [(0, 1), (1, 0)])  12.3 us
  transfers between devices with their start and end apart: 34, of which 11 were waited for; matrix products, arithmetic and copies ran while one was open for 17% of the time, Pallas kernels for 44%

profile of v4, /device:TPU:1, one launch (start us, length us, event | category | flops | bytes accessed | tf_op | source)
XLA Modules:
  0.0 443.3 jit_solution(10048212369894416120)
XLA Ops:
  11.7 4.9 %columns.2 = bf16[1024,2048]{1,0:T(8,128)(2,1)} custom-call(s32[1]{0:T(128)} %bitcast.2.core_ref, bf16[1024,8192]{1,0:T(8,128)(2,1)} %gate_own.1), custom_call_target="tpu_custom_call" | custom-call | flops 5750000128 | bytes 8388608 | tf_op jit(solution)/shard_map/columns/pallas_call | solution.py:365
  17.7 5.1 %columns.3 = bf16[1024,2048]{1,0:T(8,128)(2,1)} custom-call(s32[1]{0:T(128)} %bitcast.2.core_ref, bf16[1024,8192]{1,0:T(8,128)(2,1)} %gate_own.1), custom_call_target="tpu_custom_call" | custom-call | flops 5750000128 | bytes 8388608 | tf_op jit(solution)/shard_map/columns/pallas_call | solution.py:365
  32.7 7.1 %project.2 = bf16[512,2048]{1,0:T(8,128)(2,1)S(1)} custom-call(s32[1]{0:T(128)} %bitcast.2.core_ref, bf16[512,2048]{1,0:T(8,128)(2,1)S(1)} %fusion.2.x_ref, bf16[1024,8192]{1,0:T(8,128)(2,1)} %gate_own.1, bf16[1024,2048]{1,0:T(8,128)(2,1)} %collective-permute-done.2.got_ref.inner_got), custom_call_target="tpu_custom_call" | custom-call | flops 5750000128 | bytes 8388608 | tf_op jit(solution)/shard_map/project/pallas_call | solution.py:428
  39.8 5.0 %collective-permute-start.3 = (bf16[2,3,2048]{2,1,0:T(4,128)(2,1)S(1)}, bf16[2,3,2048]{2,1,0:T(4,128)(2,1)S(1)}, u32[]{:S(2)}, u32[]{:S(2)}) collective-permute-start(bf16[2,3,2048]{2,1,0:T(4,128)(2,1)S(1)} %slice.146), channel_id=1, source_target_pairs={{0,2},{2,4},{4,6},{6,8},{8,10},{10,12},{12,14},{14,16},{16,18},{18... | collective-permute-start | bytes 73736 | tf_op jit(solution)/shard_map/ppermute | solution.py:769
  44.8 7.3 %product.2 = f32[512,2048]{1,0:T(8,128)S(1)} custom-call(bf16[512,2048]{1,0:T(8,128)(2,1)S(1)} %pad_maximum_fusion.2.left_ref, bf16[2048,2048]{1,0:T(8,128)(2,1)} %right_ref.3), custom_call_target="tpu_custom_call" | custom-call | flops 5750000128 | bytes 1048576 | tf_op jit(solution)/shard_map/product/pallas_call | solution.py:399
  52.2 4.4 multiply_convert_fusion
  61.6 7.3 %project.3 = bf16[512,2048]{1,0:T(8,128)(2,1)S(1)} custom-call(s32[1]{0:T(128)} %bitcast.2.core_ref, bf16[512,2048]{1,0:T(8,128)(2,1)S(1)} %fusion.2.x_ref, bf16[1024,8192]{1,0:T(8,128)(2,1)} %gate_own.1, bf16[1024,2048]{1,0:T(8,128)(2,1)S(1)} %collective-permute-done.5.got_ref.gate_got), custom_call_target="tpu_custom_call" | custom-call | flops 5750000128 | bytes 8388608 | tf_op jit(solution)/shard_map/project/pallas_call | solution.py:428
  71.5 35.9 %summary.1 = (f32[2,256,2048]{2,1,0:T(8,128)}, f32[2,256,2048]{2,1,0:T(8,128)}, f32[2,256,2048]{2,1,0:T(8,128)}, bf16[16,3,32,128]{3,2,1,0:T(8,128)(2,1)}) custom-call(f32[2,256,160]{2,1,0:T(8,128)} %copy.54.sel_ref.refs_0_.refs_4_, bf16[2,256,2048]{2,1,0:T(8,128)(2,1)} %get-tuple-element.151.act_ref.refs_4_.refs_8_, bf16[2,256,2048]{2,1,0:T(8,128)(2,1)} %bitcast.246, ...), custom_call_target="tpu_custom_call" | custom-call | flops 28750000128 | bytes 22224896 | tf_op jit(solution)/shard_map/summary/pallas_call | solution.py:584
  107.4 6.0 %all-to-all-start = ((bf16[16,3,32,128]{3,2,1,0:T(8,128)(2,1)}), bf16[16,3,32,128]{3,2,1,0:T(8,128)(2,1)S(1)}, u32[]{:S(2)}, u32[]{:S(2)}) async-start(bf16[16,3,32,128]{3,2,1,0:T(8,128)(2,1)} %get-tuple-element.63), calls=%async_computation | async-start | bytes 786432 | tf_op jit(solution)/shard_map/all_to_all | solution.py:751
  113.4 10.8 %all-to-all-done.pieces_ref = bf16[16,3,32,128]{3,2,1,0:T(8,128)(2,1)S(1)} async-done(((bf16[16,3,32,128]{3,2,1,0:T(8,128)(2,1)}), bf16[16,3,32,128]{3,2,1,0:T(8,128)(2,1)S(1)}, u32[]{:S(2)}, u32[]{:S(2)}) %all-to-all-start) | async-done | bytes 393248 | tf_op jit(solution)/shard_map/all_to_all | solution.py:751
  126.8 5.4 %all-to-all-start.1 = ((bf16[16,2,32,128]{3,2,1,0:T(8,128)(2,1)}), bf16[16,2,32,128]{3,2,1,0:T(8,128)(2,1)S(1)}, u32[]{:S(2)}, u32[]{:S(2)}) async-start(bf16[16,2,32,128]{3,2,1,0:T(8,128)(2,1)} %chain.1), calls=%async_computation.1 | async-start | bytes 524288 | tf_op jit(solution)/shard_map/all_to_all | solution.py:760
  134.3 5.5 %all-to-all-done.1.init_ref.refs_6_.refs_10_ = bf16[16,2,32,128]{3,2,1,0:T(8,128)(2,1)S(1)} async-done(((bf16[16,2,32,128]{3,2,1,0:T(8,128)(2,1)}), bf16[16,2,32,128]{3,2,1,0:T(8,128)(2,1)S(1)}, u32[]{:S(2)}, u32[]{:S(2)}) %all-to-all-start.1) | async-done | bytes 262176 | tf_op jit(solution)/shard_map/all_to_all | solution.py:760
  140.5 29.7 %forward.1 = (bf16[4,512,512]{2,1,0:T(8,128)(2,1)}, bf16[4,512,512]{2,1,0:T(8,128)(2,1)}, bf16[2,256,2048]{2,1,0:T(8,128)(2,1)}, f32[2,16,16,2048]{3,2,1,0:T(8,128)}, f32[2,1,2048]{2,1,0:T(1,128)}) custom-call(f32[2,256,160]{2,1,0:T(8,128)} %copy.54.sel_ref.refs_0_.refs_4_, f32[2,256,2048]{2,1,0:T(8,128)} %get-tuple-element.61.r_ref.refs_1_.refs_5_, ...), custom_call_target="tpu_custom_call" | custom-call | flops 23000000512 | bytes 28139520 | tf_op jit(solution)/shard_map/forward/pallas_call | solution.py:584
  170.3 4.6 %all-to-all-start.2 = ((bf16[4,512,512]{2,1,0:T(8,128)(2,1)}), bf16[4,512,512]{2,1,0:T(8,128)(2,1)}, u32[]{:S(2)}, u32[]{:S(2)}) async-start(bf16[4,512,512]{2,1,0:T(8,128)(2,1)} %get-tuple-element.75), calls=%async_computation.2 | async-start | bytes 4194304 | tf_op jit(solution)/shard_map/all_to_all | solution.py:918
  177.9 35.1 %backward.2 = (bf16[2,256,2048]{2,1,0:T(8,128)(2,1)}, f32[2,256,160]{2,1,0:T(8,128)}, f32[2,256,2048]{2,1,0:T(8,128)}, f32[2,1,2048]{2,1,0:T(1,128)}) custom-call(f32[2,256,160]{2,1,0:T(8,128)} %copy.54.sel_ref.refs_0_.refs_4_, f32[2,256,2048]{2,1,0:T(8,128)} %get-tuple-element.61.r_ref.refs_1_.refs_5_, ...), custom_call_target="tpu_custom_call" | custom-call | flops 39099998208 | bytes 13180928 | tf_op jit(solution)/shard_map/backward/pallas_call | solution.py:692
  213.4 9.8 %fusion.32 = f32[2048,512]{1,0:T(8,128)} fusion(bf16[2048,2048]{1,0:T(8,128)(2,1)} %all-gather.4.cloned.1.call-done, bf16[512,512]{1,0:T(8,128)(2,1)S(1)} %get-tuple-element.154, bf16[512,512]{1,0:T(8,128)(2,1)S(1)} %get-tuple-element.155, bf16[512,512]{1,0:T(8,128)(2,1)S(1)} %get-tuple-element.156, bf16[512,512]{1,0:T(8,128)(2,1)S(1)} %get-tuple-element.153), kind=kOutput, calls=%fused_computation.56 | convolution fusion | flops 4303355904 | bytes 14680064 | tf_op jit(solution)/shard_map/dot_general | solution.py:30
  226.4 35.3 %backward.3 = (bf16[2,256,2048]{2,1,0:T(8,128)(2,1)}, f32[2,256,160]{2,1,0:T(8,128)}, f32[2,256,2048]{2,1,0:T(8,128)}, f32[2,1,2048]{2,1,0:T(1,128)}) custom-call(bf16[2,256,2048]{2,1,0:T(8,128)(2,1)} %get-tuple-element.80.refs_0_, ...), custom_call_target="tpu_custom_call", output_to_operand_aliasing={{0}: (0, {}), {1}: (1, {}), {2}: (2, {}), {3}: (3, {})} | custom-call | flops 39099998208 | bytes 13180928 | tf_op jit(solution)/shard_map/backward/pallas_call | solution.py:692
  263.9 4.8 %collective-permute-start.11 = (f32[512,160]{0,1:T(8,128)S(1)}, f32[512,160]{0,1:T(8,128)}, u32[]{:S(2)}, u32[]{:S(2)}) collective-permute-start(f32[512,160]{0,1:T(8,128)S(1)} %copy.64), channel_id=1, source_target_pairs={{0,1},{1,0},{2,3},{3,2},{4,5},{5,4},{6,7},{7,6},{8,9},{9,8},{10,11... | collective-permute-start | bytes 983048 | tf_op jit(solution)/shard_map/ppermute | solution.py:43
  272.2 6.2 %fusion.9 = (f32[2048]{0:T(1024)S(1)}, f32[2048]{0:T(1024)S(1)}, f32[2048]{0:T(1024)S(1)}, f32[512,2048]{1,0:T(8,128)S(1)}) fusion(bf16[2,256,2048]{2,1,0:T(8,128)(2,1)S(1)} %bitcast.242, bf16[2,3,2048]{2,1,0:T(4,128)(2,1)S(1)} %copy-done.41, f32[2,256,2048]{2,1,0:T(8,128)} %copy-done.18, bf16[512,160]{0,1:T(8,128)(2,1)S(1)} %add_convert_fusion, ...), kind=kOutput, calls=%fused_computation.17 | convolution fusion | flops 363849728 | bytes 15548416 | tf_op jit(solution)/shard_map/dot_general | solution.py:26
  284.7 5.1 %correlate.1.inner_ref = bf16[4,512,512]{2,1,0:T(8,128)(2,1)} custom-call(f32[2,256,2048]{2,1,0:T(8,128)} %bitcast.255, f32[2,8,2048]{2,1,0:T(8,128)} %pad.12.later_ref, f32[4,2048]{1,0:T(4,128)} %convert_bitcast_fusion.w_ref), custom_call_target="tpu_custom_call" | custom-call | flops 4600000000 | bytes 6455296 | tf_op jit(solution)/shard_map/correlate/pallas_call | solution.py:584
  298.4 16.7 %normed.1 = (f32[256,2048]{1,0:T(8,128)S(1)}, f32[256,2048]{1,0:T(8,128)}) custom-call(s32[1]{0:T(128)} %bitcast.2.core_ref, bf16[4,512,512]{2,1,0:T(8,128)(2,1)} %correlate.1.inner_ref, bf16[4,512,512]{2,1,0:T(8,128)(2,1)} %get-tuple-element.91.gate_ref, bf16[1024,8192]{1,0:T(8,128)(2,1)} %gate_own.1, bf16[1024,8192]{1,0:T(8,128)(2,1)} %gate_own.1, ...), custom_call_target="tpu_custom_call" | custom-call | flops 11500000256 | bytes 1048576 | tf_op jit(solution)/shard_map/normed/pallas_call | solution.py:506
  316.3 5.5 %collective-permute-done.13 = bf16[1,512,512]{2,1,0:T(8,128)(2,1)S(1)} collective-permute-done((bf16[1,512,512]{2,1,0:T(8,128)(2,1)S(1)}, bf16[1,512,512]{2,1,0:T(8,128)(2,1)S(1)}, u32[]{:S(2)}, u32[]{:S(2)}) %collective-permute-start.13) | collective-permute-done | bytes 524320 | tf_op jit(solution)/shard_map/ppermute | solution.py:787
  322.8 6.9 %fusion.69 = f32[2048,512]{1,0:T(8,128)S(1)} fusion(bf16[2048,2048]{1,0:T(8,128)(2,1)} %all-gather.4.cloned.1.call-done, bf16[2048,512]{1,0:T(8,128)(2,1)S(1)} %bitcast.263), kind=kOutput, calls=%fused_computation.169 | convolution fusion | flops 4294967296 | bytes 14680064 | tf_op jit(solution)/shard_map/dot_general | solution.py:30
  331.0 7.6 %fusion.70 = f32[512,2048]{1,0:T(8,128)S(1)} fusion(bf16[2048,512]{1,0:T(8,128)(2,1)} %bitcast.29, bf16[2048,2048]{1,0:T(8,128)(2,1)} %bitcast.291), kind=kOutput, calls=%fused_computation.170 | convolution fusion | flops 4294967296 | bytes 14680064 | tf_op jit(solution)/shard_map/dot_general | solution.py:30
  341.3 7.2 %product.3 = f32[512,2048]{1,0:T(8,128)S(1)} custom-call(bf16[512,2048]{1,0:T(8,128)(2,1)S(1)} %bitcast.251, bf16[2048,2048]{1,0:T(8,128)(2,1)} %right_ref.3), custom_call_target="tpu_custom_call" | custom-call | flops 5750000128 | bytes 1048576 | tf_op jit(solution)/shard_map/product/pallas_call | solution.py:399
  364.8 4.3 all-to-all-start.4
  373.9 12.9 %collective-permute-done.17 = bf16[1,512,512]{2,1,0:T(8,128)(2,1)} collective-permute-done((bf16[1,512,512]{2,1,0:T(8,128)(2,1)}, bf16[1,512,512]{2,1,0:T(8,128)(2,1)}, u32[]{:S(2)}, u32[]{:S(2)}) %collective-permute-start.17) | collective-permute-done | bytes 524320 | tf_op jit(solution)/shard_map/ppermute | solution.py:787
  390.7 5.0 %collective-permute-done.24 = bf16[1,128,2048]{2,1,0:T(8,128)(2,1)} collective-permute-done((bf16[1,128,2048]{2,1,0:T(8,128)(2,1)}, bf16[1,128,2048]{2,1,0:T(8,128)(2,1)}, u32[]{:S(2)}, u32[]{:S(2)}) %collective-permute-start.24) | collective-permute-done | bytes 524320 | tf_op jit(solution)/shard_map/ppermute | solution.py:787
  398.0 5.7 %collective-permute-start.25 = (bf16[128,2048]{1,0:T(8,128)(2,1)}, bf16[128,2048]{1,0:T(8,128)(2,1)}, u32[]{:S(2)}, u32[]{:S(2)}) collective-permute-start(bf16[128,2048]{1,0:T(8,128)(2,1)} %bitcast_convert_fusion.3), channel_id=1, source_target_pairs={{1,16},{9,24},{16,1},{24,9},{3,18},{11,26},{18,3},{26,11},{5,20},{... | collective-permute-start | bytes 1572872 | tf_op jit(solution)/shard_map/ppermute | solution.py:810
  406.8 6.0 %fusion.28 = (f32[1,256,2048]{2,1,0:T(8,128)}, bf16[1,256,2048]{2,1,0:T(8,128)(2,1)}) fusion(f32[256]{0:T(256)S(1)} %broadcast_multiply_fusion, f32[2048]{0:T(1024)S(1)} %copy-done.37, f32[256]{0:T(256)S(1)} %copy-done.43, bf16[1,256,2048]{2,1,0:T(8,128)(2,1)S(1)} %copy-done.22, bf16[1,256,2048]{2,1,0:T(8,128)(2,1)S(1)} %copy-done.17, ...), kind=kLoop, calls=%fused_computation.48 | loop fusion | flops 6291456 | bytes 13641732 | tf_op jit(solution)/shard_map/broadcast_in_dim | solution.py:1028
  413.9 4.4 all-to-all-start.5
  424.6 4.6 %all-to-all-done.5 = bf16[4,128,1024]{2,1,0:T(8,128)(2,1)} async-done(((bf16[4,128,1024]{2,1,0:T(8,128)(2,1)}), bf16[4,128,1024]{2,1,0:T(8,128)(2,1)}, u32[]{:S(2)}, u32[]{:S(2)}) %all-to-all-start.5) | async-done | bytes 1048608 | tf_op jit(solution)/shard_map/all_to_all | solution.py:928
  (252 shorter events, 105.7 us)
Async XLA Ops:
  7.2 163.0 %all-gather.6.cloned.1.call-start = ((), (), s32[]{:S(2)}) async-start(), calls=%async_computation.7 | async-start | bytes 9437184 | tf_op jit(solution)/shard_map/all_gather | solution.py:882
  7.9 162.3 %all-gather.4.cloned.1.call-start = ((), (), s32[]{:S(2)}) async-start(), calls=%async_computation.6 | async-start | bytes 9437184 | tf_op jit(solution)/shard_map/all_gather | solution.py:881
  16.6 16.0 %collective-permute-start.2 = (bf16[1024,2048]{1,0:T(8,128)(2,1)}, bf16[1024,2048]{1,0:T(8,128)(2,1)}, u32[]{:S(2)}, u32[]{:S(2)}) collective-permute-start(bf16[1024,2048]{1,0:T(8,128)(2,1)} %columns.2), channel_id=1, source_target_pairs={{0,1},{1,0},{2,3},{3,2},{4,5},{5,4},{6,7},{7,6},{8,9},{9,8},{10,11... | collective-permute-start | bytes 12582920 | tf_op jit(solution)/shard_map/ppermute | solution.py:43
  17.1 8.4 %collective-permute-start = (bf16[256,2048]{1,0:T(8,128)(2,1)S(1)}, bf16[256,2048]{1,0:T(8,128)(2,1)}, u32[]{:S(2)}, u32[]{:S(2)}) collective-permute-start(bf16[256,2048]{1,0:T(8,128)(2,1)S(1)} %bitcast.252), channel_id=1, source_target_pairs={{0,1},{1,0},{2,3},{3,2},{4,5},{5,4},{6,7},{7,6},{8,9},{9,8},{10,11... | collective-permute-start | bytes 3145736 | tf_op jit(solution)/shard_map/ppermute | solution.py:43
  17.1 12.8 %collective-permute-start.6 = (bf16[256,2048]{1,0:T(8,128)(2,1)S(1)}, bf16[256,2048]{1,0:T(8,128)(2,1)}, u32[]{:S(2)}, u32[]{:S(2)}) collective-permute-start(bf16[256,2048]{1,0:T(8,128)(2,1)S(1)} %bitcast.253), channel_id=1, source_target_pairs={{0,1},{1,0},{2,3},{3,2},{4,5},{5,4},{6,7},{7,6},{8,9},{9,8},{10,11... | collective-permute-start | bytes 3145736 | tf_op jit(solution)/shard_map/ppermute | solution.py:43
  22.7 38.9 %collective-permute-start.5 = (bf16[1024,2048]{1,0:T(8,128)(2,1)}, bf16[1024,2048]{1,0:T(8,128)(2,1)S(1)}, u32[]{:S(2)}, u32[]{:S(2)}) collective-permute-start(bf16[1024,2048]{1,0:T(8,128)(2,1)} %columns.3), channel_id=1, source_target_pairs={{0,1},{1,0},{2,3},{3,2},{4,5},{5,4},{6,7},{7,6},{8,9},{9,8},{10,11... | collective-permute-start | bytes 12582920 | tf_op jit(solution)/shard_map/ppermute | solution.py:43
  39.8 12.4 %collective-permute-start.3 = (bf16[2,3,2048]{2,1,0:T(4,128)(2,1)S(1)}, bf16[2,3,2048]{2,1,0:T(4,128)(2,1)S(1)}, u32[]{:S(2)}, u32[]{:S(2)}) collective-permute-start(bf16[2,3,2048]{2,1,0:T(4,128)(2,1)S(1)} %slice.146), channel_id=1, source_target_pairs={{0,2},{2,4},{4,6},{6,8},{8,10},{10,12},{12,14},{14,16},{16,18},{18... | collective-permute-start | bytes 73736 | tf_op jit(solution)/shard_map/ppermute | solution.py:769
  60.9 9.3 %collective-permute-start.4 = (f32[512,160]{0,1:T(8,128)S(1)}, f32[512,160]{0,1:T(8,128)S(1)}, u32[]{:S(2)}, u32[]{:S(2)}) collective-permute-start(f32[512,160]{0,1:T(8,128)S(1)} %fusion.68), channel_id=1, source_target_pairs={{0,1},{1,0},{2,3},{3,2},{4,5},{5,4},{6,7},{7,6},{8,9},{9,8},{10,11... | collective-permute-start | bytes 983048 | tf_op jit(solution)/shard_map/ppermute | solution.py:43
  107.4 16.9 %all-to-all-start = ((bf16[16,3,32,128]{3,2,1,0:T(8,128)(2,1)}), bf16[16,3,32,128]{3,2,1,0:T(8,128)(2,1)S(1)}, u32[]{:S(2)}, u32[]{:S(2)}) async-start(bf16[16,3,32,128]{3,2,1,0:T(8,128)(2,1)} %get-tuple-element.63), calls=%async_computation | async-start | bytes 786432 | tf_op jit(solution)/shard_map/all_to_all | solution.py:751
  126.8 13.0 %all-to-all-start.1 = ((bf16[16,2,32,128]{3,2,1,0:T(8,128)(2,1)}), bf16[16,2,32,128]{3,2,1,0:T(8,128)(2,1)S(1)}, u32[]{:S(2)}, u32[]{:S(2)}) async-start(bf16[16,2,32,128]{3,2,1,0:T(8,128)(2,1)} %chain.1), calls=%async_computation.1 | async-start | bytes 524288 | tf_op jit(solution)/shard_map/all_to_all | solution.py:760
  170.3 52.9 %all-to-all-start.2 = ((bf16[4,512,512]{2,1,0:T(8,128)(2,1)}), bf16[4,512,512]{2,1,0:T(8,128)(2,1)}, u32[]{:S(2)}, u32[]{:S(2)}) async-start(bf16[4,512,512]{2,1,0:T(8,128)(2,1)} %get-tuple-element.75), calls=%async_computation.2 | async-start | bytes 4194304 | tf_op jit(solution)/shard_map/all_to_all | solution.py:918
  175.1 37.8 %collective-permute-start.9 = (bf16[512,512]{1,0:T(8,128)(2,1)S(1)}, bf16[512,512]{1,0:T(8,128)(2,1)S(1)}, u32[]{:S(2)}, u32[]{:S(2)}) collective-permute-start(bf16[512,512]{1,0:T(8,128)(2,1)S(1)} %get-tuple-element.157), channel_id=1, source_target_pairs={{0,6},{2,4},{4,2},{6,0},{1,7},{3,5},{5,3},{7,1},{8,14},{10,12},{12... | collective-permute-start | bytes 1572872 | tf_op jit(solution)/shard_map/ppermute | solution.py:777
  176.0 36.9 %collective-permute-start.8 = (bf16[512,512]{1,0:T(8,128)(2,1)S(1)}, bf16[512,512]{1,0:T(8,128)(2,1)S(1)}, u32[]{:S(2)}, u32[]{:S(2)}) collective-permute-start(bf16[512,512]{1,0:T(8,128)(2,1)S(1)} %get-tuple-element.158), channel_id=1, source_target_pairs={{0,4},{2,6},{4,0},{6,2},{1,5},{3,7},{5,1},{7,3},{8,12},{10,14},{12... | collective-permute-start | bytes 1572872 | tf_op jit(solution)/shard_map/ppermute | solution.py:777
  177.4 35.6 %collective-permute-start.7 = (bf16[512,512]{1,0:T(8,128)(2,1)S(1)}, bf16[512,512]{1,0:T(8,128)(2,1)S(1)}, u32[]{:S(2)}, u32[]{:S(2)}) collective-permute-start(bf16[512,512]{1,0:T(8,128)(2,1)S(1)} %get-tuple-element.159), channel_id=1, source_target_pairs={{0,2},{2,0},{4,6},{6,4},{1,3},{3,1},{5,7},{7,5},{8,10},{10,8},{12,... | collective-permute-start | bytes 1572872 | tf_op jit(solution)/shard_map/ppermute | solution.py:777
  224.9 36.8 %collective-permute-start.10 = (bf16[2,512,512]{2,1,0:T(8,128)(2,1)S(1)}, bf16[2,512,512]{2,1,0:T(8,128)(2,1)S(1)}, u32[]{:S(2)}, u32[]{:S(2)}) collective-permute-start(bf16[2,512,512]{2,1,0:T(8,128)(2,1)S(1)} %fusion.40), channel_id=1, source_target_pairs={{0,8},{8,0},{16,24},{24,16},{1,9},{9,1},{17,25},{25,17},{2,10},{10... | collective-permute-start | bytes 3145736 | tf_op jit(solution)/shard_map/ppermute | solution.py:787
  263.9 7.2 %collective-permute-start.11 = (f32[512,160]{0,1:T(8,128)S(1)}, f32[512,160]{0,1:T(8,128)}, u32[]{:S(2)}, u32[]{:S(2)}) collective-permute-start(f32[512,160]{0,1:T(8,128)S(1)} %copy.64), channel_id=1, source_target_pairs={{0,1},{1,0},{2,3},{3,2},{4,5},{5,4},{6,7},{7,6},{8,9},{9,8},{10,11... | collective-permute-start | bytes 983048 | tf_op jit(solution)/shard_map/ppermute | solution.py:43
  278.5 5.6 %collective-permute-start.12 = (f32[2,3,2048]{2,1,0:T(4,128)S(1)}, f32[2,3,2048]{2,1,0:T(4,128)S(1)}, u32[]{:S(2)}, u32[]{:S(2)}) collective-permute-start(f32[2,3,2048]{2,1,0:T(4,128)S(1)} %slice.156), channel_id=1, source_target_pairs={{2,0},{4,2},{6,4},{8,6},{10,8},{12,10},{14,12},{16,14},{18,16},{20... | collective-permute-start | bytes 147464 | tf_op jit(solution)/shard_map/ppermute | solution.py:769
  289.8 33.0 %all-to-all-start.3 = ((bf16[4,512,512]{2,1,0:T(8,128)(2,1)}), bf16[4,512,512]{2,1,0:T(8,128)(2,1)S(1)}, u32[]{:S(2)}, u32[]{:S(2)}) async-start(bf16[4,512,512]{2,1,0:T(8,128)(2,1)} %correlate.1.inner_ref), calls=%async_computation.3 | async-start | bytes 4194304 | tf_op jit(solution)/shard_map/all_to_all | solution.py:966
  296.2 25.6 %collective-permute-start.13 = (bf16[1,512,512]{2,1,0:T(8,128)(2,1)S(1)}, bf16[1,512,512]{2,1,0:T(8,128)(2,1)S(1)}, u32[]{:S(2)}, u32[]{:S(2)}) collective-permute-start(bf16[1,512,512]{2,1,0:T(8,128)(2,1)S(1)} %dynamic-slice_convert_fusion.2), channel_id=1, source_target_pairs={{0,16},{8,24},{16,0},{24,8},{1,17},{9,25},{17,1},{25,9},{2,18},{10... | collective-permute-start | bytes 1572872 | tf_op jit(solution)/shard_map/ppermute | solution.py:787
  329.9 23.9 %collective-permute-start.16 = (bf16[2,512,512]{2,1,0:T(8,128)(2,1)S(1)}, bf16[2,512,512]{2,1,0:T(8,128)(2,1)S(1)}, u32[]{:S(2)}, u32[]{:S(2)}) collective-permute-start(bf16[2,512,512]{2,1,0:T(8,128)(2,1)S(1)} %fusion.41), channel_id=1, source_target_pairs={{0,8},{8,0},{16,24},{24,16},{1,9},{9,1},{17,25},{25,17},{2,10},{10... | collective-permute-start | bytes 3145736 | tf_op jit(solution)/shard_map/ppermute | solution.py:787
  330.0 25.5 %collective-permute-start.15 = (f32[256,2048]{1,0:T(8,128)}, f32[256,2048]{1,0:T(8,128)S(1)}, u32[]{:S(2)}, u32[]{:S(2)}) collective-permute-start(f32[256,2048]{1,0:T(8,128)} %get-tuple-element.99), channel_id=1, source_target_pairs={{0,1},{1,0},{2,3},{3,2},{4,5},{5,4},{6,7},{7,6},{8,9},{9,8},{10,11... | collective-permute-start | bytes 6291464 | tf_op jit(solution)/shard_map/ppermute | solution.py:43
  339.9 24.9 %collective-permute-start.19 = (bf16[2,128,2048]{2,1,0:T(8,128)(2,1)}, bf16[2,128,2048]{2,1,0:T(8,128)(2,1)}, u32[]{:S(2)}, u32[]{:S(2)}) collective-permute-start(bf16[2,128,2048]{2,1,0:T(8,128)(2,1)} %fusion.42), channel_id=1, source_target_pairs={{0,2},{2,0},{4,6},{6,4},{1,3},{3,1},{5,7},{7,5},{8,10},{10,8},{12,... | collective-permute-start | bytes 3145736 | tf_op jit(solution)/shard_map/ppermute | solution.py:787
  350.4 56.4 %collective-permute-start.14 = (f32[256,2048]{1,0:T(8,128)}, f32[256,2048]{1,0:T(8,128)}, u32[]{:S(2)}, u32[]{:S(2)}) collective-permute-start(f32[256,2048]{1,0:T(8,128)} %dynamic-slice_bitcast_fusion), channel_id=1, source_target_pairs={{0,1},{1,0},{2,3},{3,2},{4,5},{5,4},{6,7},{7,6},{8,9},{9,8},{10,11... | collective-permute-start | bytes 6291464 | tf_op jit(solution)/shard_map/ppermute | solution.py:43
  356.9 3.9 collective-permute-start.18
  360.7 26.1 %collective-permute-start.17 = (bf16[1,512,512]{2,1,0:T(8,128)(2,1)}, bf16[1,512,512]{2,1,0:T(8,128)(2,1)}, u32[]{:S(2)}, u32[]{:S(2)}) collective-permute-start(bf16[1,512,512]{2,1,0:T(8,128)(2,1)} %dynamic-slice_convert_fusion.1), channel_id=1, source_target_pairs={{0,16},{8,24},{16,0},{24,8},{1,17},{9,25},{17,1},{25,9},{2,18},{10... | collective-permute-start | bytes 1572872 | tf_op jit(solution)/shard_map/ppermute | solution.py:787
  364.8 24.0 %all-to-all-start.4 = ((bf16[4,2,304,256]{3,2,1,0:T(8,128)(2,1)}), bf16[4,2,304,256]{3,2,1,0:T(8,128)(2,1)}, u32[]{:S(2)}, u32[]{:S(2)}) async-start(bf16[4,2,304,256]{3,2,1,0:T(8,128)(2,1)} %copy-done.9), calls=%async_computation.4 | async-start | bytes 2490368 | tf_op jit(solution)/shard_map/all_to_all | solution.py:1009
  372.4 23.3 %collective-permute-start.24 = (bf16[1,128,2048]{2,1,0:T(8,128)(2,1)}, bf16[1,128,2048]{2,1,0:T(8,128)(2,1)}, u32[]{:S(2)}, u32[]{:S(2)}) collective-permute-start(bf16[1,128,2048]{2,1,0:T(8,128)(2,1)} %dynamic-slice_convert_fusion), channel_id=1, source_target_pairs={{0,4},{2,6},{4,0},{6,2},{1,5},{3,7},{5,1},{7,3},{8,12},{10,14},{12... | collective-permute-start | bytes 1572872 | tf_op jit(solution)/shard_map/ppermute | solution.py:787
  390.6 13.1 %collective-permute-start.20 = (bf16[1,304,256]{2,1,0:T(8,128)(2,1)S(1)}, bf16[1,304,256]{2,1,0:T(8,128)(2,1)S(1)}, u32[]{:S(2)}, u32[]{:S(2)}) collective-permute-start(bf16[1,304,256]{2,1,0:T(8,128)(2,1)S(1)} %dynamic-slice_convert_fusion.3), channel_id=1, source_target_pairs={{0,8},{8,0},{16,24},{24,16},{1,9},{9,1},{17,25},{25,17},{2,10},{10... | collective-permute-start | bytes 466952 | tf_op jit(solution)/shard_map/ppermute | solution.py:787
  398.0 24.3 %collective-permute-start.25 = (bf16[128,2048]{1,0:T(8,128)(2,1)}, bf16[128,2048]{1,0:T(8,128)(2,1)}, u32[]{:S(2)}, u32[]{:S(2)}) collective-permute-start(bf16[128,2048]{1,0:T(8,128)(2,1)} %bitcast_convert_fusion.3), channel_id=1, source_target_pairs={{1,16},{9,24},{16,1},{24,9},{3,18},{11,26},{18,3},{26,11},{5,20},{... | collective-permute-start | bytes 1572872 | tf_op jit(solution)/shard_map/ppermute | solution.py:810
  404.4 13.9 %collective-permute-start.21 = (bf16[304,256]{1,0:T(8,128)(2,1)}, bf16[304,256]{1,0:T(8,128)(2,1)}, u32[]{:S(2)}, u32[]{:S(2)}) collective-permute-start(bf16[304,256]{1,0:T(8,128)(2,1)} %bitcast_convert_fusion.4), channel_id=1, source_target_pairs={{1,17},{9,25},{16,0},{24,8},{3,19},{11,27},{18,2},{26,10},{5,21},{... | collective-permute-start | bytes 466952 | tf_op jit(solution)/shard_map/ppermute | solution.py:821
  413.9 15.3 %all-to-all-start.5 = ((bf16[4,128,1024]{2,1,0:T(8,128)(2,1)}), bf16[4,128,1024]{2,1,0:T(8,128)(2,1)}, u32[]{:S(2)}, u32[]{:S(2)}) async-start(bf16[4,128,1024]{2,1,0:T(8,128)(2,1)} %bitcast.256), calls=%async_computation.5 | async-start | bytes 2097152 | tf_op jit(solution)/shard_map/all_to_all | solution.py:928
  420.0 10.4 %collective-permute-start.22 = (f32[304,128]{1,0:T(8,128)S(1)}, f32[304,128]{1,0:T(8,128)S(1)}, u32[]{:S(2)}, u32[]{:S(2)}) collective-permute-start(f32[304,128]{1,0:T(8,128)S(1)} %constant_dynamic-slice_fusion), channel_id=1, source_target_pairs={{0,1},{1,0},{2,3},{3,2},{4,5},{5,4},{6,7},{7,6},{8,9},{9,8},{10,11... | collective-permute-start | bytes 466952 | tf_op jit(solution)/shard_map/ppermute | solution.py:43
  (50 other events, 541.7 us)
Sparse Core Ops, SparseCore 0:
  9.6 84.5 all-gather.5
  96.7 59.6 all-gather.3

commit v5 on v4

--- a/solution.py
+++ b/solution.py
@@ -266,7 +266,7 @@
         eight = index * (span // 8)
         rows = pl.ds(base, span)
         diagonal = kd_ref[0, rows, :]
-        d_query, d_key = None, None
+        d_key = None
         for first in range(0, tiles, narrow):
             places = [(h, j) for j in range(first, first + narrow) for h in group]
             cols = pl.ds(first * lanes, narrow * lanes)
@@ -277,8 +277,7 @@
                 key, square = (halves(ref, base + step, states) for ref in (kb, k2b))
                 advance(rates, feds, key, square, eight, step, current, places)
                 keep(s_hist, step, states, places, current)
-            part = matmul_nt(s_hist[:, cols], d_ref[0, rows, cols].astype(bf16))
-            d_query = part if d_query is None else d_query + part
+        d_query = matmul_nt(s_hist[...], d_ref[0, rows, :].astype(bf16))
         for first in range(0, tiles, narrow):
             places = [(h, j) for j in range(first, first + narrow) for h in group]
             cols = pl.ds(first * lanes, narrow * lanes)

time: 449 us -> 449 us (level)
  no operation moved by 1% of the time
where the time goes in v5:
time: 449 us; the launch traced here: 443 us
  Pallas kernels  199 us (44%)
  starting transfers between devices  64.9 us (14%)
  waiting for transfers between devices  57.1 us (13%)
  other arithmetic  46.6 us (10%)
  matrix products  31.4 us (7%)
  local copies, waits for them, and re-layouts  28.7 us (6%)
  between operations  15.5 us (3%)
    pallas_call x3, Pallas kernels, per_sequence(): pl.pallas_call(kernel, grid=(sequences,), in_specs=[(in_specs or {}).get(...  70.7 us
    pallas_call x2, Pallas kernels, run_backward(): pl.pallas_call(kernel, grid=(1,), in_specs=[pl.BlockSpec(memory_space=pl....  69.9 us
    ppermute x7, waiting for transfers between devices, line_trade(): got = lax.ppermute(sent, axis, [(o, o ^ bit) for o in range(count)])  26.8 us
    dot_general x3, matrix products, matmul_tn(): lax.dot_general(left, right, (((0,), (0,)), ((), ())), preferred_element_...  24.3 us
    pallas_call x1, Pallas kernels, run_normed(): pl.pallas_call(normed_kernel, grid_spec=pltpu.PrefetchScalarGridSpec(num_...  16.7 us
    pallas_call x2, Pallas kernels, run_product(): pl.pallas_call(functools.partial(whole_kernel, transposed), grid=(columns...  14.5 us
    pallas_call x2, Pallas kernels, run_project(): pl.pallas_call(project_kernel, grid_spec=pltpu.PrefetchScalarGridSpec(num...  14.4 us
    ppermute x12, starting transfers between devices, swap(): return lax.ppermute(value, 'fsdp', [(0, 1), (1, 0)])  12.3 us
  transfers between devices with their start and end apart: 34, of which 11 were waited for; matrix products, arithmetic and copies ran while one was open for 17% of the time, Pallas kernels for 44%

profile of v5, /device:TPU:1, one launch (start us, length us, event | category | flops | bytes accessed | tf_op | source)
XLA Modules:
  0.0 442.9 jit_solution(15274396884399418083)
XLA Ops:
  11.7 4.9 %columns.2 = bf16[1024,2048]{1,0:T(8,128)(2,1)} custom-call(s32[1]{0:T(128)} %bitcast.2.core_ref, bf16[1024,8192]{1,0:T(8,128)(2,1)} %gate_own.1), custom_call_target="tpu_custom_call" | custom-call | flops 5750000128 | bytes 8388608 | tf_op jit(solution)/shard_map/columns/pallas_call | solution.py:364
  17.7 5.1 %columns.3 = bf16[1024,2048]{1,0:T(8,128)(2,1)} custom-call(s32[1]{0:T(128)} %bitcast.2.core_ref, bf16[1024,8192]{1,0:T(8,128)(2,1)} %gate_own.1), custom_call_target="tpu_custom_call" | custom-call | flops 5750000128 | bytes 8388608 | tf_op jit(solution)/shard_map/columns/pallas_call | solution.py:364
  32.7 7.1 %project.2 = bf16[512,2048]{1,0:T(8,128)(2,1)S(1)} custom-call(s32[1]{0:T(128)} %bitcast.2.core_ref, bf16[512,2048]{1,0:T(8,128)(2,1)S(1)} %fusion.2.x_ref, bf16[1024,8192]{1,0:T(8,128)(2,1)} %gate_own.1, bf16[1024,2048]{1,0:T(8,128)(2,1)} %collective-permute-done.2.got_ref.inner_got), custom_call_target="tpu_custom_call" | custom-call | flops 5750000128 | bytes 8388608 | tf_op jit(solution)/shard_map/project/pallas_call | solution.py:427
  39.8 5.0 %collective-permute-start.3 = (bf16[2,3,2048]{2,1,0:T(4,128)(2,1)S(1)}, bf16[2,3,2048]{2,1,0:T(4,128)(2,1)S(1)}, u32[]{:S(2)}, u32[]{:S(2)}) collective-permute-start(bf16[2,3,2048]{2,1,0:T(4,128)(2,1)S(1)} %slice.146), channel_id=1, source_target_pairs={{0,2},{2,4},{4,6},{6,8},{8,10},{10,12},{12,14},{14,16},{16,18},{18... | collective-permute-start | bytes 73736 | tf_op jit(solution)/shard_map/ppermute | solution.py:768
  44.8 7.3 %product.2 = f32[512,2048]{1,0:T(8,128)S(1)} custom-call(bf16[512,2048]{1,0:T(8,128)(2,1)S(1)} %pad_maximum_fusion.2.left_ref, bf16[2048,2048]{1,0:T(8,128)(2,1)} %right_ref.3), custom_call_target="tpu_custom_call" | custom-call | flops 5750000128 | bytes 1048576 | tf_op jit(solution)/shard_map/product/pallas_call | solution.py:398
  52.2 4.4 multiply_convert_fusion
  61.6 7.3 %project.3 = bf16[512,2048]{1,0:T(8,128)(2,1)S(1)} custom-call(s32[1]{0:T(128)} %bitcast.2.core_ref, bf16[512,2048]{1,0:T(8,128)(2,1)S(1)} %fusion.2.x_ref, bf16[1024,8192]{1,0:T(8,128)(2,1)} %gate_own.1, bf16[1024,2048]{1,0:T(8,128)(2,1)S(1)} %collective-permute-done.5.got_ref.gate_got), custom_call_target="tpu_custom_call" | custom-call | flops 5750000128 | bytes 8388608 | tf_op jit(solution)/shard_map/project/pallas_call | solution.py:427
  71.5 35.9 %summary.1 = (f32[2,256,2048]{2,1,0:T(8,128)}, f32[2,256,2048]{2,1,0:T(8,128)}, f32[2,256,2048]{2,1,0:T(8,128)}, bf16[16,3,32,128]{3,2,1,0:T(8,128)(2,1)}) custom-call(f32[2,256,160]{2,1,0:T(8,128)} %copy.54.sel_ref.refs_0_.refs_4_, bf16[2,256,2048]{2,1,0:T(8,128)(2,1)} %get-tuple-element.151.act_ref.refs_4_.refs_8_, bf16[2,256,2048]{2,1,0:T(8,128)(2,1)} %bitcast.246, ...), custom_call_target="tpu_custom_call" | custom-call | flops 28750000128 | bytes 22224896 | tf_op jit(solution)/shard_map/summary/pallas_call | solution.py:583
  107.4 6.0 %all-to-all-start = ((bf16[16,3,32,128]{3,2,1,0:T(8,128)(2,1)}), bf16[16,3,32,128]{3,2,1,0:T(8,128)(2,1)S(1)}, u32[]{:S(2)}, u32[]{:S(2)}) async-start(bf16[16,3,32,128]{3,2,1,0:T(8,128)(2,1)} %get-tuple-element.63), calls=%async_computation | async-start | bytes 786432 | tf_op jit(solution)/shard_map/all_to_all | solution.py:750
  113.4 10.8 %all-to-all-done.pieces_ref = bf16[16,3,32,128]{3,2,1,0:T(8,128)(2,1)S(1)} async-done(((bf16[16,3,32,128]{3,2,1,0:T(8,128)(2,1)}), bf16[16,3,32,128]{3,2,1,0:T(8,128)(2,1)S(1)}, u32[]{:S(2)}, u32[]{:S(2)}) %all-to-all-start) | async-done | bytes 393248 | tf_op jit(solution)/shard_map/all_to_all | solution.py:750
  126.8 5.4 %all-to-all-start.1 = ((bf16[16,2,32,128]{3,2,1,0:T(8,128)(2,1)}), bf16[16,2,32,128]{3,2,1,0:T(8,128)(2,1)S(1)}, u32[]{:S(2)}, u32[]{:S(2)}) async-start(bf16[16,2,32,128]{3,2,1,0:T(8,128)(2,1)} %chain.1), calls=%async_computation.1 | async-start | bytes 524288 | tf_op jit(solution)/shard_map/all_to_all | solution.py:759
  134.3 5.5 %all-to-all-done.1.init_ref.refs_6_.refs_10_ = bf16[16,2,32,128]{3,2,1,0:T(8,128)(2,1)S(1)} async-done(((bf16[16,2,32,128]{3,2,1,0:T(8,128)(2,1)}), bf16[16,2,32,128]{3,2,1,0:T(8,128)(2,1)S(1)}, u32[]{:S(2)}, u32[]{:S(2)}) %all-to-all-start.1) | async-done | bytes 262176 | tf_op jit(solution)/shard_map/all_to_all | solution.py:759
  140.5 29.7 %forward.1 = (bf16[4,512,512]{2,1,0:T(8,128)(2,1)}, bf16[4,512,512]{2,1,0:T(8,128)(2,1)}, bf16[2,256,2048]{2,1,0:T(8,128)(2,1)}, f32[2,16,16,2048]{3,2,1,0:T(8,128)}, f32[2,1,2048]{2,1,0:T(1,128)}) custom-call(f32[2,256,160]{2,1,0:T(8,128)} %copy.54.sel_ref.refs_0_.refs_4_, f32[2,256,2048]{2,1,0:T(8,128)} %get-tuple-element.61.r_ref.refs_1_.refs_5_, ...), custom_call_target="tpu_custom_call" | custom-call | flops 23000000512 | bytes 28139520 | tf_op jit(solution)/shard_map/forward/pallas_call | solution.py:583
  170.3 4.6 %all-to-all-start.2 = ((bf16[4,512,512]{2,1,0:T(8,128)(2,1)}), bf16[4,512,512]{2,1,0:T(8,128)(2,1)}, u32[]{:S(2)}, u32[]{:S(2)}) async-start(bf16[4,512,512]{2,1,0:T(8,128)(2,1)} %get-tuple-element.75), calls=%async_computation.2 | async-start | bytes 4194304 | tf_op jit(solution)/shard_map/all_to_all | solution.py:917
  177.9 34.9 %backward.2 = (bf16[2,256,2048]{2,1,0:T(8,128)(2,1)}, f32[2,256,160]{2,1,0:T(8,128)}, f32[2,256,2048]{2,1,0:T(8,128)}, f32[2,1,2048]{2,1,0:T(1,128)}) custom-call(f32[2,256,160]{2,1,0:T(8,128)} %copy.54.sel_ref.refs_0_.refs_4_, f32[2,256,2048]{2,1,0:T(8,128)} %get-tuple-element.61.r_ref.refs_1_.refs_5_, ...), custom_call_target="tpu_custom_call" | custom-call | flops 39099998208 | bytes 13180928 | tf_op jit(solution)/shard_map/backward/pallas_call | solution.py:691
  213.2 9.8 %fusion.32 = f32[2048,512]{1,0:T(8,128)} fusion(bf16[2048,2048]{1,0:T(8,128)(2,1)} %all-gather.4.cloned.1.call-done, bf16[512,512]{1,0:T(8,128)(2,1)S(1)} %get-tuple-element.154, bf16[512,512]{1,0:T(8,128)(2,1)S(1)} %get-tuple-element.155, bf16[512,512]{1,0:T(8,128)(2,1)S(1)} %get-tuple-element.156, bf16[512,512]{1,0:T(8,128)(2,1)S(1)} %get-tuple-element.153), kind=kOutput, calls=%fused_computation.56 | convolution fusion | flops 4303355904 | bytes 14680064 | tf_op jit(solution)/shard_map/dot_general | solution.py:30
  226.2 35.1 %backward.3 = (bf16[2,256,2048]{2,1,0:T(8,128)(2,1)}, f32[2,256,160]{2,1,0:T(8,128)}, f32[2,256,2048]{2,1,0:T(8,128)}, f32[2,1,2048]{2,1,0:T(1,128)}) custom-call(bf16[2,256,2048]{2,1,0:T(8,128)(2,1)} %get-tuple-element.80.refs_0_, ...), custom_call_target="tpu_custom_call", output_to_operand_aliasing={{0}: (0, {}), {1}: (1, {}), {2}: (2, {}), {3}: (3, {})} | custom-call | flops 39099998208 | bytes 13180928 | tf_op jit(solution)/shard_map/backward/pallas_call | solution.py:691
  263.5 4.8 %collective-permute-start.11 = (f32[512,160]{0,1:T(8,128)S(1)}, f32[512,160]{0,1:T(8,128)}, u32[]{:S(2)}, u32[]{:S(2)}) collective-permute-start(f32[512,160]{0,1:T(8,128)S(1)} %copy.64), channel_id=1, source_target_pairs={{0,1},{1,0},{2,3},{3,2},{4,5},{5,4},{6,7},{7,6},{8,9},{9,8},{10,11... | collective-permute-start | bytes 983048 | tf_op jit(solution)/shard_map/ppermute | solution.py:43
  271.7 6.2 %fusion.9 = (f32[2048]{0:T(1024)S(1)}, f32[2048]{0:T(1024)S(1)}, f32[2048]{0:T(1024)S(1)}, f32[512,2048]{1,0:T(8,128)S(1)}) fusion(bf16[2,256,2048]{2,1,0:T(8,128)(2,1)S(1)} %bitcast.242, bf16[2,3,2048]{2,1,0:T(4,128)(2,1)S(1)} %copy-done.41, f32[2,256,2048]{2,1,0:T(8,128)} %copy-done.18, bf16[512,160]{0,1:T(8,128)(2,1)S(1)} %add_convert_fusion, ...), kind=kOutput, calls=%fused_computation.17 | convolution fusion | flops 363849728 | bytes 15548416 | tf_op jit(solution)/shard_map/dot_general | solution.py:26
  284.3 5.1 %correlate.1.inner_ref = bf16[4,512,512]{2,1,0:T(8,128)(2,1)} custom-call(f32[2,256,2048]{2,1,0:T(8,128)} %bitcast.255, f32[2,8,2048]{2,1,0:T(8,128)} %pad.12.later_ref, f32[4,2048]{1,0:T(4,128)} %convert_bitcast_fusion.w_ref), custom_call_target="tpu_custom_call" | custom-call | flops 4600000000 | bytes 6455296 | tf_op jit(solution)/shard_map/correlate/pallas_call | solution.py:583
  297.9 16.7 %normed.1 = (f32[256,2048]{1,0:T(8,128)S(1)}, f32[256,2048]{1,0:T(8,128)}) custom-call(s32[1]{0:T(128)} %bitcast.2.core_ref, bf16[4,512,512]{2,1,0:T(8,128)(2,1)} %correlate.1.inner_ref, bf16[4,512,512]{2,1,0:T(8,128)(2,1)} %get-tuple-element.91.gate_ref, bf16[1024,8192]{1,0:T(8,128)(2,1)} %gate_own.1, bf16[1024,8192]{1,0:T(8,128)(2,1)} %gate_own.1, ...), custom_call_target="tpu_custom_call" | custom-call | flops 11500000256 | bytes 1048576 | tf_op jit(solution)/shard_map/normed/pallas_call | solution.py:505
  315.9 5.5 %collective-permute-done.13 = bf16[1,512,512]{2,1,0:T(8,128)(2,1)S(1)} collective-permute-done((bf16[1,512,512]{2,1,0:T(8,128)(2,1)S(1)}, bf16[1,512,512]{2,1,0:T(8,128)(2,1)S(1)}, u32[]{:S(2)}, u32[]{:S(2)}) %collective-permute-start.13) | collective-permute-done | bytes 524320 | tf_op jit(solution)/shard_map/ppermute | solution.py:786
  322.3 6.9 %fusion.69 = f32[2048,512]{1,0:T(8,128)S(1)} fusion(bf16[2048,2048]{1,0:T(8,128)(2,1)} %all-gather.4.cloned.1.call-done, bf16[2048,512]{1,0:T(8,128)(2,1)S(1)} %bitcast.263), kind=kOutput, calls=%fused_computation.169 | convolution fusion | flops 4294967296 | bytes 14680064 | tf_op jit(solution)/shard_map/dot_general | solution.py:30
  330.5 7.6 %fusion.70 = f32[512,2048]{1,0:T(8,128)S(1)} fusion(bf16[2048,512]{1,0:T(8,128)(2,1)} %bitcast.29, bf16[2048,2048]{1,0:T(8,128)(2,1)} %bitcast.291), kind=kOutput, calls=%fused_computation.170 | convolution fusion | flops 4294967296 | bytes 14680064 | tf_op jit(solution)/shard_map/dot_general | solution.py:30
  340.8 7.2 %product.3 = f32[512,2048]{1,0:T(8,128)S(1)} custom-call(bf16[512,2048]{1,0:T(8,128)(2,1)S(1)} %bitcast.251, bf16[2048,2048]{1,0:T(8,128)(2,1)} %right_ref.3), custom_call_target="tpu_custom_call" | custom-call | flops 5750000128 | bytes 1048576 | tf_op jit(solution)/shard_map/product/pallas_call | solution.py:398
  364.3 4.3 all-to-all-start.4
  373.4 12.9 %collective-permute-done.17 = bf16[1,512,512]{2,1,0:T(8,128)(2,1)} collective-permute-done((bf16[1,512,512]{2,1,0:T(8,128)(2,1)}, bf16[1,512,512]{2,1,0:T(8,128)(2,1)}, u32[]{:S(2)}, u32[]{:S(2)}) %collective-permute-start.17) | collective-permute-done | bytes 524320 | tf_op jit(solution)/shard_map/ppermute | solution.py:786
  390.1 5.1 %collective-permute-done.24 = bf16[1,128,2048]{2,1,0:T(8,128)(2,1)} collective-permute-done((bf16[1,128,2048]{2,1,0:T(8,128)(2,1)}, bf16[1,128,2048]{2,1,0:T(8,128)(2,1)}, u32[]{:S(2)}, u32[]{:S(2)}) %collective-permute-start.24) | collective-permute-done | bytes 524320 | tf_op jit(solution)/shard_map/ppermute | solution.py:786
  397.5 5.7 %collective-permute-start.25 = (bf16[128,2048]{1,0:T(8,128)(2,1)}, bf16[128,2048]{1,0:T(8,128)(2,1)}, u32[]{:S(2)}, u32[]{:S(2)}) collective-permute-start(bf16[128,2048]{1,0:T(8,128)(2,1)} %bitcast_convert_fusion.3), channel_id=1, source_target_pairs={{1,16},{9,24},{16,1},{24,9},{3,18},{11,26},{18,3},{26,11},{5,20},{... | collective-permute-start | bytes 1572872 | tf_op jit(solution)/shard_map/ppermute | solution.py:809
  406.3 6.0 %fusion.28 = (f32[1,256,2048]{2,1,0:T(8,128)}, bf16[1,256,2048]{2,1,0:T(8,128)(2,1)}) fusion(f32[256]{0:T(256)S(1)} %broadcast_multiply_fusion, f32[2048]{0:T(1024)S(1)} %copy-done.37, f32[256]{0:T(256)S(1)} %copy-done.43, bf16[1,256,2048]{2,1,0:T(8,128)(2,1)S(1)} %copy-done.22, bf16[1,256,2048]{2,1,0:T(8,128)(2,1)S(1)} %copy-done.17, ...), kind=kLoop, calls=%fused_computation.48 | loop fusion | flops 6291456 | bytes 13641732 | tf_op jit(solution)/shard_map/broadcast_in_dim | solution.py:1027
  413.4 4.4 all-to-all-start.5
  424.1 4.6 %all-to-all-done.5 = bf16[4,128,1024]{2,1,0:T(8,128)(2,1)} async-done(((bf16[4,128,1024]{2,1,0:T(8,128)(2,1)}), bf16[4,128,1024]{2,1,0:T(8,128)(2,1)}, u32[]{:S(2)}, u32[]{:S(2)}) %all-to-all-start.5) | async-done | bytes 1048608 | tf_op jit(solution)/shard_map/all_to_all | solution.py:927
  (252 shorter events, 105.7 us)
Async XLA Ops:
  7.2 163.0 %all-gather.6.cloned.1.call-start = ((), (), s32[]{:S(2)}) async-start(), calls=%async_computation.7 | async-start | bytes 9437184 | tf_op jit(solution)/shard_map/all_gather | solution.py:881
  7.9 162.3 %all-gather.4.cloned.1.call-start = ((), (), s32[]{:S(2)}) async-start(), calls=%async_computation.6 | async-start | bytes 9437184 | tf_op jit(solution)/shard_map/all_gather | solution.py:880
  16.6 16.0 %collective-permute-start.2 = (bf16[1024,2048]{1,0:T(8,128)(2,1)}, bf16[1024,2048]{1,0:T(8,128)(2,1)}, u32[]{:S(2)}, u32[]{:S(2)}) collective-permute-start(bf16[1024,2048]{1,0:T(8,128)(2,1)} %columns.2), channel_id=1, source_target_pairs={{0,1},{1,0},{2,3},{3,2},{4,5},{5,4},{6,7},{7,6},{8,9},{9,8},{10,11... | collective-permute-start | bytes 12582920 | tf_op jit(solution)/shard_map/ppermute | solution.py:43
  17.1 8.4 %collective-permute-start = (bf16[256,2048]{1,0:T(8,128)(2,1)S(1)}, bf16[256,2048]{1,0:T(8,128)(2,1)}, u32[]{:S(2)}, u32[]{:S(2)}) collective-permute-start(bf16[256,2048]{1,0:T(8,128)(2,1)S(1)} %bitcast.252), channel_id=1, source_target_pairs={{0,1},{1,0},{2,3},{3,2},{4,5},{5,4},{6,7},{7,6},{8,9},{9,8},{10,11... | collective-permute-start | bytes 3145736 | tf_op jit(solution)/shard_map/ppermute | solution.py:43
  17.1 12.8 %collective-permute-start.6 = (bf16[256,2048]{1,0:T(8,128)(2,1)S(1)}, bf16[256,2048]{1,0:T(8,128)(2,1)}, u32[]{:S(2)}, u32[]{:S(2)}) collective-permute-start(bf16[256,2048]{1,0:T(8,128)(2,1)S(1)} %bitcast.253), channel_id=1, source_target_pairs={{0,1},{1,0},{2,3},{3,2},{4,5},{5,4},{6,7},{7,6},{8,9},{9,8},{10,11... | collective-permute-start | bytes 3145736 | tf_op jit(solution)/shard_map/ppermute | solution.py:43
  22.7 38.9 %collective-permute-start.5 = (bf16[1024,2048]{1,0:T(8,128)(2,1)}, bf16[1024,2048]{1,0:T(8,128)(2,1)S(1)}, u32[]{:S(2)}, u32[]{:S(2)}) collective-permute-start(bf16[1024,2048]{1,0:T(8,128)(2,1)} %columns.3), channel_id=1, source_target_pairs={{0,1},{1,0},{2,3},{3,2},{4,5},{5,4},{6,7},{7,6},{8,9},{9,8},{10,11... | collective-permute-start | bytes 12582920 | tf_op jit(solution)/shard_map/ppermute | solution.py:43
  39.8 12.4 %collective-permute-start.3 = (bf16[2,3,2048]{2,1,0:T(4,128)(2,1)S(1)}, bf16[2,3,2048]{2,1,0:T(4,128)(2,1)S(1)}, u32[]{:S(2)}, u32[]{:S(2)}) collective-permute-start(bf16[2,3,2048]{2,1,0:T(4,128)(2,1)S(1)} %slice.146), channel_id=1, source_target_pairs={{0,2},{2,4},{4,6},{6,8},{8,10},{10,12},{12,14},{14,16},{16,18},{18... | collective-permute-start | bytes 73736 | tf_op jit(solution)/shard_map/ppermute | solution.py:768
  60.9 9.3 %collective-permute-start.4 = (f32[512,160]{0,1:T(8,128)S(1)}, f32[512,160]{0,1:T(8,128)S(1)}, u32[]{:S(2)}, u32[]{:S(2)}) collective-permute-start(f32[512,160]{0,1:T(8,128)S(1)} %fusion.68), channel_id=1, source_target_pairs={{0,1},{1,0},{2,3},{3,2},{4,5},{5,4},{6,7},{7,6},{8,9},{9,8},{10,11... | collective-permute-start | bytes 983048 | tf_op jit(solution)/shard_map/ppermute | solution.py:43
  107.4 16.9 %all-to-all-start = ((bf16[16,3,32,128]{3,2,1,0:T(8,128)(2,1)}), bf16[16,3,32,128]{3,2,1,0:T(8,128)(2,1)S(1)}, u32[]{:S(2)}, u32[]{:S(2)}) async-start(bf16[16,3,32,128]{3,2,1,0:T(8,128)(2,1)} %get-tuple-element.63), calls=%async_computation | async-start | bytes 786432 | tf_op jit(solution)/shard_map/all_to_all | solution.py:750
  126.8 13.0 %all-to-all-start.1 = ((bf16[16,2,32,128]{3,2,1,0:T(8,128)(2,1)}), bf16[16,2,32,128]{3,2,1,0:T(8,128)(2,1)S(1)}, u32[]{:S(2)}, u32[]{:S(2)}) async-start(bf16[16,2,32,128]{3,2,1,0:T(8,128)(2,1)} %chain.1), calls=%async_computation.1 | async-start | bytes 524288 | tf_op jit(solution)/shard_map/all_to_all | solution.py:759
  170.3 52.7 %all-to-all-start.2 = ((bf16[4,512,512]{2,1,0:T(8,128)(2,1)}), bf16[4,512,512]{2,1,0:T(8,128)(2,1)}, u32[]{:S(2)}, u32[]{:S(2)}) async-start(bf16[4,512,512]{2,1,0:T(8,128)(2,1)} %get-tuple-element.75), calls=%async_computation.2 | async-start | bytes 4194304 | tf_op jit(solution)/shard_map/all_to_all | solution.py:917
  175.1 37.6 %collective-permute-start.9 = (bf16[512,512]{1,0:T(8,128)(2,1)S(1)}, bf16[512,512]{1,0:T(8,128)(2,1)S(1)}, u32[]{:S(2)}, u32[]{:S(2)}) collective-permute-start(bf16[512,512]{1,0:T(8,128)(2,1)S(1)} %get-tuple-element.157), channel_id=1, source_target_pairs={{0,6},{2,4},{4,2},{6,0},{1,7},{3,5},{5,3},{7,1},{8,14},{10,12},{12... | collective-permute-start | bytes 1572872 | tf_op jit(solution)/shard_map/ppermute | solution.py:776
  176.0 36.7 %collective-permute-start.8 = (bf16[512,512]{1,0:T(8,128)(2,1)S(1)}, bf16[512,512]{1,0:T(8,128)(2,1)S(1)}, u32[]{:S(2)}, u32[]{:S(2)}) collective-permute-start(bf16[512,512]{1,0:T(8,128)(2,1)S(1)} %get-tuple-element.158), channel_id=1, source_target_pairs={{0,4},{2,6},{4,0},{6,2},{1,5},{3,7},{5,1},{7,3},{8,12},{10,14},{12... | collective-permute-start | bytes 1572872 | tf_op jit(solution)/shard_map/ppermute | solution.py:776
  177.4 35.4 %collective-permute-start.7 = (bf16[512,512]{1,0:T(8,128)(2,1)S(1)}, bf16[512,512]{1,0:T(8,128)(2,1)S(1)}, u32[]{:S(2)}, u32[]{:S(2)}) collective-permute-start(bf16[512,512]{1,0:T(8,128)(2,1)S(1)} %get-tuple-element.159), channel_id=1, source_target_pairs={{0,2},{2,0},{4,6},{6,4},{1,3},{3,1},{5,7},{7,5},{8,10},{10,8},{12,... | collective-permute-start | bytes 1572872 | tf_op jit(solution)/shard_map/ppermute | solution.py:776
  224.7 36.5 %collective-permute-start.10 = (bf16[2,512,512]{2,1,0:T(8,128)(2,1)S(1)}, bf16[2,512,512]{2,1,0:T(8,128)(2,1)S(1)}, u32[]{:S(2)}, u32[]{:S(2)}) collective-permute-start(bf16[2,512,512]{2,1,0:T(8,128)(2,1)S(1)} %fusion.40), channel_id=1, source_target_pairs={{0,8},{8,0},{16,24},{24,16},{1,9},{9,1},{17,25},{25,17},{2,10},{10... | collective-permute-start | bytes 3145736 | tf_op jit(solution)/shard_map/ppermute | solution.py:786
  263.5 7.2 %collective-permute-start.11 = (f32[512,160]{0,1:T(8,128)S(1)}, f32[512,160]{0,1:T(8,128)}, u32[]{:S(2)}, u32[]{:S(2)}) collective-permute-start(f32[512,160]{0,1:T(8,128)S(1)} %copy.64), channel_id=1, source_target_pairs={{0,1},{1,0},{2,3},{3,2},{4,5},{5,4},{6,7},{7,6},{8,9},{9,8},{10,11... | collective-permute-start | bytes 983048 | tf_op jit(solution)/shard_map/ppermute | solution.py:43
  278.0 5.6 %collective-permute-start.12 = (f32[2,3,2048]{2,1,0:T(4,128)S(1)}, f32[2,3,2048]{2,1,0:T(4,128)S(1)}, u32[]{:S(2)}, u32[]{:S(2)}) collective-permute-start(f32[2,3,2048]{2,1,0:T(4,128)S(1)} %slice.156), channel_id=1, source_target_pairs={{2,0},{4,2},{6,4},{8,6},{10,8},{12,10},{14,12},{16,14},{18,16},{20... | collective-permute-start | bytes 147464 | tf_op jit(solution)/shard_map/ppermute | solution.py:768
  289.3 33.0 %all-to-all-start.3 = ((bf16[4,512,512]{2,1,0:T(8,128)(2,1)}), bf16[4,512,512]{2,1,0:T(8,128)(2,1)S(1)}, u32[]{:S(2)}, u32[]{:S(2)}) async-start(bf16[4,512,512]{2,1,0:T(8,128)(2,1)} %correlate.1.inner_ref), calls=%async_computation.3 | async-start | bytes 4194304 | tf_op jit(solution)/shard_map/all_to_all | solution.py:965
  295.7 25.6 %collective-permute-start.13 = (bf16[1,512,512]{2,1,0:T(8,128)(2,1)S(1)}, bf16[1,512,512]{2,1,0:T(8,128)(2,1)S(1)}, u32[]{:S(2)}, u32[]{:S(2)}) collective-permute-start(bf16[1,512,512]{2,1,0:T(8,128)(2,1)S(1)} %dynamic-slice_convert_fusion.2), channel_id=1, source_target_pairs={{0,16},{8,24},{16,0},{24,8},{1,17},{9,25},{17,1},{25,9},{2,18},{10... | collective-permute-start | bytes 1572872 | tf_op jit(solution)/shard_map/ppermute | solution.py:786
  329.4 23.9 %collective-permute-start.16 = (bf16[2,512,512]{2,1,0:T(8,128)(2,1)S(1)}, bf16[2,512,512]{2,1,0:T(8,128)(2,1)S(1)}, u32[]{:S(2)}, u32[]{:S(2)}) collective-permute-start(bf16[2,512,512]{2,1,0:T(8,128)(2,1)S(1)} %fusion.41), channel_id=1, source_target_pairs={{0,8},{8,0},{16,24},{24,16},{1,9},{9,1},{17,25},{25,17},{2,10},{10... | collective-permute-start | bytes 3145736 | tf_op jit(solution)/shard_map/ppermute | solution.py:786
  329.5 25.5 %collective-permute-start.15 = (f32[256,2048]{1,0:T(8,128)}, f32[256,2048]{1,0:T(8,128)S(1)}, u32[]{:S(2)}, u32[]{:S(2)}) collective-permute-start(f32[256,2048]{1,0:T(8,128)} %get-tuple-element.99), channel_id=1, source_target_pairs={{0,1},{1,0},{2,3},{3,2},{4,5},{5,4},{6,7},{7,6},{8,9},{9,8},{10,11... | collective-permute-start | bytes 6291464 | tf_op jit(solution)/shard_map/ppermute | solution.py:43
  339.4 25.0 %collective-permute-start.19 = (bf16[2,128,2048]{2,1,0:T(8,128)(2,1)}, bf16[2,128,2048]{2,1,0:T(8,128)(2,1)}, u32[]{:S(2)}, u32[]{:S(2)}) collective-permute-start(bf16[2,128,2048]{2,1,0:T(8,128)(2,1)} %fusion.42), channel_id=1, source_target_pairs={{0,2},{2,0},{4,6},{6,4},{1,3},{3,1},{5,7},{7,5},{8,10},{10,8},{12,... | collective-permute-start | bytes 3145736 | tf_op jit(solution)/shard_map/ppermute | solution.py:786
  349.9 56.4 %collective-permute-start.14 = (f32[256,2048]{1,0:T(8,128)}, f32[256,2048]{1,0:T(8,128)}, u32[]{:S(2)}, u32[]{:S(2)}) collective-permute-start(f32[256,2048]{1,0:T(8,128)} %dynamic-slice_bitcast_fusion), channel_id=1, source_target_pairs={{0,1},{1,0},{2,3},{3,2},{4,5},{5,4},{6,7},{7,6},{8,9},{9,8},{10,11... | collective-permute-start | bytes 6291464 | tf_op jit(solution)/shard_map/ppermute | solution.py:43
  356.3 3.9 collective-permute-start.18
  360.2 26.1 %collective-permute-start.17 = (bf16[1,512,512]{2,1,0:T(8,128)(2,1)}, bf16[1,512,512]{2,1,0:T(8,128)(2,1)}, u32[]{:S(2)}, u32[]{:S(2)}) collective-permute-start(bf16[1,512,512]{2,1,0:T(8,128)(2,1)} %dynamic-slice_convert_fusion.1), channel_id=1, source_target_pairs={{0,16},{8,24},{16,0},{24,8},{1,17},{9,25},{17,1},{25,9},{2,18},{10... | collective-permute-start | bytes 1572872 | tf_op jit(solution)/shard_map/ppermute | solution.py:786
  364.3 24.0 %all-to-all-start.4 = ((bf16[4,2,304,256]{3,2,1,0:T(8,128)(2,1)}), bf16[4,2,304,256]{3,2,1,0:T(8,128)(2,1)}, u32[]{:S(2)}, u32[]{:S(2)}) async-start(bf16[4,2,304,256]{3,2,1,0:T(8,128)(2,1)} %copy-done.9), calls=%async_computation.4 | async-start | bytes 2490368 | tf_op jit(solution)/shard_map/all_to_all | solution.py:1008
  371.9 23.3 %collective-permute-start.24 = (bf16[1,128,2048]{2,1,0:T(8,128)(2,1)}, bf16[1,128,2048]{2,1,0:T(8,128)(2,1)}, u32[]{:S(2)}, u32[]{:S(2)}) collective-permute-start(bf16[1,128,2048]{2,1,0:T(8,128)(2,1)} %dynamic-slice_convert_fusion), channel_id=1, source_target_pairs={{0,4},{2,6},{4,0},{6,2},{1,5},{3,7},{5,1},{7,3},{8,12},{10,14},{12... | collective-permute-start | bytes 1572872 | tf_op jit(solution)/shard_map/ppermute | solution.py:786
  390.1 13.1 %collective-permute-start.20 = (bf16[1,304,256]{2,1,0:T(8,128)(2,1)S(1)}, bf16[1,304,256]{2,1,0:T(8,128)(2,1)S(1)}, u32[]{:S(2)}, u32[]{:S(2)}) collective-permute-start(bf16[1,304,256]{2,1,0:T(8,128)(2,1)S(1)} %dynamic-slice_convert_fusion.3), channel_id=1, source_target_pairs={{0,8},{8,0},{16,24},{24,16},{1,9},{9,1},{17,25},{25,17},{2,10},{10... | collective-permute-start | bytes 466952 | tf_op jit(solution)/shard_map/ppermute | solution.py:786
  397.5 24.3 %collective-permute-start.25 = (bf16[128,2048]{1,0:T(8,128)(2,1)}, bf16[128,2048]{1,0:T(8,128)(2,1)}, u32[]{:S(2)}, u32[]{:S(2)}) collective-permute-start(bf16[128,2048]{1,0:T(8,128)(2,1)} %bitcast_convert_fusion.3), channel_id=1, source_target_pairs={{1,16},{9,24},{16,1},{24,9},{3,18},{11,26},{18,3},{26,11},{5,20},{... | collective-permute-start | bytes 1572872 | tf_op jit(solution)/shard_map/ppermute | solution.py:809
  403.9 13.9 %collective-permute-start.21 = (bf16[304,256]{1,0:T(8,128)(2,1)}, bf16[304,256]{1,0:T(8,128)(2,1)}, u32[]{:S(2)}, u32[]{:S(2)}) collective-permute-start(bf16[304,256]{1,0:T(8,128)(2,1)} %bitcast_convert_fusion.4), channel_id=1, source_target_pairs={{1,17},{9,25},{16,0},{24,8},{3,19},{11,27},{18,2},{26,10},{5,21},{... | collective-permute-start | bytes 466952 | tf_op jit(solution)/shard_map/ppermute | solution.py:820
  413.4 15.3 %all-to-all-start.5 = ((bf16[4,128,1024]{2,1,0:T(8,128)(2,1)}), bf16[4,128,1024]{2,1,0:T(8,128)(2,1)}, u32[]{:S(2)}, u32[]{:S(2)}) async-start(bf16[4,128,1024]{2,1,0:T(8,128)(2,1)} %bitcast.256), calls=%async_computation.5 | async-start | bytes 2097152 | tf_op jit(solution)/shard_map/all_to_all | solution.py:927
  419.5 10.4 %collective-permute-start.22 = (f32[304,128]{1,0:T(8,128)S(1)}, f32[304,128]{1,0:T(8,128)S(1)}, u32[]{:S(2)}, u32[]{:S(2)}) collective-permute-start(f32[304,128]{1,0:T(8,128)S(1)} %constant_dynamic-slice_fusion), channel_id=1, source_target_pairs={{0,1},{1,0},{2,3},{3,2},{4,5},{5,4},{6,7},{7,6},{8,9},{9,8},{10,11... | collective-permute-start | bytes 466952 | tf_op jit(solution)/shard_map/ppermute | solution.py:43
  (50 other events, 541.1 us)
Sparse Core Ops, SparseCore 0:
  9.6 84.5 all-gather.5
  96.7 59.6 all-gather.3
